TPU v7x, 256 devices: a whole 4x4x8 slice. The times are simulated.
256 devices in a mesh: grp: 2 (over core), gx: 32 (over z, x), gy: 4 (over y).
Axes of the slice: x: 4, y: 4, z: 8, core: 2. Of those that a mesh axis runs over, the one named last changes fastest.
Arguments:
- pressure_start: float32 [128, 32, 256], P('gx', 'gy', 'grp'), may hold values from -6 to 6
- source: float32 [128, 32, 256], P('gx', 'gy', 'grp'), may hold values from -6 to 6
- storage: float32 [128, 32, 256], P('gx', 'gy', 'grp'), may hold values from 0.02 to 0.2
- perm_class: int32 [128, 32, 256], P('gx', 'gy', 'grp'), may hold values from 0 to 15
- class_perm: float32 [16], replicated, may hold values from 0.1 to 10
- block_route: int32 [32, 8, 512], P('gx'), may hold values from 0 to 511, each once within a row
- displacement_start: float32 [3, 131072], P(None, ('grp', 'gx', 'gy')), may hold values from -3 to 3
- load: float32 [3, 131072], P(None, ('grp', 'gx', 'gy')), may hold values from -6 to 6
- support: float32 [3, 131072], P(None, ('grp', 'gx', 'gy')), may hold values from 0.2 to 2
- lame_lambda: float32 [256, 512], P(('grp', 'gx', 'gy')), may hold values from 0.5 to 2
- lame_mu: float32 [256, 512], P(('grp', 'gx', 'gy')), may hold values from 0.3 to 1.5
- stiff_lambda: float32 [24, 24], replicated, may hold values from -0.8 to 0.8, as said below
- stiff_mu: float32 [24, 24], replicated, may hold values from -0.8 to 0.8, as said below
- coupling_vec: float32 [24], replicated, may hold values from -0.36 to 0.36, as said below
Outputs:
- pressure: float32 [128, 32, 256], P('gx', 'gy', 'grp')
- displacement: float32 [3, 131072], P(None, ('grp', 'gx', 'gy'))
Inputs may be any that keep to these rules, and one draw needn't show every extreme that they name: For each gx and each k, block_route[gx][k] holds every number of 0 to 511 once. `stiff_lambda`: symmetric; each row sums to zero. `stiff_mu`: symmetric; each row sums to zero. `coupling_vec`: the eight entries of each component sum to zero.
All inputs are finite; a program needn't handle non-finite values.
Results may differ from a plain program's by a relative error of at most 0.0001.
Values sent between devices are 32-bit elements; how exact they have to be, the bound alone decides.
No kernel may reach another device: no remote copies, remote signals or barrier semaphores. Data moves between devices by JAX's collectives and lax.ppermute only.
A program may use at most 64 MiB of HBM per device.

v0:
```python
import jax
import jax.numpy as jnp
import numpy as np
from jax import lax
from jax.experimental import pallas as pl
from jax.experimental.pallas import tpu as pltpu
from jax.sharding import Mesh
from jax.sharding import PartitionSpec as P

SWEEPS = 6
CLASSES = 16
CHIPS = 16
PLANES = 16
NODES = 16
TILES = 13

stabilize = 0.5
biot_coef = 0.8
damping = 0.7
tiny = 1e-30

f32 = jnp.float32
bf16 = jnp.bfloat16

VM = pl.BlockSpec(memory_space=pltpu.VMEM)
SM = pl.BlockSpec(memory_space=pltpu.SMEM)


def call(body, out_shapes, in_specs, scratch=(), budget=40 * 1024 * 1024):
    return pl.pallas_call(
        body,
        out_shape=out_shapes,
        in_specs=in_specs,
        out_specs=jax.tree.map(lambda _: VM, out_shapes),
        scratch_shapes=list(scratch),
        compiler_params=pltpu.CompilerParams(vmem_limit_bytes=budget),
    )


def lanes(shape):
    return lax.broadcasted_iota(jnp.int32, shape, 1)


def rows(shape):
    return lax.broadcasted_iota(jnp.int32, shape, 0)


def roll(x, shift, axis=1):
    shift = shift % x.shape[axis]
    return x if shift == 0 else pltpu.roll(x, shift, axis)


def three_parts(x):
    high = x.astype(bf16)
    rest = x - high.astype(f32)
    middle = rest.astype(bf16)
    return high, middle, (rest - middle.astype(f32)).astype(bf16)


def nt_dot(a, b):
    return lax.dot_general(a, b, (((1,), (1,)), ((), ())), preferred_element_type=f32)


def stage_kernel(perms, p0, src, sto, cls, disp, load, sup, lam, mu, cells, nodes, held, small, pair, classes, sems):
    copies = [
        pltpu.make_async_copy(perms, classes, sems.at[9]),
        pltpu.make_async_copy(p0, cells.at[0:4], sems.at[0]),
        pltpu.make_async_copy(src, cells.at[4:8], sems.at[1]),
        pltpu.make_async_copy(sto, cells.at[8:12], sems.at[2]),
        pltpu.make_async_copy(cls, held, sems.at[3]),
        pltpu.make_async_copy(disp, small.at[0], sems.at[4]),
        pltpu.make_async_copy(load, small.at[1], sems.at[5]),
        pltpu.make_async_copy(sup, small.at[2], sems.at[6]),
        pltpu.make_async_copy(lam, pair.at[0], sems.at[7]),
        pltpu.make_async_copy(mu, pair.at[1], sems.at[8]),
    ]
    for copy in copies:
        copy.start()
    nodes[...] = jnp.zeros((16, 512), f32)
    for copy in copies:
        copy.wait()
    for i in range(4):
        which = held[i]
        perm = jnp.zeros((8, 128), f32)
        for member in range(CLASSES):
            perm = jnp.where(which == member, classes[member], perm)
        cells[12 + i] = perm
    nodes[0:3] = small[0]
    nodes[3:4] = pair[0]
    nodes[4:7] = small[1]
    nodes[7:8] = pair[1]
    nodes[8:11] = small[2]


def pack_kernel(core, cells, cells_other, nodes, nodes_other, routes, out):
    first = core[0] == 0
    lane = lanes((8, 128))
    low = lane < 64
    sub = rows((8, 128))

    placed = jnp.zeros((192, 128), f32)
    device = lanes((1, 512)) // 64
    for half in range(2):
        block = routes[half : half + 1, :]
        row = block // 64 % 4 * 8 + block // 256 * 4 + device % 4
        depth = device // 4 * 64 + block % 64
        at_row = rows((32, 512)) == row
        at_depth = jnp.where(rows((128, 512)) == depth, 1.0, 0.0).astype(bf16)
        spread = []
        for source in (3, 7):
            own = nodes[source : source + 1, :]
            other = nodes_other[source : source + 1, :]
            value = jnp.where(first, own, other) if half == 0 else jnp.where(first, other, own)
            for part in three_parts(value):
                spread.append(jnp.where(at_row, part.astype(f32), 0.0))
        placed = placed + nt_dot(jnp.concatenate(spread, axis=0).astype(bf16), at_depth)
    grids = [placed[96 * v : 96 * v + 32] + placed[96 * v + 32 : 96 * v + 64] + placed[96 * v + 64 : 96 * v + 96] for v in range(2)]

    for pair in range(2):
        for i in range(4):
            tiles = []
            for field in (2 * pair, 2 * pair + 1):
                own = cells[4 * field + i]
                other = cells_other[4 * field + i]
                tiles.append((jnp.where(first, own, other), jnp.where(first, other, own)))
            for chip in range(CHIPS):
                start = 16 * chip - 24
                spot = lane % 64 + start
                in_low = (spot >= 0) & (spot < 128)
                in_high = (spot >= 128) & (spot < 256)
                found = []
                for member in range(2):
                    shift = 64 * member - start
                    win = jnp.zeros((8, 128), f32)
                    if start < 128:
                        win = jnp.where(in_low, roll(tiles[member][0], shift), win)
                    if start + 64 > 128:
                        win = jnp.where(in_high, roll(tiles[member][1], shift), win)
                    found.append(win)
                out[chip, 4 * pair + i] = jnp.where(low, found[0], found[1])

    def full_depth(i, r):
        full = []
        for j in range(4):
            at = (i * 4 + j) // 2 * 128
            own = nodes[8 * r : 8 * r + 8, at : at + 128]
            other = nodes_other[8 * r : 8 * r + 8, at : at + 128]
            near = jnp.where(first, own, other)
            deep = jnp.where(first, other, own)
            if j % 2 == 0:
                full.append(jnp.where(low, near, roll(deep, 64)))
            else:
                full.append(jnp.where(low, roll(near, 64), deep))
        return full

    supports = [jnp.where(sub < 4, a, pltpu.roll(b, 4, 0)) for a, b in zip(full_depth(0, 1), full_depth(1, 1))]
    members = [full_depth(0, 0), full_depth(1, 0), supports]
    members += [[grid[8 * j : 8 * j + 8] for j in range(4)] for grid in grids]
    for at, full in enumerate(members):
        for chip in range(CHIPS):
            start = 8 * chip - 12
            spot = lane % 32 + start
            tile = jnp.zeros((8, 128), f32)
            for j in range(4):
                tile = jnp.where(lane // 32 == j, roll(full[j], 32 * j - start), tile)
            out[chip, 8 + at] = jnp.where((spot >= 0) & (spot < 128), tile, 0.0)


def low_mask(shape):
    return lanes(shape) < 64


def above(ref, x):
    return ref[x + 1] if x < PLANES - 1 else roll(ref[0], 64)


def below(ref, x):
    return ref[x - 1] if x > 0 else roll(ref[PLANES - 1], 64)


def window(core, places, then):
    for c in range(2):
        @pl.when(core[0] == c)
        def _():
            then(places[c])


def cell_coefs(start, source, storage, perm, coef, fixed, inverse):
    keep_top = rows((32, 128)) < 31
    for x in range(PLANES):
        p = perm[x]
        q = above(perm, x)
        coef[0, x] = 2.0 * p * q / jnp.maximum(p + q, tiny)
        q = roll(p, 31, 0)
        coef[2, x] = jnp.where(keep_top, 2.0 * p * q / jnp.maximum(p + q, tiny), 0.0)
        q = roll(p, 127)
        coef[4, x] = 2.0 * p * q / jnp.maximum(p + q, tiny)
    for x in range(PLANES):
        coef[1, x] = coef[0, x - 1] if x > 0 else roll(coef[0, PLANES - 1], 64)
        coef[3, x] = roll(coef[2, x], 1, 0)
        coef[5, x] = roll(coef[4, x], 1)
    for x in range(PLANES):
        total = coef[0, x] + coef[1, x] + coef[2, x] + coef[3, x] + coef[4, x] + coef[5, x]
        inv = jnp.where(storage[x] > 0.0, 1.0 / (storage[x] + stabilize + total), 0.0)
        inverse[x] = inv
        fixed[x] = source[x] + storage[x] * start[x]
        for face in range(6):
            coef[face, x] = coef[face, x] * inv


def one_sweep(src, dst, coef, rhs):
    for x in range(PLANES):
        p = src[x]
        total = rhs[x] + coef[0, x] * above(src, x) + coef[1, x] * below(src, x)
        total = total + coef[2, x] * roll(p, 31, 0) + coef[3, x] * roll(p, 1, 0)
        dst[x] = total + coef[4, x] * roll(p, 127) + coef[5, x] * roll(p, 1)


def sweeps(press, coef, rhs):
    def two(_, carry):
        one_sweep(press.at[0], press.at[1], coef, rhs)
        one_sweep(press.at[1], press.at[0], coef, rhs)
        return carry

    lax.fori_loop(0, SWEEPS // 2, two, 0)


def pair_matrix():
    cell = rows((128, 256))
    n = lanes((128, 256))
    hit = (cell // 2 % 32 == n % 32) & (cell // 64 == n // 128)
    return jnp.where(hit, 0.125, 0.0).astype(bf16)


def row_mask(shape):
    return lanes(shape) % 128 // 32 == rows(shape) % 8 // 2


def block_means(press, means):
    sums = jnp.concatenate([press[2 * q] + press[2 * q + 1] for q in range(8)], axis=0)
    matrix = pair_matrix()
    got = jnp.zeros((256, 256), f32)
    for part in three_parts(sums):
        got = got + jnp.dot(part, matrix, preferred_element_type=f32)
    got = jnp.where(row_mask((256, 256)), got, 0.0)
    for b in range(3, 12):
        piece = got[32 * (b % 8) : 32 * (b % 8) + 32, 128 * (b // 8) : 128 * (b // 8) + 128]
        for y in range(4):
            means[b, 0:1, 128 * y : 128 * y + 128] = jnp.sum(piece[8 * y : 8 * y + 8], axis=0, keepdims=True)


def last_row(shape):
    return lanes(shape) // 32 % 16 == 15


def corner_rolls(u):
    last = last_row(u.shape)
    return [
        u,
        roll(u, 511),
        jnp.where(last, 0.0, roll(u, 480)),
        jnp.where(last, 0.0, roll(u, 479)),
    ]


def assembled(here, under):
    summed = here[0:32] + under[32:64]
    last = last_row((8, 512))
    return (
        summed[0:8]
        + roll(summed[8:16], 1)
        + roll(jnp.where(last, 0.0, summed[16:24]), 32)
        + roll(jnp.where(last, 0.0, summed[24:32]), 33)
    )


def diag_of(lam, mu, sup, aux, safe, gain):
    depth = lanes((8, 512)) % 32
    inside = (depth >= 6) & (depth < 26)
    terms = {}
    for b in range(3, 12):
        terms[b] = aux[:, 1:2] * lam[b] + aux[:, 2:3] * mu[b]
        if b > 3:
            node_sup = sup[b]
            total = node_sup + assembled(terms[b], terms[b - 1])
            valid = inside & (node_sup > 0.0)
            safe[b] = jnp.where(valid, total, 1.0)
            gain[b] = jnp.where(valid, damping, 0.0)


def stiff_parts(stiff):
    high = stiff.astype(bf16)
    low = (stiff - high.astype(f32)).astype(bf16)
    return jnp.concatenate([high, high, low], axis=1)


def element_terms(matrix, coupling, v_here, v_next, lam, mu, press):
    vals = jnp.concatenate(v_here + v_next, axis=0)
    high = vals.astype(bf16)
    low = (vals - high.astype(f32)).astype(bf16)
    both = jnp.dot(matrix, jnp.concatenate([high, low, high], axis=0), preferred_element_type=f32)
    return coupling * (biot_coef * press) - (lam * both[0:64] + mu * both[64:128])


def displacements(u, lam, mu, load, sup, safe, gain, means, stiff, aux, moved, least, most):
    matrix = stiff_parts(stiff[...])
    coupling = aux[:, 0:1]

    def half(old, new, least, most):
        under = None
        v_here = corner_rolls(old[least - 1])
        for b in range(least - 1, most + 1):
            v_next = corner_rolls(old[b + 1])
            terms = element_terms(matrix, coupling, v_here, v_next, lam[b], mu[b], means[b])
            if b >= least:
                value = old[b]
                residual = load[b] - sup[b] * value + assembled(terms, under)
                new[b] = value + gain[b] * residual / safe[b]
            under = terms
            v_here = v_next

    half(u, moved.at[0], least - 1, most + 1)
    half(moved.at[0], moved.at[1], least, most)


def pack_mid(core, press, moved, out):
    low = low_mask((32, 128))
    pairs = [jnp.where(low, press[12 + q], press[q]) for q in range(4)]
    extra = jnp.where(low, press[10], roll(press[11], 64))
    node = jnp.where(core[0] == 0, moved[1, 10], moved[1, 5])
    for y in range(4):
        for q in range(4):
            out[y, q] = pairs[q][8 * y : 8 * y + 8]
            out[y, 4 + q] = moved[1, 6 + q, :, 128 * y : 128 * y + 128]
        out[y, 8] = extra[8 * y : 8 * y + 8]
        out[y, 9] = node[:, 128 * y : 128 * y + 128]


def pack_last(press, moved, out):
    lane = lanes((32, 128))
    for x in range(2):
        cells = jnp.zeros((32, 128), f32)
        for i in range(4):
            if x == 0:
                tile = roll(press[12 + i], 16 * i - 24)
            else:
                tile = roll(press[i], 16 * i - 88)
            cells = jnp.where(lane // 16 == i, tile, cells)
        for y in range(4):
            total = cells[8 * y : 8 * y + 8]
            for i in range(2):
                tile = moved[1, 6 + 2 * x + i, :, 128 * y : 128 * y + 128]
                for j in range(4):
                    total = jnp.where(lane[0:8] // 8 == 8 + 4 * i + j, roll(tile, 52 + 32 * i - 24 * j), total)
            out[4 * x + y] = total


def first_kernel(
    core, ok, grid, halo, share, stiff, aux,
    mid, coef, fixed, inverse, u, lam, mu, load, sup, safe, gain,
    press, storage, perm, rhs, means, moved,
):
    low = low_mask((32, 128))

    def unpack(units):
        def read(unit, y, at):
            ref, index, flag = units[unit]
            value = ref[4 * index + y, at] if y is not None else ref[4 * index : 4 * index + 4, at]
            return value if flag is None else value * ok[flag]

        def tile(cell, at):
            return read(cell // 4, None, at + cell % 4).reshape(32, 128)

        for x in range(PLANES):
            a = tile(x, 0)
            b = tile(x + PLANES, 0)
            press[0, x] = jnp.where(low, a, roll(b, 64))
            rhs[x] = jnp.where(low, roll(a, 64), b)
            a = tile(x, 4)
            b = tile(x + PLANES, 4)
            storage[x] = jnp.where(low, a, roll(b, 64))
            perm[x] = jnp.where(low, roll(a, 64), b)
        sub = rows((8, 128))
        for unit in range(8):
            for y in range(4):
                at = slice(128 * y, 128 * y + 128)
                support = read(unit, y, 10)
                for i in range(2):
                    n = 2 * unit + i
                    tile_a = read(unit, y, 8 + i)
                    u[n, :, at] = jnp.where(sub < 3, tile_a, 0.0)
                    if 4 <= n <= 11:
                        load[n, :, at] = jnp.where(sub < 3, pltpu.roll(tile_a, 4, 0), 0.0)
                        tile_b = support if i == 0 else pltpu.roll(support, 4, 0)
                        sup[n, :, at] = jnp.where(sub < 3, tile_b, 0.0)
            if 1 <= unit <= 5:
                for at, param in ((11, lam), (12, mu)):
                    total = read(unit, 0, at) + read(unit, 1, at) + read(unit, 2, at) + read(unit, 3, at)
                    for i in range(2):
                        for y in range(4):
                            row = 4 * i + y
                            param[2 * unit + i, :, 128 * y : 128 * y + 128] = total[row : row + 1]

    below = [(halo, 0, 0), (halo, 1, 0), (halo, 2, 0)]
    plane = [(grid, 0, None), (grid, 1, None), (grid, 2, None), (grid, 3, None)]
    beside = [(share, 0, 1)]
    window(core, [below + plane + beside, beside + plane + below], unpack)
    cell_coefs(press.at[0], rhs, storage, perm, coef, fixed, inverse)
    for x in range(PLANES):
        rhs[x] = (fixed[x] + stabilize * press[0, x]) * inverse[x]
    sweeps(press, coef, rhs)
    block_means(press.at[0], means)
    diag_of(lam, mu, sup, aux, safe, gain)
    displacements(u, lam, mu, load, sup, safe, gain, means, stiff, aux, moved, 5, 10)
    pack_mid(core, press.at[0], moved, mid)


def second_kernel(
    core, ok, own, partner, near, across, stiff, aux,
    coef, fixed, inverse, start, lam, mu, load, sup, safe, gain,
    last, press, rhs, means, u, strain, moved,
):
    low = low_mask((32, 128))

    def unpack(runs, extra):
        def piece(cell, want_low):
            if cell in extra["cells"]:
                ref, q, is_low = extra["cells"][cell]
            elif 4 <= cell < 28:
                k = (cell - 4) % 8
                ref, q, is_low = runs[(cell - 4) // 8][0], k % 4, k < 4
            else:
                return jnp.zeros((32, 128), f32)
            value = ref[:, q].reshape(32, 128)
            return value if is_low == want_low else roll(value, 64)

        for x in range(PLANES):
            press[0, x] = jnp.where(low, piece(x, True), piece(x + PLANES, False))
        for n in range(NODES):
            if n in extra["nodes"]:
                ref, q, flag = extra["nodes"][n]
            elif 2 <= n < 14:
                (ref, flag), q = runs[(n - 2) // 4], 4 + (n - 2) % 4
            else:
                u[n] = jnp.zeros((8, 512), f32)
                continue
            for y in range(4):
                value = ref[y, q]
                u[n, :, 128 * y : 128 * y + 128] = value if flag is None else value * ok[flag]

    @pl.when(core[0] == 0)
    def _():
        unpack(
            [(near, 0), (own, None), (partner, None)],
            {"cells": {2: (near, 8, True), 3: (near, 8, False)}, "nodes": {1: (near, 9, 0), 14: (across, 4, 1)}},
        )

    @pl.when(core[0] == 1)
    def _():
        unpack(
            [(partner, None), (own, None), (near, 0)],
            {"cells": {2: (across, 2, False), 3: (across, 3, False)}, "nodes": {1: (across, 7, 1), 14: (near, 9, 0)}},
        )

    strain[...] = jnp.zeros((PLANES, 1, 512), f32)
    last_y = last_row((8, 512))
    here = u[1] - start[1]
    for b in range(1, 14):
        following = u[b + 1] - start[b + 1]
        parts = [
            aux[8 * a : 8 * a + 8, 0:1] * here + aux[32 + 8 * a : 40 + 8 * a, 0:1] * following
            for a in range(4)
        ]
        total = (
            parts[0]
            + roll(parts[1], 511)
            + jnp.where(last_y, 0.0, roll(parts[2], 480) + roll(parts[3], 479))
        )
        strain[b] = jnp.sum(total, axis=0, keepdims=True)
        here = following
    mask = row_mask((8, 128))
    spread = []
    for q in range(8):
        for y in range(4):
            at = slice(128 * y, 128 * y + 128)
            spread.append(
                jnp.concatenate(
                    [jnp.where(mask, strain[q, :, at], 0.0), jnp.where(mask, strain[8 + q, :, at], 0.0)],
                    axis=1,
                )
            )
    matrix = pair_matrix()
    got = jnp.zeros((256, 128), f32)
    for part in three_parts(jnp.concatenate(spread, axis=0)):
        got = got + nt_dot(part, matrix)
    for x in range(PLANES):
        change = got[32 * (x // 2) : 32 * (x // 2) + 32]
        right = fixed[x] + stabilize * press[0, x] - (8.0 * biot_coef) * change
        rhs[x] = right * inverse[x]
    sweeps(press, coef, rhs)
    block_means(press.at[0], means)
    displacements(u, lam, mu, load, sup, safe, gain, means, stiff, aux, moved, 6, 9)
    pack_last(press.at[0], moved, last)


def unpack_kernel(core, got, pressure, disp, held):
    lane = lanes((8, 128))
    base = core[0] * 8
    tiles = [got[base + s] for s in range(8)]
    for i in range(4):
        total = jnp.zeros((8, 128), f32)
        for s in range(8):
            total = jnp.where(lane // 16 == s, roll(tiles[s], 16 * s - 16 * i), total)
        pressure[i] = total
    for i in range(2):
        for pair in range(2):
            total = jnp.zeros((8, 128), f32)
            for s in range(8):
                for side in range(2):
                    shift = 64 * side + 8 * s - 64 - 32 * i - 8 * (2 * pair + side)
                    total = jnp.where(lane // 8 == 8 * side + s, roll(tiles[s], shift), total)
            held[:, 128 * (2 * i + pair) : 128 * (2 * i + pair) + 128] = total
    disp[...] = held[0:3]


def corner_major(stiff):
    grid = stiff.reshape(3, 8, 3, 8).transpose(1, 0, 3, 2)
    return jnp.pad(grid, ((0, 0), (0, 5), (0, 0), (0, 5))).reshape(64, 64)


def corner_column(vec):
    return jnp.pad(vec.reshape(3, 8).T, ((0, 0), (0, 5))).reshape(64)


def shape(*dims):
    return jax.ShapeDtypeStruct(dims, f32)


def shards(
    pressure_start, source, storage, perm_class, class_perm, block_route, displacement_start,
    load, support, lame_lambda, lame_mu, stiff_lambda, stiff_mu, coupling_vec,
):
    core = lax.axis_index("grp")
    layer = lax.axis_index("gz")
    core_arg = jnp.full((1,), core, jnp.int32)
    has_below, has_above = layer > 0, layer < 7
    ok = jnp.stack(
        [jnp.where(core == 0, has_below, has_above), jnp.where(core == 0, has_above, has_below)]
    ).astype(f32)
    swap = [(0, 1), (1, 0)]

    cells, nodes = call(
        stage_kernel,
        (shape(16, 8, 128), shape(16, 512)),
        [pl.BlockSpec(memory_space=pltpu.HBM)] * 10,
        [
            pltpu.VMEM((4, 8, 128), jnp.int32),
            pltpu.VMEM((3, 3, 512), f32),
            pltpu.VMEM((2, 1, 512), f32),
            pltpu.SMEM((CLASSES,), f32),
            pltpu.SemaphoreType.DMA((10,)),
        ],
        64 * 1024 * 1024 - 65536,
    )(class_perm, pressure_start, source, storage, perm_class, displacement_start, load, support,
      lame_lambda, lame_mu)
    cells_other = lax.ppermute(cells, "grp", swap)
    nodes_other = lax.ppermute(nodes, "grp", swap)
    routes = lax.dynamic_index_in_dim(
        block_route[0].reshape(8, 2, 4, 64), lax.axis_index("gy"), 2, keepdims=False
    ).transpose(1, 0, 2).reshape(2, 512)
    packed = call(pack_kernel, shape(16, TILES, 8, 128), [SM] + [VM] * 5)(
        core_arg, cells, cells_other, nodes, nodes_other, routes
    )
    grid = lax.all_to_all(packed, ("gx", "gy"), 0, 0, tiled=True)

    ring = [(8 + z, (z + 1) % 8) for z in range(8)] + [(z, 8 + (z - 1) % 8) for z in range(8)]
    halo = lax.ppermute(lax.dynamic_slice_in_dim(grid, 4 * core, 12, 0), ("grp", "gz"), ring)
    share = lax.ppermute(lax.dynamic_slice_in_dim(halo, 8 * (1 - core), 4, 0), "grp", swap)

    stiff = jnp.concatenate([corner_major(stiff_lambda), corner_major(stiff_mu)], axis=0)
    columns = [corner_column(coupling_vec), corner_column(jnp.diag(stiff_lambda)), corner_column(jnp.diag(stiff_mu))]
    aux = jnp.pad(jnp.stack(columns, axis=1), ((0, 0), (0, 125)))

    kept = (
        shape(6, PLANES, 32, 128), shape(PLANES, 32, 128), shape(PLANES, 32, 128),
        shape(NODES, 8, 512), shape(12, 1, 512), shape(12, 1, 512), shape(12, 8, 512),
        shape(12, 8, 512), shape(12, 8, 512), shape(12, 8, 512),
    )
    mid, *statics = call(
        first_kernel,
        (shape(4, 10, 8, 128),) + kept,
        [SM, SM] + [VM] * 5,
        [
            pltpu.VMEM((2, PLANES, 32, 128), f32),
            pltpu.VMEM((PLANES, 32, 128), f32),
            pltpu.VMEM((PLANES, 32, 128), f32),
            pltpu.VMEM((PLANES, 32, 128), f32),
            pltpu.VMEM((PLANES, 1, 512), f32),
            pltpu.VMEM((2, NODES, 8, 512), f32),
        ],
    )(core_arg, ok, grid, halo, share, stiff, aux)

    near = lax.ppermute(mid, ("grp", "gz"), ring)
    partner = lax.ppermute(mid, "grp", swap)
    across = lax.ppermute(near, "grp", swap)
    last = call(
        second_kernel,
        shape(8, 8, 128),
        [SM, SM] + [VM] * 16,
        [
            pltpu.VMEM((2, PLANES, 32, 128), f32),
            pltpu.VMEM((PLANES, 32, 128), f32),
            pltpu.VMEM((PLANES, 1, 512), f32),
            pltpu.VMEM((NODES, 8, 512), f32),
            pltpu.VMEM((PLANES, 1, 512), f32),
            pltpu.VMEM((2, NODES, 8, 512), f32),
        ],
    )(core_arg, ok, mid, partner, near, across, stiff, aux, *statics)

    other = lax.ppermute(last, "grp", swap)
    whole = jnp.concatenate([jnp.where(core == 0, last, other), jnp.where(core == 0, other, last)], axis=0)
    back = lax.all_to_all(whole, ("gx", "gy"), 0, 0, tiled=True)
    return call(
        unpack_kernel,
        (shape(4, 8, 128), shape(3, 512)),
        [SM, VM],
        [pltpu.VMEM((8, 512), f32)],
    )(core_arg, back)


def solution(mesh):
    fine = Mesh(np.asarray(mesh.devices).reshape(2, 8, 4, 4), ("grp", "gz", "gx", "gy"))
    cell = P(("gz", "gx"), "gy", "grp")
    node = P(None, ("grp", "gz", "gx", "gy"))
    elem = P(("grp", "gz", "gx", "gy"), None)
    return jax.shard_map(
        shards,
        mesh=fine,
        in_specs=(
            cell, cell, cell, cell, P(), P(("gz", "gx"), None, None), node, node, node, elem, elem,
            P(), P(), P(),
        ),
        out_specs=(cell, node),
        check_vma=False,
    )
```

profile of v0, /device:TPU:1, one launch (start us, length us, event | category | flops | bytes accessed | tf_op | source)
XLA Modules:
  0.0 72.8 jit_solution(18264213058224616344)
XLA Ops:
  0.6 1.6 %shard_map.149 = (f32[16,8,128]{2,1,0:T(8,128)}, f32[16,512]{1,0:T(8,128)}) custom-call(f32[16]{0:T(128)} %perms.1, f32[4,8,128]{2,1,0:T(8,128)} %p0.1, f32[4,8,128]{2,1,0:T(8,128)} %src.1, f32[4,8,128]{2,1,0:T(8,128)} %sto.1, s32[4,8,128]{2,1,0:T(8,128)} %cls.1, f32[3,512]{1,0:T(4,128)} %disp.1, f32[3,512]{1,0:T(4,128)} %load.1, f32[3,512]{1,0:T(4,128)} %sup.1, ...), custom_call_target="tpu_custom_call" | custom-call | tf_op jit(solution)/shard_map/pallas_call | solution.py:552
  2.2 3.3 %collective-permute-start.1 = (f32[16,512]{1,0:T(8,128)}, f32[16,512]{1,0:T(8,128)S(1)}, u32[]{:S(2)}, u32[]{:S(2)}) collective-permute-start(f32[16,512]{1,0:T(8,128)} %get-tuple-element.16.nodes), channel_id=1, source_target_pairs={{0,128},{128,0},{1,129},{129,1},{2,130},{130,2},{3,131},{131,3},{4... | collective-permute-start | bytes 98312 | tf_op jit(solution)/shard_map/ppermute | solution.py:567
  5.5 0.1 collective-permute-start
  5.6 0.8 %reshape_squeeze.3 = s32[8,2,4,64]{3,2,1,0:T(4,128)S(1)} reshape(s32[1,8,512]{2,1,0:T(8,128)} %param.19) | data formatting | bytes 32768 | tf_op jit(solution)/shard_map/reshape;squeeze | solution.py:569
  6.5 0.1 reshape.28.routes
  6.6 0.1 collective-permute-done.1.nodes_other
  6.6 0.4 collective-permute-done.cells_other
  7.0 0.0 copy-start
  7.0 0.8 %copy-done = f32[16,8,128]{2,1,0:T(8,128)S(1)} copy-done((f32[16,8,128]{2,1,0:T(8,128)S(1)}, f32[16,8,128]{2,1,0:T(8,128)}, u32[]{:S(2)}) %copy-start) | copy-done | bytes 65560
  7.9 0.0 copy-start.1
  7.9 0.8 %copy-done.1 = f32[16,512]{1,0:T(8,128)S(1)} copy-done((f32[16,512]{1,0:T(8,128)S(1)}, f32[16,512]{1,0:T(8,128)}, u32[]{:S(2)}) %copy-start.1) | copy-done | bytes 32792
  8.6 1.7 %shard_map.150 = f32[16,13,8,128]{3,2,1,0:T(8,128)} custom-call(s32[1]{0:T(128)} %bitcast.core, f32[16,8,128]{2,1,0:T(8,128)S(1)} %copy-done, f32[16,8,128]{2,1,0:T(8,128)S(1)} %collective-permute-done.cells_other, f32[16,512]{1,0:T(8,128)S(1)} %copy-done.1, f32[16,512]{1,0:T(8,128)S(1)} %collective-permute-done.1.nodes_other, s32[2,512]{1,0:T(2,128)S(1)} %reshape.28.routes), custom_call_target="tpu_custom_call" | custom-call | tf_op jit(solution)/shard_map/pallas_call | solution.py:571
  10.3 0.0 copy-start.2
  10.3 0.0 copy-start.3
  10.3 5.1 %all-to-all-start = ((f32[16,13,8,128]{3,2,1,0:T(8,128)}), f32[16,13,8,128]{3,2,1,0:T(8,128)S(1)}, u32[]{:S(2)}, u32[]{:S(2)}) async-start(f32[16,13,8,128]{3,2,1,0:T(8,128)} %shard_map.150), calls=%async_computation | async-start | bytes 1703936 | tf_op jit(solution)/shard_map/all_to_all | solution.py:574
  15.5 0.0 copy-start.4
  15.5 13.3 %all-to-all-done.grid = f32[16,13,8,128]{3,2,1,0:T(8,128)S(1)} async-done(((f32[16,13,8,128]{3,2,1,0:T(8,128)}), f32[16,13,8,128]{3,2,1,0:T(8,128)S(1)}, u32[]{:S(2)}, u32[]{:S(2)}) %all-to-all-start) | async-done | bytes 852000 | tf_op jit(solution)/shard_map/all_to_all | solution.py:574
  28.8 4.7 %collective-permute-start.2 = (f32[12,13,8,128]{3,2,1,0:T(8,128)S(1)}, f32[12,13,8,128]{3,2,1,0:T(8,128)S(1)}, u32[]{:S(2)}, u32[]{:S(2)}) collective-permute-start(f32[12,13,8,128]{3,2,1,0:T(8,128)S(1)} %constant_dynamic-slice_fusion.1), channel_id=1, source_target_pairs={{128,16},{144,32},{160,48},{176,64},{192,80},{208,96},{224,112},{2... | collective-permute-start | bytes 1916936 | tf_op jit(solution)/shard_map/ppermute | solution.py:577
  33.5 0.0 copy-done.2
  33.5 0.1 reshape.29
  33.6 0.8 %gather_fusion = f32[24]{0:T(128)S(1)} fusion(f32[24,24]{1,0:T(8,128)S(1)} %copy-done.2, s32[24]{0:T(128)S(1)} %or_bitcast_fusion), kind=kCustom, calls=%fused_computation | custom fusion | bytes 384 | tf_op jit(solution)/shard_map/jit(_diag)/jit(diagonal)/cond/branch_0_fun/gather | solution.py:581
  34.4 0.0 copy-done.3
  34.4 0.8 %gather_fusion.1 = f32[24]{0:T(128)S(1)} fusion(f32[24,24]{1,0:T(8,128)S(1)} %copy-done.3, s32[24]{0:T(128)S(1)} %or_bitcast_fusion), kind=kCustom, calls=%fused_computation.1 | custom fusion | bytes 384 | tf_op jit(solution)/shard_map/jit(_diag)/jit(diagonal)/cond/branch_0_fun/gather | solution.py:581
  35.2 0.1 reshape.31
  35.3 0.1 reshape.34
  35.3 0.1 reshape.35
  35.4 0.1 copy.45
  35.5 0.1 stack_reshape.11
  35.6 0.1 copy.44
  35.7 0.1 stack_reshape.10
  35.8 0.0 copy-done.4
  35.8 0.1 reshape.33
  35.9 0.1 copy.43
  36.0 0.1 stack_reshape.9
  36.1 0.1 copy.40
  36.2 0.2 copy.41
  36.4 0.2 copy.42
  36.6 0.1 reshape.32
  36.8 0.1 reshape.30
  36.9 5.0 %collective-permute-done.2.halo = f32[12,13,8,128]{3,2,1,0:T(8,128)S(1)} collective-permute-done((f32[12,13,8,128]{3,2,1,0:T(8,128)S(1)}, f32[12,13,8,128]{3,2,1,0:T(8,128)S(1)}, u32[]{:S(2)}, u32[]{:S(2)}) %collective-permute-start.2) | collective-permute-done | bytes 639008 | tf_op jit(solution)/shard_map/ppermute | solution.py:577
  41.9 1.2 %collective-permute-start.3 = (f32[4,13,8,128]{3,2,1,0:T(8,128)S(1)}, f32[4,13,8,128]{3,2,1,0:T(8,128)S(1)}, u32[]{:S(2)}, u32[]{:S(2)}) collective-permute-start(f32[4,13,8,128]{3,2,1,0:T(8,128)S(1)} %constant_dynamic-slice_fusion), channel_id=1, source_target_pairs={{0,128},{128,0},{1,129},{129,1},{2,130},{130,2},{3,131},{131,3},{4... | collective-permute-start | bytes 638984 | tf_op jit(solution)/shard_map/ppermute | solution.py:578
  43.1 0.1 add_convert_fusion.ok
  43.2 1.0 %collective-permute-done.3.share = f32[4,13,8,128]{3,2,1,0:T(8,128)S(1)} collective-permute-done((f32[4,13,8,128]{3,2,1,0:T(8,128)S(1)}, f32[4,13,8,128]{3,2,1,0:T(8,128)S(1)}, u32[]{:S(2)}, u32[]{:S(2)}) %collective-permute-start.3) | collective-permute-done | bytes 213024 | tf_op jit(solution)/shard_map/ppermute | solution.py:578
  44.2 4.1 %shard_map.151 = (f32[4,10,8,128]{3,2,1,0:T(8,128)S(1)}, f32[6,16,32,128]{3,2,1,0:T(8,128)S(1)}, f32[16,32,128]{2,1,0:T(8,128)S(1)}, f32[16,32,128]{2,1,0:T(8,12...) custom-call(s32[1]{0:T(128)} %bitcast.core, ...), custom_call_target="tpu_custom_call" | custom-call | tf_op jit(solution)/shard_map/pallas_call | solution.py:589
  48.3 0.8 %collective-permute-start.5 = (f32[4,10,8,128]{3,2,1,0:T(8,128)S(1)}, f32[4,10,8,128]{3,2,1,0:T(8,128)S(1)}, u32[]{:S(2)}, u32[]{:S(2)}) collective-permute-start(f32[4,10,8,128]{3,2,1,0:T(8,128)S(1)} %get-tuple-element.17.own), channel_id=1, source_target_pairs={{128,16},{144,32},{160,48},{176,64},{192,80},{208,96},{224,112},{2... | collective-permute-start | bytes 491528 | tf_op jit(solution)/shard_map/ppermute | solution.py:603
  49.1 4.1 %collective-permute-start.4 = (f32[4,10,8,128]{3,2,1,0:T(8,128)S(1)}, f32[4,10,8,128]{3,2,1,0:T(8,128)S(1)}, u32[]{:S(2)}, u32[]{:S(2)}) collective-permute-start(f32[4,10,8,128]{3,2,1,0:T(8,128)S(1)} %get-tuple-element.17.own), channel_id=1, source_target_pairs={{0,128},{128,0},{1,129},{129,1},{2,130},{130,2},{3,131},{131,3},{4... | collective-permute-start | bytes 491528 | tf_op jit(solution)/shard_map/ppermute | solution.py:604
  53.2 0.0 collective-permute-done.5.near
  53.2 3.0 %collective-permute-start.6 = (f32[4,10,8,128]{3,2,1,0:T(8,128)S(1)}, f32[4,10,8,128]{3,2,1,0:T(8,128)S(1)}, u32[]{:S(2)}, u32[]{:S(2)}) collective-permute-start(f32[4,10,8,128]{3,2,1,0:T(8,128)S(1)} %collective-permute-done.5.near), channel_id=1, source_target_pairs={{0,128},{128,0},{1,129},{129,1},{2,130},{130,2},{3,131},{131,3},{4... | collective-permute-start | bytes 491528 | tf_op jit(solution)/shard_map/ppermute | solution.py:605
  56.2 0.0 collective-permute-done.4.partner
  56.2 1.0 %collective-permute-done.6.across = f32[4,10,8,128]{3,2,1,0:T(8,128)S(1)} collective-permute-done((f32[4,10,8,128]{3,2,1,0:T(8,128)S(1)}, f32[4,10,8,128]{3,2,1,0:T(8,128)S(1)}, u32[]{:S(2)}, u32[]{:S(2)}) %collective-permute-start.6) | collective-permute-done | bytes 163872 | tf_op jit(solution)/shard_map/ppermute | solution.py:605
  57.2 3.8 %shard_map.152 = f32[8,8,128]{2,1,0:T(8,128)S(1)} custom-call(s32[1]{0:T(128)} %bitcast.core, f32[2]{0:T(128)S(1)} %add_convert_fusion.ok, f32[4,10,8,128]{3,2,1,0:T(8,128)S(1)} %get-tuple-element.17.own, f32[4,10,8,128]{3,2,1,0:T(8,128)S(1)} %collective-permute-done.4.partner, f32[4,10,8,128]{3,2,1,0:T(8,128)S(1)} %collective-permute-done.5.near, ...), custom_call_target="tpu_custom_call" | custom-call | tf_op jit(solution)/shard_map/pallas_call | solution.py:606
  61.0 0.4 collective-permute-start.7
  61.5 0.9 %collective-permute-done.7 = f32[8,8,128]{2,1,0:T(8,128)S(1)} collective-permute-done((f32[8,8,128]{2,1,0:T(8,128)S(1)}, f32[8,8,128]{2,1,0:T(8,128)S(1)}, u32[]{:S(2)}, u32[]{:S(2)}) %collective-permute-start.7) | collective-permute-done | bytes 32800 | tf_op jit(solution)/shard_map/ppermute | solution.py:620
  62.3 9.7 %all_to_all.10.got = f32[16,8,128]{2,1,0:T(8,128)S(1)} all-to-all(f32[16,8,128]{2,1,0:T(8,128)S(1)} %pad_maximum_fusion), channel_id=1, replica_groups=mesh['grp'=2,'gz'=8,'gx'=4,'gy'=4] {'gx','gy'}, dimensions={0} | all-to-all | bytes 131072 | tf_op jit(solution)/shard_map/all_to_all | solution.py:622
  72.0 0.8 %shard_map.153 = (f32[4,8,128]{2,1,0:T(8,128)}, f32[3,512]{1,0:T(4,128)}) custom-call(s32[1]{0:T(128)} %bitcast.core, f32[16,8,128]{2,1,0:T(8,128)S(1)} %all_to_all.10.got), custom_call_target="tpu_custom_call" | custom-call | tf_op jit(solution)/shard_map/pallas_call | solution.py:623
  (16 shorter events, 0.2 us)
Async XLA Ops:
  2.2 4.4 %collective-permute-start.1 = (f32[16,512]{1,0:T(8,128)}, f32[16,512]{1,0:T(8,128)S(1)}, u32[]{:S(2)}, u32[]{:S(2)}) collective-permute-start(f32[16,512]{1,0:T(8,128)} %get-tuple-element.16.nodes), channel_id=1, source_target_pairs={{0,128},{128,0},{1,129},{129,1},{2,130},{130,2},{3,131},{131,3},{4... | collective-permute-start | bytes 98312 | tf_op jit(solution)/shard_map/ppermute | solution.py:567
  5.5 1.5 %collective-permute-start = (f32[16,8,128]{2,1,0:T(8,128)}, f32[16,8,128]{2,1,0:T(8,128)S(1)}, u32[]{:S(2)}, u32[]{:S(2)}) collective-permute-start(f32[16,8,128]{2,1,0:T(8,128)} %get-tuple-element.15.cells), channel_id=1, source_target_pairs={{0,128},{128,0},{1,129},{129,1},{2,130},{130,2},{3,131},{131,3},{4... | collective-permute-start | bytes 196616 | tf_op jit(solution)/shard_map/ppermute | solution.py:566
  7.0 0.8 %copy-start = (f32[16,8,128]{2,1,0:T(8,128)S(1)}, f32[16,8,128]{2,1,0:T(8,128)}, u32[]{:S(2)}) copy-start(f32[16,8,128]{2,1,0:T(8,128)} %get-tuple-element.15.cells) | copy-start | bytes 196612
  7.9 0.8 %copy-start.1 = (f32[16,512]{1,0:T(8,128)S(1)}, f32[16,512]{1,0:T(8,128)}, u32[]{:S(2)}) copy-start(f32[16,512]{1,0:T(8,128)} %get-tuple-element.16.nodes) | copy-start | bytes 98308
  10.3 23.2 %copy-start.2 = (f32[24,24]{1,0:T(8,128)S(1)}, f32[24,24]{1,0:T(8,128)}, u32[]{:S(2)}) copy-start(f32[24,24]{1,0:T(8,128)} %param.25) | copy-start | bytes 6916
  10.3 24.1 %copy-start.3 = (f32[24,24]{1,0:T(8,128)S(1)}, f32[24,24]{1,0:T(8,128)}, u32[]{:S(2)}) copy-start(f32[24,24]{1,0:T(8,128)} %param.26) | copy-start | bytes 6916
  10.3 18.4 %all-to-all-start = ((f32[16,13,8,128]{3,2,1,0:T(8,128)}), f32[16,13,8,128]{3,2,1,0:T(8,128)S(1)}, u32[]{:S(2)}, u32[]{:S(2)}) async-start(f32[16,13,8,128]{3,2,1,0:T(8,128)} %shard_map.150), calls=%async_computation | async-start | bytes 1703936 | tf_op jit(solution)/shard_map/all_to_all | solution.py:574
  15.5 20.3 %copy-start.4 = (f32[24]{0:T(128)S(1)}, f32[24]{0:T(128)}, u32[]{:S(2)}) copy-start(f32[24]{0:T(128)} %param.27) | copy-start | bytes 292
  28.8 13.1 %collective-permute-start.2 = (f32[12,13,8,128]{3,2,1,0:T(8,128)S(1)}, f32[12,13,8,128]{3,2,1,0:T(8,128)S(1)}, u32[]{:S(2)}, u32[]{:S(2)}) collective-permute-start(f32[12,13,8,128]{3,2,1,0:T(8,128)S(1)} %constant_dynamic-slice_fusion.1), channel_id=1, source_target_pairs={{128,16},{144,32},{160,48},{176,64},{192,80},{208,96},{224,112},{2... | collective-permute-start | bytes 1916936 | tf_op jit(solution)/shard_map/ppermute | solution.py:577
  41.9 2.3 %collective-permute-start.3 = (f32[4,13,8,128]{3,2,1,0:T(8,128)S(1)}, f32[4,13,8,128]{3,2,1,0:T(8,128)S(1)}, u32[]{:S(2)}, u32[]{:S(2)}) collective-permute-start(f32[4,13,8,128]{3,2,1,0:T(8,128)S(1)} %constant_dynamic-slice_fusion), channel_id=1, source_target_pairs={{0,128},{128,0},{1,129},{129,1},{2,130},{130,2},{3,131},{131,3},{4... | collective-permute-start | bytes 638984 | tf_op jit(solution)/shard_map/ppermute | solution.py:578
  48.3 4.8 %collective-permute-start.5 = (f32[4,10,8,128]{3,2,1,0:T(8,128)S(1)}, f32[4,10,8,128]{3,2,1,0:T(8,128)S(1)}, u32[]{:S(2)}, u32[]{:S(2)}) collective-permute-start(f32[4,10,8,128]{3,2,1,0:T(8,128)S(1)} %get-tuple-element.17.own), channel_id=1, source_target_pairs={{128,16},{144,32},{160,48},{176,64},{192,80},{208,96},{224,112},{2... | collective-permute-start | bytes 491528 | tf_op jit(solution)/shard_map/ppermute | solution.py:603
  49.1 7.1 %collective-permute-start.4 = (f32[4,10,8,128]{3,2,1,0:T(8,128)S(1)}, f32[4,10,8,128]{3,2,1,0:T(8,128)S(1)}, u32[]{:S(2)}, u32[]{:S(2)}) collective-permute-start(f32[4,10,8,128]{3,2,1,0:T(8,128)S(1)} %get-tuple-element.17.own), channel_id=1, source_target_pairs={{0,128},{128,0},{1,129},{129,1},{2,130},{130,2},{3,131},{131,3},{4... | collective-permute-start | bytes 491528 | tf_op jit(solution)/shard_map/ppermute | solution.py:604
  53.2 4.0 %collective-permute-start.6 = (f32[4,10,8,128]{3,2,1,0:T(8,128)S(1)}, f32[4,10,8,128]{3,2,1,0:T(8,128)S(1)}, u32[]{:S(2)}, u32[]{:S(2)}) collective-permute-start(f32[4,10,8,128]{3,2,1,0:T(8,128)S(1)} %collective-permute-done.5.near), channel_id=1, source_target_pairs={{0,128},{128,0},{1,129},{129,1},{2,130},{130,2},{3,131},{131,3},{4... | collective-permute-start | bytes 491528 | tf_op jit(solution)/shard_map/ppermute | solution.py:605
  61.0 1.3 %collective-permute-start.7 = (f32[8,8,128]{2,1,0:T(8,128)S(1)}, f32[8,8,128]{2,1,0:T(8,128)S(1)}, u32[]{:S(2)}, u32[]{:S(2)}) collective-permute-start(f32[8,8,128]{2,1,0:T(8,128)S(1)} %shard_map.152), channel_id=1, source_target_pairs={{0,128},{128,0},{1,129},{129,1},{2,130},{130,2},{3,131},{131,3},{4... | collective-permute-start | bytes 98312 | tf_op jit(solution)/shard_map/ppermute | solution.py:620
where the time goes:
time: 73.3 us; the launch traced here: 72.8 us
  starting transfers between devices  22.8 us (31%)
  waiting for transfers between devices  21.6 us (29%)
  Pallas kernels  11.9 us (16%)
  blocking collectives  9.69 us (13%)
  local copies, waits for them, and re-layouts  5.89 us (8%)
  between operations  0.8 us (1%)
    all_to_all x1, waiting for transfers between devices, shards(): grid = lax.all_to_all(packed, ('gx', 'gy'), 0, 0, tiled=True)  13.3 us
    all_to_all x1, blocking collectives, shards(): back = lax.all_to_all(whole, ('gx', 'gy'), 0, 0, tiled=True)  9.69 us
    all_to_all x1, starting transfers between devices, shards(): grid = lax.all_to_all(packed, ('gx', 'gy'), 0, 0, tiled=True)  5.15 us
    ppermute x1, waiting for transfers between devices, shards(): lax.ppermute(lax.dynamic_slice_in_dim(grid, 4 * core, 12, 0), ('grp', 'gz...  4.95 us
    ppermute x1, starting transfers between devices, shards(): lax.ppermute(lax.dynamic_slice_in_dim(grid, 4 * core, 12, 0), ('grp', 'gz...  4.69 us
    pallas_call x1, Pallas kernels, shards(): call(first_kernel, (shape(4, 10, 8, 128),) + kept, [SM, SM] + [VM] * 5, [...  4.12 us
    ppermute x1, starting transfers between devices, shards(): partner = lax.ppermute(mid, 'grp', swap)  4.07 us
    pallas_call x1, Pallas kernels, shards(): call(second_kernel, shape(8, 8, 128), [SM, SM] + [VM] * 16, [pltpu.VMEM((...  3.79 us
  transfers between devices with their start and end apart: 9, of which 7 were waited for; matrix products, arithmetic and copies ran while one was open for 6% of the time, Pallas kernels for 0%

commit v1 on v0

--- a/solution.py
+++ b/solution.py
@@ -13,6 +13,8 @@
 PLANES = 16
 NODES = 16
 TILES = 13
+EARLY = 5
+FAR = (2, 3, 6, 7, 8, 9)
 
 stabilize = 0.5
 biot_coef = 0.8
@@ -24,6 +26,8 @@
 
 VM = pl.BlockSpec(memory_space=pltpu.VMEM)
 SM = pl.BlockSpec(memory_space=pltpu.SMEM)
+HB = pl.BlockSpec(memory_space=pltpu.HBM)
+WHOLE = 64 * 1024 * 1024 - 65536
 
 
 def call(body, out_shapes, in_specs, scratch=(), budget=40 * 1024 * 1024):
@@ -92,7 +96,13 @@
     nodes[8:11] = small[2]
 
 
-def pack_kernel(core, cells, cells_other, nodes, nodes_other, routes, out):
+def pack_kernel(core, across, a, b, c, d, e, out, cells, cells_other, nodes, nodes_other, routes, sems):
+    pairs = [(a, cells), (b, cells_other), (c, nodes), (d, nodes_other), (e, routes)]
+    copies = [pltpu.make_async_copy(src, dst, sems.at[n]) for n, (src, dst) in enumerate(pairs)]
+    for copy in copies:
+        copy.start()
+    for copy in copies:
+        copy.wait()
     first = core[0] == 0
     lane = lanes((8, 128))
     low = lane < 64
@@ -101,7 +111,14 @@
     placed = jnp.zeros((192, 128), f32)
     device = lanes((1, 512)) // 64
     for half in range(2):
-        block = routes[half : half + 1, :]
+        mine = jnp.zeros((8, 128), jnp.int32)
+        for y in range(4):
+            at = 256 * half + y // 2 * 128
+            mine = jnp.where(across[0] == y, roll(routes[0, :, at : at + 128], 64 * (y % 2)), mine)
+        block = jnp.concatenate(
+            [jnp.where(low[0:1], mine[2 * m : 2 * m + 1], roll(mine[2 * m + 1 : 2 * m + 2], 64)) for m in range(4)],
+            axis=1,
+        )
         row = block // 64 % 4 * 8 + block // 256 * 4 + device % 4
         depth = device // 4 * 64 + block % 64
         at_row = rows((32, 512)) == row
@@ -170,14 +187,6 @@
     return lanes(shape) < 64
 
 
-def above(ref, x):
-    return ref[x + 1] if x < PLANES - 1 else roll(ref[0], 64)
-
-
-def below(ref, x):
-    return ref[x - 1] if x > 0 else roll(ref[PLANES - 1], 64)
-
-
 def window(core, places, then):
     for c in range(2):
         @pl.when(core[0] == c)
@@ -185,44 +194,53 @@
             then(places[c])
 
 
-def cell_coefs(start, source, storage, perm, coef, fixed, inverse):
+def face(p, q):
+    return 2.0 * p * q / jnp.maximum(p + q, tiny)
+
+
+def cell_coefs(least, most, start, source, storage, perm, coef, fixed, inverse):
     keep_top = rows((32, 128)) < 31
-    for x in range(PLANES):
-        p = perm[x]
-        q = above(perm, x)
-        coef[0, x] = 2.0 * p * q / jnp.maximum(p + q, tiny)
-        q = roll(p, 31, 0)
-        coef[2, x] = jnp.where(keep_top, 2.0 * p * q / jnp.maximum(p + q, tiny), 0.0)
-        q = roll(p, 127)
-        coef[4, x] = 2.0 * p * q / jnp.maximum(p + q, tiny)
-    for x in range(PLANES):
-        coef[1, x] = coef[0, x - 1] if x > 0 else roll(coef[0, PLANES - 1], 64)
-        coef[3, x] = roll(coef[2, x], 1, 0)
-        coef[5, x] = roll(coef[4, x], 1)
-    for x in range(PLANES):
-        total = coef[0, x] + coef[1, x] + coef[2, x] + coef[3, x] + coef[4, x] + coef[5, x]
-        inv = jnp.where(storage[x] > 0.0, 1.0 / (storage[x] + stabilize + total), 0.0)
-        inverse[x] = inv
-        fixed[x] = source[x] + storage[x] * start[x]
-        for face in range(6):
-            coef[face, x] = coef[face, x] * inv
-
-
-def one_sweep(src, dst, coef, rhs):
-    for x in range(PLANES):
-        p = src[x]
-        total = rhs[x] + coef[0, x] * above(src, x) + coef[1, x] * below(src, x)
-        total = total + coef[2, x] * roll(p, 31, 0) + coef[3, x] * roll(p, 1, 0)
-        dst[x] = total + coef[4, x] * roll(p, 127) + coef[5, x] * roll(p, 1)
-
-
-def sweeps(press, coef, rhs):
-    def two(_, carry):
-        one_sweep(press.at[0], press.at[1], coef, rhs)
-        one_sweep(press.at[1], press.at[0], coef, rhs)
-        return carry
-
-    lax.fori_loop(0, SWEEPS // 2, two, 0)
+    outer = face(perm(least - 1), perm(least)) if least else jnp.zeros((32, 128), f32)
+    for x in range(least, most):
+        p = perm(x)
+        inner = face(p, perm(x + 1) if x < PLANES - 1 else roll(p, 64))
+        up = jnp.where(keep_top, face(p, roll(p, 31, 0)), 0.0)
+        deep = face(p, roll(p, 127))
+        coef[0, x - least] = inner
+        coef[1, x - least] = up
+        coef[2, x - least] = deep
+        total = inner + outer + up + roll(up, 1, 0) + deep + roll(deep, 1)
+        outer = inner
+        store = storage(x)
+        inverse[x - least] = jnp.where(store > 0.0, 1.0 / (store + stabilize + total), 0.0)
+        fixed[x - least] = source(x) + store * start(x)
+
+
+def both(early, late):
+    return lambda x: early[x] if x < EARLY else late[x - EARLY]
+
+
+def both_faces(early, late):
+    return lambda way, x: early[way, x] if x < EARLY else late[way, x - EARLY]
+
+
+def one_sweep(src, dst, coef, rhs, inverse, least):
+    outer = coef(0, least - 1) * src[least - 1]
+    p = src[least]
+    for x in range(least, PLANES):
+        q = src[x + 1] if x < PLANES - 1 else roll(p, 64)
+        inner, up, deep = coef(0, x), coef(1, x), coef(2, x)
+        total = rhs[x] + inner * q + outer
+        total = total + up * roll(p, 31, 0) + roll(up * p, 1, 0)
+        total = total + deep * roll(p, 127) + roll(deep * p, 1)
+        dst[x] = total * inverse(x)
+        outer = inner * p
+        p = q
+
+
+def sweeps(press, coef, rhs, inverse, first):
+    for n in range(SWEEPS):
+        one_sweep(press.at[n % 2], press.at[1 - n % 2], coef, rhs, inverse, first + n)
 
 
 def pair_matrix():
@@ -236,15 +254,16 @@
     return lanes(shape) % 128 // 32 == rows(shape) % 8 // 2
 
 
-def block_means(press, means):
-    sums = jnp.concatenate([press[2 * q] + press[2 * q + 1] for q in range(8)], axis=0)
+def block_means(press, means, least, most):
+    sums = jnp.concatenate([press[2 * q] + press[2 * q + 1] for q in range(3, 8)], axis=0)
     matrix = pair_matrix()
-    got = jnp.zeros((256, 256), f32)
+    got = jnp.zeros((160, 256), f32)
     for part in three_parts(sums):
         got = got + jnp.dot(part, matrix, preferred_element_type=f32)
-    got = jnp.where(row_mask((256, 256)), got, 0.0)
-    for b in range(3, 12):
-        piece = got[32 * (b % 8) : 32 * (b % 8) + 32, 128 * (b // 8) : 128 * (b // 8) + 128]
+    got = jnp.where(row_mask((160, 256)), got, 0.0)
+    for b in range(least, most + 1):
+        q, side = (b, 0) if b < 8 else (15 - b, 128)
+        piece = got[32 * q - 96 : 32 * q - 64, side : side + 128]
         for y in range(4):
             means[b, 0:1, 128 * y : 128 * y + 128] = jnp.sum(piece[8 * y : 8 * y + 8], axis=0, keepdims=True)
 
@@ -325,15 +344,17 @@
 
 def pack_mid(core, press, moved, out):
     low = low_mask((32, 128))
-    pairs = [jnp.where(low, press[12 + q], press[q]) for q in range(4)]
+    upper = rows((8, 512)) < 4
     extra = jnp.where(low, press[10], roll(press[11], 64))
     node = jnp.where(core[0] == 0, moved[1, 10], moved[1, 5])
+    pairs = [(moved[1, 6], moved[1, 7]), (moved[1, 8], moved[1, 9])]
+    held = [jnp.where(upper, a, roll(b, 4, 0)) for a, b in pairs] + [node]
     for y in range(4):
         for q in range(4):
-            out[y, q] = pairs[q][8 * y : 8 * y + 8]
-            out[y, 4 + q] = moved[1, 6 + q, :, 128 * y : 128 * y + 128]
-        out[y, 8] = extra[8 * y : 8 * y + 8]
-        out[y, 9] = node[:, 128 * y : 128 * y + 128]
+            out[y, q] = press[12 + q, 8 * y : 8 * y + 8]
+        out[y, 4] = extra[8 * y : 8 * y + 8]
+        for q in range(3):
+            out[y, 5 + q] = held[q][:, 128 * y : 128 * y + 128]
 
 
 def pack_last(press, moved, out):
@@ -344,7 +365,7 @@
             if x == 0:
                 tile = roll(press[12 + i], 16 * i - 24)
             else:
-                tile = roll(press[i], 16 * i - 88)
+                tile = roll(press[15 - i], 16 * i - 88)
             cells = jnp.where(lane // 16 == i, tile, cells)
         for y in range(4):
             total = cells[8 * y : 8 * y + 8]
@@ -355,151 +376,247 @@
             out[4 * x + y] = total
 
 
-def first_kernel(
-    core, ok, grid, halo, share, stiff, aux,
-    mid, coef, fixed, inverse, u, lam, mu, load, sup, safe, gain,
-    press, storage, perm, rhs, means, moved,
+def inside_flags(core, layer):
+    below = jnp.where(layer[0] > 0, 1.0, 0.0)
+    above = jnp.where(layer[0] < 7, 1.0, 0.0)
+    first = core[0] == 0
+    return jnp.where(first, below, above), jnp.where(first, above, below)
+
+
+def units_of(grid, halo, share, ok):
+    def plane(x):
+        return lambda y, at: grid[4 * x + y, at]
+
+    def near(y, at):
+        return halo[13 * y + at] * ok[0]
+
+    def middle(y, at):
+        return halo[52 + 10 * y + at] * ok[0] if at < 10 else jnp.zeros((8, 128), f32)
+
+    def far(y, at):
+        if at not in FAR:
+            return jnp.zeros((8, 128), f32)
+        return halo[92 + 6 * y + FAR.index(at)] * ok[0]
+
+    def beside(y, at):
+        return jnp.zeros((8, 128), f32) if share is None else share[13 * y + at] * ok[1]
+
+    inside = [plane(x) for x in range(4)]
+    return [[far, middle, near] + inside + [beside], [beside] + inside + [near, middle, far]]
+
+
+def unpack_cells(units, planes, press, source, storage, perm):
+    low = low_mask((32, 128))
+
+    def tile(cell, at):
+        return jnp.concatenate([units[cell // 4](y, at + cell % 4) for y in range(4)], axis=0)
+
+    for x in planes:
+        a = tile(x, 0)
+        b = tile(31 - x, 0)
+        press(x)[...] = jnp.where(low, a, roll(b, 64))
+        source(x)[...] = jnp.where(low, roll(a, 64), b)
+        a = tile(x, 4)
+        b = tile(31 - x, 4)
+        storage(x)[...] = jnp.where(low, a, roll(b, 64))
+        perm(x)[...] = jnp.where(low, roll(a, 64), b)
+
+
+def prepare_kernel(
+    core, layer, grid, halo, aux,
+    start, edge, coef, fixed, inverse, u, lam, mu, load, sup, safe, gain,
+    source, storage, perm,
 ):
-    low = low_mask((32, 128))
-
+    ok = inside_flags(core, layer)
     def unpack(units):
-        def read(unit, y, at):
-            ref, index, flag = units[unit]
-            value = ref[4 * index + y, at] if y is not None else ref[4 * index : 4 * index + 4, at]
-            return value if flag is None else value * ok[flag]
-
-        def tile(cell, at):
-            return read(cell // 4, None, at + cell % 4).reshape(32, 128)
-
-        for x in range(PLANES):
-            a = tile(x, 0)
-            b = tile(x + PLANES, 0)
-            press[0, x] = jnp.where(low, a, roll(b, 64))
-            rhs[x] = jnp.where(low, roll(a, 64), b)
-            a = tile(x, 4)
-            b = tile(x + PLANES, 4)
-            storage[x] = jnp.where(low, a, roll(b, 64))
-            perm[x] = jnp.where(low, roll(a, 64), b)
+        unpack_cells(
+            units, range(4, PLANES), lambda x: start.at[x - 4], lambda x: source.at[x],
+            lambda x: storage.at[x], lambda x: perm.at[x],
+        )
         sub = rows((8, 128))
         for unit in range(8):
             for y in range(4):
                 at = slice(128 * y, 128 * y + 128)
-                support = read(unit, y, 10)
                 for i in range(2):
                     n = 2 * unit + i
-                    tile_a = read(unit, y, 8 + i)
+                    tile_a = units[unit](y, 8 + i)
                     u[n, :, at] = jnp.where(sub < 3, tile_a, 0.0)
                     if 4 <= n <= 11:
                         load[n, :, at] = jnp.where(sub < 3, pltpu.roll(tile_a, 4, 0), 0.0)
-                        tile_b = support if i == 0 else pltpu.roll(support, 4, 0)
+                        tile_b = units[unit](y, 10)
+                        if i == 1:
+                            tile_b = pltpu.roll(tile_b, 4, 0)
                         sup[n, :, at] = jnp.where(sub < 3, tile_b, 0.0)
             if 1 <= unit <= 5:
                 for at, param in ((11, lam), (12, mu)):
-                    total = read(unit, 0, at) + read(unit, 1, at) + read(unit, 2, at) + read(unit, 3, at)
+                    total = units[unit](0, at) + units[unit](1, at) + units[unit](2, at) + units[unit](3, at)
                     for i in range(2):
                         for y in range(4):
                             row = 4 * i + y
                             param[2 * unit + i, :, 128 * y : 128 * y + 128] = total[row : row + 1]
 
-    below = [(halo, 0, 0), (halo, 1, 0), (halo, 2, 0)]
-    plane = [(grid, 0, None), (grid, 1, None), (grid, 2, None), (grid, 3, None)]
-    beside = [(share, 0, 1)]
-    window(core, [below + plane + beside, beside + plane + below], unpack)
-    cell_coefs(press.at[0], rhs, storage, perm, coef, fixed, inverse)
+    window(core, units_of(grid, halo, None, ok), unpack)
+    cell_coefs(
+        EARLY, PLANES, lambda x: start[x - 4], lambda x: source[x], lambda x: storage[x],
+        lambda x: perm[x], coef, fixed, inverse,
+    )
+    edge[0] = perm[4]
+    edge[1] = perm[5]
+    edge[2] = source[4]
+    edge[3] = storage[4]
+    diag_of(lam, mu, sup, aux, safe, gain)
+
+
+def first_kernel(
+    core, layer, halo, share, stiff, aux,
+    start, edge, coef_late, fixed_late, inverse_late, u, lam, mu, load, sup, safe, gain,
+    mid, coef_early, fixed_early, inverse_early, beside,
+    press, source, storage, perm, rhs, means, moved,
+):
+    ok = inside_flags(core, layer)
+    sub = rows((8, 128))
+
+    def unpack(units):
+        unpack_cells(
+            units, range(4), lambda x: press.at[0, x], lambda x: source.at[x],
+            lambda x: storage.at[x], lambda x: perm.at[x],
+        )
+
+    window(core, units_of(None, halo, share, ok), unpack)
+    for y in range(4):
+        for i in range(2):
+            tile = share[13 * y + 8 + i] * ok[1]
+            beside[i, :, 128 * y : 128 * y + 128] = jnp.where(sub < 3, tile, 0.0)
+    for x in range(4, PLANES):
+        press[0, x] = start[x - 4]
+    cell_coefs(
+        0, EARLY, lambda x: press[0, x],
+        lambda x: source[x] if x < 4 else edge[2], lambda x: storage[x] if x < 4 else edge[3],
+        lambda x: perm[x] if x < 4 else edge[x - 4], coef_early, fixed_early, inverse_early,
+    )
+    fixed = both(fixed_early, fixed_late)
     for x in range(PLANES):
-        rhs[x] = (fixed[x] + stabilize * press[0, x]) * inverse[x]
-    sweeps(press, coef, rhs)
-    block_means(press.at[0], means)
-    diag_of(lam, mu, sup, aux, safe, gain)
+        rhs[x] = fixed(x) + stabilize * press[0, x]
+    sweeps(press, both_faces(coef_early, coef_late), rhs, both(inverse_early, inverse_late), 1)
+    block_means(press.at[0], means, 3, 11)
     displacements(u, lam, mu, load, sup, safe, gain, means, stiff, aux, moved, 5, 10)
     pack_mid(core, press.at[0], moved, mid)
 
 
-def second_kernel(
-    core, ok, own, partner, near, across, stiff, aux,
-    coef, fixed, inverse, start, lam, mu, load, sup, safe, gain,
-    last, press, rhs, means, u, strain, moved,
-):
+def node_of(ref, k, y):
+    value = ref[y, 5 + k // 2]
+    return jnp.where(rows((8, 128)) < 4, roll(value, 4, 0) if k % 2 else value, 0.0)
+
+
+def strain_rows(aux, nodes, blocks, strain):
+    last_y = last_row((8, 512))
+    column = [jnp.broadcast_to(aux[8 * a : 8 * a + 8, 0:1], (8, 512)) for a in range(8)]
+    for b in blocks:
+        here, following = nodes(b), nodes(b + 1)
+        parts = [column[a] * here + column[4 + a] * following for a in range(4)]
+        total = (
+            parts[0]
+            + roll(parts[1], 511)
+            + jnp.where(last_y, 0.0, roll(parts[2] + roll(parts[3], 511), 480))
+        )
+        strain[b] = jnp.sum(total, axis=0, keepdims=True)
+
+
+def right_sides(strain, groups, press, fixed, rhs):
+    mask = row_mask((8, 128))
+    spread = []
+    for q in groups:
+        for y in range(4):
+            at = slice(128 * y, 128 * y + 128)
+            pair = [jnp.where(mask, strain[q, :, at], 0.0), jnp.where(mask, strain[15 - q, :, at], 0.0)]
+            spread.append(jnp.concatenate(pair, axis=1))
+    matrix = pair_matrix()
+    got = jnp.zeros((32 * len(groups), 128), f32)
+    for part in three_parts(jnp.concatenate(spread, axis=0)):
+        got = got + nt_dot(part, matrix)
+    for n, q in enumerate(groups):
+        change = got[32 * n : 32 * n + 32]
+        for x in (2 * q, 2 * q + 1):
+            rhs[x] = fixed(x) + stabilize * press[x] - (8.0 * biot_coef) * change
+
+
+def resume_kernel(core, layer, own, partner, near, aux, start, fixed_late, press, u, rhs, strain, moved):
+    ok = inside_flags(core, layer)
     low = low_mask((32, 128))
 
-    def unpack(runs, extra):
+    def unpack(runs, extra_cells, extra_node):
         def piece(cell, want_low):
-            if cell in extra["cells"]:
-                ref, q, is_low = extra["cells"][cell]
+            if cell in extra_cells:
+                ref, q, is_low = near, 4, cell == 2
             elif 4 <= cell < 28:
                 k = (cell - 4) % 8
-                ref, q, is_low = runs[(cell - 4) // 8][0], k % 4, k < 4
+                ref, q, is_low = runs[(cell - 4) // 8][0], min(k, 7 - k), k < 4
             else:
                 return jnp.zeros((32, 128), f32)
             value = ref[:, q].reshape(32, 128)
             return value if is_low == want_low else roll(value, 64)
 
-        for x in range(PLANES):
-            press[0, x] = jnp.where(low, piece(x, True), piece(x + PLANES, False))
-        for n in range(NODES):
-            if n in extra["nodes"]:
-                ref, q, flag = extra["nodes"][n]
+        for x in range(2, PLANES):
+            press[x] = jnp.where(low, piece(x, True), piece(31 - x, False))
+        for n in range(1, 15):
+            if n == extra_node:
+                ref, k, flag = near, 4, 0
             elif 2 <= n < 14:
-                (ref, flag), q = runs[(n - 2) // 4], 4 + (n - 2) % 4
+                (ref, flag), k = runs[(n - 2) // 4], (n - 2) % 4
             else:
                 u[n] = jnp.zeros((8, 512), f32)
                 continue
             for y in range(4):
-                value = ref[y, q]
+                value = node_of(ref, k, y)
                 u[n, :, 128 * y : 128 * y + 128] = value if flag is None else value * ok[flag]
 
     @pl.when(core[0] == 0)
     def _():
-        unpack(
-            [(near, 0), (own, None), (partner, None)],
-            {"cells": {2: (near, 8, True), 3: (near, 8, False)}, "nodes": {1: (near, 9, 0), 14: (across, 4, 1)}},
-        )
+        unpack([(near, 0), (own, None), (partner, None)], (2, 3), 1)
 
     @pl.when(core[0] == 1)
     def _():
-        unpack(
-            [(partner, None), (own, None), (near, 0)],
-            {"cells": {2: (across, 2, False), 3: (across, 3, False)}, "nodes": {1: (across, 7, 1), 14: (near, 9, 0)}},
-        )
-
-    strain[...] = jnp.zeros((PLANES, 1, 512), f32)
-    last_y = last_row((8, 512))
-    here = u[1] - start[1]
-    for b in range(1, 14):
-        following = u[b + 1] - start[b + 1]
-        parts = [
-            aux[8 * a : 8 * a + 8, 0:1] * here + aux[32 + 8 * a : 40 + 8 * a, 0:1] * following
-            for a in range(4)
-        ]
-        total = (
-            parts[0]
-            + roll(parts[1], 511)
-            + jnp.where(last_y, 0.0, roll(parts[2], 480) + roll(parts[3], 479))
-        )
-        strain[b] = jnp.sum(total, axis=0, keepdims=True)
-        here = following
-    mask = row_mask((8, 128))
-    spread = []
-    for q in range(8):
-        for y in range(4):
-            at = slice(128 * y, 128 * y + 128)
-            spread.append(
-                jnp.concatenate(
-                    [jnp.where(mask, strain[q, :, at], 0.0), jnp.where(mask, strain[8 + q, :, at], 0.0)],
-                    axis=1,
-                )
-            )
-    matrix = pair_matrix()
-    got = jnp.zeros((256, 128), f32)
-    for part in three_parts(jnp.concatenate(spread, axis=0)):
-        got = got + nt_dot(part, matrix)
-    for x in range(PLANES):
-        change = got[32 * (x // 2) : 32 * (x // 2) + 32]
-        right = fixed[x] + stabilize * press[0, x] - (8.0 * biot_coef) * change
-        rhs[x] = right * inverse[x]
-    sweeps(press, coef, rhs)
-    block_means(press.at[0], means)
-    displacements(u, lam, mu, load, sup, safe, gain, means, stiff, aux, moved, 6, 9)
+        unpack([(partner, None), (own, None), (near, 0)], (), 14)
+
+    for n in range(3, 14):
+        moved[n] = u[n] - start[n]
+    strain_rows(aux, lambda n: moved[n], range(3, 13), strain)
+    right_sides(strain, range(3, 8), press, lambda x: fixed_late[x - EARLY], rhs)
+
+
+def second_kernel(
+    core, layer, across, stiff, aux, held, u, rhs_late,
+    coef_late, fixed_late, inverse_late, start, lam, mu, load, sup, safe, gain,
+    coef_early, fixed_early, inverse_early, beside,
+    last, press, rhs, means, nodes, strain, moved,
+):
+    ok = inside_flags(core, layer)
+    low = low_mask((32, 128))
+    first = core[0] == 0
+    for x in range(2, PLANES):
+        press[0, x] = held[x]
+    for x in range(6, PLANES):
+        rhs[x] = rhs_late[x]
+    for n in range(2, 14):
+        nodes[n] = u[n]
+
+    for x, q in ((2, 1), (3, 0)):
+        turned = roll(across[:, q].reshape(32, 128), 64)
+        press[0, x] = jnp.where(low & jnp.logical_not(first), turned, held[x])
+    for y in range(4):
+        at = slice(128 * y, 128 * y + 128)
+        nodes[1, :, at] = jnp.where(first, u[1, :, at], node_of(across, 3, y) * ok[1])
+        nodes[14, :, at] = jnp.where(first, node_of(across, 0, y) * ok[1], u[14, :, at])
+    for n in (2, 3, 13):
+        moved[0, n] = nodes[n] - start[n]
+    moved[0, 1] = nodes[1] - jnp.where(first, start[1], beside[1])
+    moved[0, 14] = nodes[14] - jnp.where(first, beside[0], start[14])
+    strain[14] = jnp.zeros((1, 512), f32)
+    strain_rows(aux, lambda n: moved[0, n], (1, 2, 13), strain)
+    right_sides(strain, (1, 2), press.at[0], both(fixed_early, fixed_late), rhs)
+    sweeps(press, both_faces(coef_early, coef_late), rhs, both(inverse_early, inverse_late), 3)
+    block_means(press.at[0], means, 4, 10)
+    displacements(nodes, lam, mu, load, sup, safe, gain, means, stiff, aux, moved, 6, 9)
     pack_last(press.at[0], moved, last)
 
 
@@ -532,6 +649,10 @@
     return jnp.pad(vec.reshape(3, 8).T, ((0, 0), (0, 5))).reshape(64)
 
 
+def pick_far(tiles):
+    return jnp.concatenate([tiles[:, 2:4], tiles[:, 6:10]], axis=1)
+
+
 def shape(*dims):
     return jax.ShapeDtypeStruct(dims, f32)
 
@@ -543,16 +664,14 @@
     core = lax.axis_index("grp")
     layer = lax.axis_index("gz")
     core_arg = jnp.full((1,), core, jnp.int32)
-    has_below, has_above = layer > 0, layer < 7
-    ok = jnp.stack(
-        [jnp.where(core == 0, has_below, has_above), jnp.where(core == 0, has_above, has_below)]
-    ).astype(f32)
+    row_arg = jnp.full((1,), lax.axis_index("gy"), jnp.int32)
+    layer_arg = jnp.full((1,), layer, jnp.int32)
     swap = [(0, 1), (1, 0)]
 
     cells, nodes = call(
         stage_kernel,
         (shape(16, 8, 128), shape(16, 512)),
-        [pl.BlockSpec(memory_space=pltpu.HBM)] * 10,
+        [HB] * 10,
         [
             pltpu.VMEM((4, 8, 128), jnp.int32),
             pltpu.VMEM((3, 3, 512), f32),
@@ -560,53 +679,84 @@
             pltpu.SMEM((CLASSES,), f32),
             pltpu.SemaphoreType.DMA((10,)),
         ],
-        64 * 1024 * 1024 - 65536,
+        WHOLE,
     )(class_perm, pressure_start, source, storage, perm_class, displacement_start, load, support,
       lame_lambda, lame_mu)
     cells_other = lax.ppermute(cells, "grp", swap)
     nodes_other = lax.ppermute(nodes, "grp", swap)
-    routes = lax.dynamic_index_in_dim(
-        block_route[0].reshape(8, 2, 4, 64), lax.axis_index("gy"), 2, keepdims=False
-    ).transpose(1, 0, 2).reshape(2, 512)
-    packed = call(pack_kernel, shape(16, TILES, 8, 128), [SM] + [VM] * 5)(
-        core_arg, cells, cells_other, nodes, nodes_other, routes
-    )
+    packed = call(
+        pack_kernel,
+        shape(16, TILES, 8, 128),
+        [SM, SM] + [HB] * 5,
+        [
+            pltpu.VMEM((16, 8, 128), f32),
+            pltpu.VMEM((16, 8, 128), f32),
+            pltpu.VMEM((16, 512), f32),
+            pltpu.VMEM((16, 512), f32),
+            pltpu.VMEM((1, 8, 512), jnp.int32),
+            pltpu.SemaphoreType.DMA((5,)),
+        ],
+        WHOLE,
+    )(core_arg, row_arg, cells, cells_other, nodes, nodes_other, block_route)
     grid = lax.all_to_all(packed, ("gx", "gy"), 0, 0, tiled=True)
 
     ring = [(8 + z, (z + 1) % 8) for z in range(8)] + [(z, 8 + (z - 1) % 8) for z in range(8)]
-    halo = lax.ppermute(lax.dynamic_slice_in_dim(grid, 4 * core, 12, 0), ("grp", "gz"), ring)
-    share = lax.ppermute(lax.dynamic_slice_in_dim(halo, 8 * (1 - core), 4, 0), "grp", swap)
+    sent = [
+        lax.dynamic_slice_in_dim(grid, 12 * core, 4, 0),
+        lax.dynamic_slice_in_dim(grid, 4 + 4 * core, 4, 0)[:, :10],
+        pick_far(lax.dynamic_slice_in_dim(grid, 8 - 4 * core, 4, 0)),
+    ]
+    sent = jnp.concatenate([part.reshape(-1, 8, 128) for part in sent], axis=0)
+    halo = lax.ppermute(sent, ("grp", "gz"), ring)
+    share = lax.ppermute(halo[:52], "grp", swap)
 
     stiff = jnp.concatenate([corner_major(stiff_lambda), corner_major(stiff_mu)], axis=0)
     columns = [corner_column(coupling_vec), corner_column(jnp.diag(stiff_lambda)), corner_column(jnp.diag(stiff_mu))]
     aux = jnp.pad(jnp.stack(columns, axis=1), ((0, 0), (0, 125)))
 
-    kept = (
-        shape(6, PLANES, 32, 128), shape(PLANES, 32, 128), shape(PLANES, 32, 128),
-        shape(NODES, 8, 512), shape(12, 1, 512), shape(12, 1, 512), shape(12, 8, 512),
-        shape(12, 8, 512), shape(12, 8, 512), shape(12, 8, 512),
-    )
-    mid, *statics = call(
+    late = PLANES - EARLY
+    statics = call(
+        prepare_kernel,
+        (
+            shape(PLANES - 4, 32, 128), shape(4, 32, 128),
+            shape(3, late, 32, 128), shape(late, 32, 128), shape(late, 32, 128),
+            shape(NODES, 8, 512), shape(12, 1, 512), shape(12, 1, 512), shape(12, 8, 512),
+            shape(12, 8, 512), shape(12, 8, 512), shape(12, 8, 512),
+        ),
+        [SM, SM] + [VM] * 3,
+        [pltpu.VMEM((PLANES, 32, 128), f32)] * 3,
+    )(core_arg, layer_arg, grid, halo, aux)
+    mid, *early = call(
         first_kernel,
-        (shape(4, 10, 8, 128),) + kept,
-        [SM, SM] + [VM] * 5,
+        (
+            shape(4, 8, 8, 128), shape(3, EARLY, 32, 128), shape(EARLY, 32, 128),
+            shape(EARLY, 32, 128), shape(2, 8, 512),
+        ),
+        [SM, SM] + [VM] * 16,
         [
             pltpu.VMEM((2, PLANES, 32, 128), f32),
-            pltpu.VMEM((PLANES, 32, 128), f32),
-            pltpu.VMEM((PLANES, 32, 128), f32),
+            pltpu.VMEM((4, 32, 128), f32),
+            pltpu.VMEM((4, 32, 128), f32),
+            pltpu.VMEM((4, 32, 128), f32),
             pltpu.VMEM((PLANES, 32, 128), f32),
             pltpu.VMEM((PLANES, 1, 512), f32),
             pltpu.VMEM((2, NODES, 8, 512), f32),
         ],
-    )(core_arg, ok, grid, halo, share, stiff, aux)
+    )(core_arg, layer_arg, halo, share, stiff, aux, *statics)
 
     near = lax.ppermute(mid, ("grp", "gz"), ring)
     partner = lax.ppermute(mid, "grp", swap)
     across = lax.ppermute(near, "grp", swap)
+    resumed = call(
+        resume_kernel,
+        (shape(PLANES, 32, 128), shape(NODES, 8, 512), shape(PLANES, 32, 128)),
+        [SM, SM] + [VM] * 6,
+        [pltpu.VMEM((PLANES, 1, 512), f32), pltpu.VMEM((NODES, 8, 512), f32)],
+    )(core_arg, layer_arg, mid, partner, near, aux, statics[5], statics[3])
     last = call(
         second_kernel,
         shape(8, 8, 128),
-        [SM, SM] + [VM] * 16,
+        [SM, SM] + [VM] * 20,
         [
             pltpu.VMEM((2, PLANES, 32, 128), f32),
             pltpu.VMEM((PLANES, 32, 128), f32),
@@ -615,7 +765,7 @@
             pltpu.VMEM((PLANES, 1, 512), f32),
             pltpu.VMEM((2, NODES, 8, 512), f32),
         ],
-    )(core_arg, ok, mid, partner, near, across, stiff, aux, *statics)
+    )(core_arg, layer_arg, across, stiff, aux, *resumed, *statics[2:], *early)
 
     other = lax.ppermute(last, "grp", swap)
     whole = jnp.concatenate([jnp.where(core == 0, last, other), jnp.where(core == 0, other, last)], axis=0)

time: 73.3 us -> 66.7 us (0.910)
  waiting for transfers between devices: 21.6 us -> 18.6 us
  local copies, waits for them, and re-layouts: 5.89 us -> 4 us
  Pallas kernels: 11.9 us -> 10.9 us
    ppermute x2, waiting for transfers between devices: 5.96 us -> 2.63 us  [the longest x1 2.63 us: shards(): halo = lax.ppermute(sent, ('grp', 'gz'), ring)]
    ppermute x1, starting transfers between devices: 0.1 us -> 3.33 us  [shards(): cells_other = lax.ppermute(cells, 'grp', swap)]
    ppermute x1, starting transfers between devices: 3.33 us -> 0.1 us  [shards(): nodes_other = lax.ppermute(nodes, 'grp', swap)]
    ppermute x1, waiting for transfers between devices: 0.06 us -> 1.45 us  [shards(): nodes_other = lax.ppermute(nodes, 'grp', swap)]
    pallas_call x4 -> x6, Pallas kernels: 11.2 us -> 10.1 us  [the longest x1 2.68 us: shards(): call(pack_kernel, shape(16, TILES, 8, 128), [SM, SM] + [HB] * 5, [pltpu.V...]
    unnamed x16 -> x12, local copies, waits for them, and re-layouts: 2.29 us -> 1.28 us
    another operation x1 -> x0, local copies, waits for them, and re-layouts: 0.8 us -> none  [shards(): block_route[0].reshape(8, 2, 4, 64)]
  transfers between devices with their start and end apart: 9 -> 9, of which waited for: 7 -> 5; matrix products, arithmetic and copies ran while one was open for 6% -> 5% of each run, Pallas kernels for 0% -> 3%
where the time goes in v1:
time: 66.7 us; the launch traced here: 66.3 us
  starting transfers between devices  22.3 us (33%)
  waiting for transfers between devices  18.6 us (28%)
  Pallas kernels  10.9 us (16%)
  blocking collectives  9.6 us (14%)
  local copies, waits for them, and re-layouts  4 us (6%)
  between operations  0.82 us (1%)
    all_to_all x1, waiting for transfers between devices, shards(): grid = lax.all_to_all(packed, ('gx', 'gy'), 0, 0, tiled=True)  13.3 us
    all_to_all x1, blocking collectives, shards(): back = lax.all_to_all(whole, ('gx', 'gy'), 0, 0, tiled=True)  9.6 us
    all_to_all x1, starting transfers between devices, shards(): grid = lax.all_to_all(packed, ('gx', 'gy'), 0, 0, tiled=True)  5.04 us
    ppermute x1, starting transfers between devices, shards(): halo = lax.ppermute(sent, ('grp', 'gz'), ring)  4.69 us
    ppermute x1, starting transfers between devices, shards(): partner = lax.ppermute(mid, 'grp', swap)  4.17 us
    ppermute x1, starting transfers between devices, shards(): cells_other = lax.ppermute(cells, 'grp', swap)  3.33 us
    pallas_call x1, Pallas kernels, shards(): call(pack_kernel, shape(16, TILES, 8, 128), [SM, SM] + [HB] * 5, [pltpu.V...  2.68 us
    ppermute x1, starting transfers between devices, shards(): across = lax.ppermute(near, 'grp', swap)  2.65 us
  transfers between devices with their start and end apart: 9, of which 5 were waited for; matrix products, arithmetic and copies ran while one was open for 5% of the time, Pallas kernels for 3%

profile of v1, /device:TPU:1, one launch (start us, length us, event | category | flops | bytes accessed | tf_op | source)
XLA Modules:
  0.0 66.3 jit_solution(16817397607496183823)
XLA Ops:
  0.6 1.6 %shard_map.149 = (f32[16,8,128]{2,1,0:T(8,128)}, f32[16,512]{1,0:T(8,128)}) custom-call(f32[16]{0:T(128)} %perms.1, f32[4,8,128]{2,1,0:T(8,128)} %p0.1, f32[4,8,128]{2,1,0:T(8,128)} %src.1, f32[4,8,128]{2,1,0:T(8,128)} %sto.1, s32[4,8,128]{2,1,0:T(8,128)} %cls.1, f32[3,512]{1,0:T(4,128)} %disp.1, f32[3,512]{1,0:T(4,128)} %load.1, f32[3,512]{1,0:T(4,128)} %sup.1, ...), custom_call_target="tpu_custom_call" | custom-call | tf_op jit(solution)/shard_map/pallas_call | solution.py:671
  2.2 3.3 %collective-permute-start = (f32[16,8,128]{2,1,0:T(8,128)}, f32[16,8,128]{2,1,0:T(8,128)}, u32[]{:S(2)}, u32[]{:S(2)}) collective-permute-start(f32[16,8,128]{2,1,0:T(8,128)} %get-tuple-element.24.a), channel_id=1, source_target_pairs={{0,128},{128,0},{1,129},{129,1},{2,130},{130,2},{3,131},{131,3},{4... | collective-permute-start | bytes 196616 | tf_op jit(solution)/shard_map/ppermute | solution.py:685
  5.5 0.1 collective-permute-start.1
  5.6 1.4 %collective-permute-done.1.d = f32[16,512]{1,0:T(8,128)} collective-permute-done((f32[16,512]{1,0:T(8,128)}, f32[16,512]{1,0:T(8,128)}, u32[]{:S(2)}, u32[]{:S(2)}) %collective-permute-start.1) | collective-permute-done | bytes 32800 | tf_op jit(solution)/shard_map/ppermute | solution.py:686
  7.1 0.0 collective-permute-done.b
  7.1 2.7 %shard_map.150 = f32[16,13,8,128]{3,2,1,0:T(8,128)} custom-call(s32[1]{0:T(128)} %bitcast.core, s32[1]{0:T(128)} %bitcast.2.across, f32[16,8,128]{2,1,0:T(8,128)} %get-tuple-element.24.a, f32[16,8,128]{2,1,0:T(8,128)} %collective-permute-done.b, f32[16,512]{1,0:T(8,128)} %get-tuple-element.25.c, f32[16,512]{1,0:T(8,128)} %collective-permute-done.1.d, ...), custom_call_target="tpu_custom_call" | custom-call | tf_op jit(solution)/shard_map/pallas_call | solution.py:687
  9.8 5.0 %all-to-all-start = ((f32[16,13,8,128]{3,2,1,0:T(8,128)}), f32[16,13,8,128]{3,2,1,0:T(8,128)S(1)}, u32[]{:S(2)}, u32[]{:S(2)}) async-start(f32[16,13,8,128]{3,2,1,0:T(8,128)} %shard_map.150), calls=%async_computation | async-start | bytes 1703936 | tf_op jit(solution)/shard_map/all_to_all | solution.py:701
  14.8 13.3 %all-to-all-done.grid = f32[16,13,8,128]{3,2,1,0:T(8,128)S(1)} async-done(((f32[16,13,8,128]{3,2,1,0:T(8,128)}), f32[16,13,8,128]{3,2,1,0:T(8,128)S(1)}, u32[]{:S(2)}, u32[]{:S(2)}) %all-to-all-start) | async-done | bytes 852000 | tf_op jit(solution)/shard_map/all_to_all | solution.py:701
  28.2 0.0 copy-start
  28.2 4.7 %collective-permute-start.2 = (f32[116,8,128]{2,1,0:T(8,128)S(1)}, f32[116,8,128]{2,1,0:T(8,128)S(1)}, u32[]{:S(2)}, u32[]{:S(2)}) collective-permute-start(f32[116,8,128]{2,1,0:T(8,128)S(1)} %pad_maximum_fusion), channel_id=1, source_target_pairs={{128,16},{144,32},{160,48},{176,64},{192,80},{208,96},{224,112},{2... | collective-permute-start | bytes 1425416 | tf_op jit(solution)/shard_map/ppermute | solution.py:710
  32.9 0.0 copy-done
  32.9 0.1 reshape.37
  33.0 0.0 copy-start.1
  33.0 0.8 %gather_fusion = f32[24]{0:T(128)S(1)} fusion(f32[24,24]{1,0:T(8,128)S(1)} %copy-done, s32[24]{0:T(128)S(1)} %or_bitcast_fusion), kind=kCustom, calls=%fused_computation | custom fusion | bytes 384 | tf_op jit(solution)/shard_map/jit(_diag)/jit(diagonal)/cond/branch_0_fun/gather | solution.py:714
  33.8 0.0 copy-done.1
  33.8 0.8 %gather_fusion.1 = f32[24]{0:T(128)S(1)} fusion(f32[24,24]{1,0:T(8,128)S(1)} %copy-done.1, s32[24]{0:T(128)S(1)} %or_bitcast_fusion), kind=kCustom, calls=%fused_computation.1 | custom fusion | bytes 384 | tf_op jit(solution)/shard_map/jit(_diag)/jit(diagonal)/cond/branch_0_fun/gather | solution.py:714
  34.6 0.1 reshape.39
  34.7 0.1 reshape.42
  34.8 0.1 copy.41
  34.9 0.1 stack_reshape.10
  35.0 0.1 reshape.43
  35.0 0.1 copy.42
  35.1 0.0 copy-start.2
  35.1 0.1 stack_reshape.11
  35.2 0.6 copy-done.2
  35.8 0.1 reshape.41
  35.9 0.1 copy.40
  36.0 0.1 stack_reshape.9
  36.1 0.1 copy.37
  36.2 0.2 copy.38
  36.4 0.1 reshape.38
  36.6 0.2 copy.39
  36.8 0.1 reshape.40
  36.9 2.6 %collective-permute-done.2.halo = f32[116,8,128]{2,1,0:T(8,128)S(1)} collective-permute-done((f32[116,8,128]{2,1,0:T(8,128)S(1)}, f32[116,8,128]{2,1,0:T(8,128)S(1)}, u32[]{:S(2)}, u32[]{:S(2)}) %collective-permute-start.2) | collective-permute-done | bytes 475168 | tf_op jit(solution)/shard_map/ppermute | solution.py:710
  39.6 1.2 %collective-permute-start.3 = (f32[52,8,128]{2,1,0:T(8,128)S(1)}, f32[52,8,128]{2,1,0:T(8,128)S(1)}, u32[]{:S(2)}, u32[]{:S(2)}) collective-permute-start(f32[52,8,128]{2,1,0:T(8,128)S(1)} %slice.20), channel_id=1, source_target_pairs={{0,128},{128,0},{1,129},{129,1},{2,130},{130,2},{3,131},{131,3},{4... | collective-permute-start | bytes 638984 | tf_op jit(solution)/shard_map/ppermute | solution.py:711
  40.8 1.3 %shard_map.151 = (f32[12,32,128]{2,1,0:T(8,128)S(1)}, f32[4,32,128]{2,1,0:T(8,128)S(1)}, f32[3,11,32,128]{3,2,1,0:T(8,128)S(1)}, f32[11,32,128]{2,1,0:T(8,128)S(...) custom-call(s32[1]{0:T(128)} %bitcast.core, ...), custom_call_target="tpu_custom_call" | custom-call | tf_op jit(solution)/shard_map/pallas_call | solution.py:718
  42.1 0.0 collective-permute-done.3.share
  42.2 2.2 %shard_map.152 = (f32[4,8,8,128]{3,2,1,0:T(8,128)S(1)}, f32[3,5,32,128]{3,2,1,0:T(8,128)S(1)}, f32[5,32,128]{2,1,0:T(8,128)S(1)}, f32[5,32,128]{2,1,0:T(8,128)S(1)}, f32[2,8,512]{2,1,0:T(8,128)S(1)}) custom-call(s32[1]{0:T(128)} %bitcast.core, s32[1]{0:T(128)} %bitcast.1.layer, f32[116,8,128]{2,1,0:T(8,128)S(1)} %collective-permute-done.2.halo, ...), custom_call_target="tpu_custom_call" | custom-call | tf_op jit(solution)/shard_map/pallas_call | solution.py:729
  44.3 0.7 %collective-permute-start.4 = (f32[4,8,8,128]{3,2,1,0:T(8,128)S(1)}, f32[4,8,8,128]{3,2,1,0:T(8,128)S(1)}, u32[]{:S(2)}, u32[]{:S(2)}) collective-permute-start(f32[4,8,8,128]{3,2,1,0:T(8,128)S(1)} %get-tuple-element.38.own), channel_id=1, source_target_pairs={{128,16},{144,32},{160,48},{176,64},{192,80},{208,96},{224,112},{2... | collective-permute-start | bytes 393224 | tf_op jit(solution)/shard_map/ppermute | solution.py:747
  45.0 4.2 %collective-permute-start.6 = (f32[4,8,8,128]{3,2,1,0:T(8,128)S(1)}, f32[4,8,8,128]{3,2,1,0:T(8,128)S(1)}, u32[]{:S(2)}, u32[]{:S(2)}) collective-permute-start(f32[4,8,8,128]{3,2,1,0:T(8,128)S(1)} %get-tuple-element.38.own), channel_id=1, source_target_pairs={{0,128},{128,0},{1,129},{129,1},{2,130},{130,2},{3,131},{131,3},{4... | collective-permute-start | bytes 393224 | tf_op jit(solution)/shard_map/ppermute | solution.py:748
  49.2 0.0 collective-permute-done.4.near
  49.2 2.6 %collective-permute-start.5 = (f32[4,8,8,128]{3,2,1,0:T(8,128)S(1)}, f32[4,8,8,128]{3,2,1,0:T(8,128)S(1)}, u32[]{:S(2)}, u32[]{:S(2)}) collective-permute-start(f32[4,8,8,128]{3,2,1,0:T(8,128)S(1)} %collective-permute-done.4.near), channel_id=1, source_target_pairs={{0,128},{128,0},{1,129},{129,1},{2,130},{130,2},{3,131},{131,3},{4... | collective-permute-start | bytes 393224 | tf_op jit(solution)/shard_map/ppermute | solution.py:749
  51.8 0.0 collective-permute-done.6.partner
  51.8 0.6 shard_map.153
  52.4 0.4 collective-permute-done.5.across
  52.8 1.8 %shard_map.154 = f32[8,8,128]{2,1,0:T(8,128)S(1)} custom-call(s32[1]{0:T(128)} %bitcast.core, s32[1]{0:T(128)} %bitcast.1.layer, f32[4,8,8,128]{3,2,1,0:T(8,128)S(1)} %collective-permute-done.5.across, f32[128,64]{1,0:T(8,128)S(1)} %constant_dynamic-update-slice_fusion.stiff, f32[64,128]{1,0:T(8,128)S(1)} %pad.26.aux, ...), custom_call_target="tpu_custom_call" | custom-call | tf_op jit(solution)/shard_map/pallas_call | solution.py:756
  54.7 0.4 collective-permute-start.7
  55.1 0.9 %collective-permute-done.7 = f32[8,8,128]{2,1,0:T(8,128)S(1)} collective-permute-done((f32[8,8,128]{2,1,0:T(8,128)S(1)}, f32[8,8,128]{2,1,0:T(8,128)S(1)}, u32[]{:S(2)}, u32[]{:S(2)}) %collective-permute-start.7) | collective-permute-done | bytes 32800 | tf_op jit(solution)/shard_map/ppermute | solution.py:770
  56.0 9.6 %all_to_all.10.got = f32[16,8,128]{2,1,0:T(8,128)S(1)} all-to-all(f32[16,8,128]{2,1,0:T(8,128)S(1)} %pad_maximum_fusion.2), channel_id=1, replica_groups=mesh['grp'=2,'gz'=8,'gx'=4,'gy'=4] {'gx','gy'}, dimensions={0} | all-to-all | bytes 131072 | tf_op jit(solution)/shard_map/all_to_all | solution.py:772
  65.6 0.8 %shard_map.155 = (f32[4,8,128]{2,1,0:T(8,128)}, f32[3,512]{1,0:T(4,128)}) custom-call(s32[1]{0:T(128)} %bitcast.core, f32[16,8,128]{2,1,0:T(8,128)S(1)} %all_to_all.10.got), custom_call_target="tpu_custom_call" | custom-call | tf_op jit(solution)/shard_map/pallas_call | solution.py:773
  (19 shorter events, 0.2 us)
Async XLA Ops:
  2.2 4.9 %collective-permute-start = (f32[16,8,128]{2,1,0:T(8,128)}, f32[16,8,128]{2,1,0:T(8,128)}, u32[]{:S(2)}, u32[]{:S(2)}) collective-permute-start(f32[16,8,128]{2,1,0:T(8,128)} %get-tuple-element.24.a), channel_id=1, source_target_pairs={{0,128},{128,0},{1,129},{129,1},{2,130},{130,2},{3,131},{131,3},{4... | collective-permute-start | bytes 196616 | tf_op jit(solution)/shard_map/ppermute | solution.py:685
  5.5 1.6 %collective-permute-start.1 = (f32[16,512]{1,0:T(8,128)}, f32[16,512]{1,0:T(8,128)}, u32[]{:S(2)}, u32[]{:S(2)}) collective-permute-start(f32[16,512]{1,0:T(8,128)} %get-tuple-element.25.c), channel_id=1, source_target_pairs={{0,128},{128,0},{1,129},{129,1},{2,130},{130,2},{3,131},{131,3},{4... | collective-permute-start | bytes 98312 | tf_op jit(solution)/shard_map/ppermute | solution.py:686
  9.8 18.3 %all-to-all-start = ((f32[16,13,8,128]{3,2,1,0:T(8,128)}), f32[16,13,8,128]{3,2,1,0:T(8,128)S(1)}, u32[]{:S(2)}, u32[]{:S(2)}) async-start(f32[16,13,8,128]{3,2,1,0:T(8,128)} %shard_map.150), calls=%async_computation | async-start | bytes 1703936 | tf_op jit(solution)/shard_map/all_to_all | solution.py:701
  28.2 4.7 %copy-start = (f32[24,24]{1,0:T(8,128)S(1)}, f32[24,24]{1,0:T(8,128)}, u32[]{:S(2)}) copy-start(f32[24,24]{1,0:T(8,128)} %param.25) | copy-start | bytes 6916
  28.2 11.3 %collective-permute-start.2 = (f32[116,8,128]{2,1,0:T(8,128)S(1)}, f32[116,8,128]{2,1,0:T(8,128)S(1)}, u32[]{:S(2)}, u32[]{:S(2)}) collective-permute-start(f32[116,8,128]{2,1,0:T(8,128)S(1)} %pad_maximum_fusion), channel_id=1, source_target_pairs={{128,16},{144,32},{160,48},{176,64},{192,80},{208,96},{224,112},{2... | collective-permute-start | bytes 1425416 | tf_op jit(solution)/shard_map/ppermute | solution.py:710
  33.0 0.8 %copy-start.1 = (f32[24,24]{1,0:T(8,128)S(1)}, f32[24,24]{1,0:T(8,128)}, u32[]{:S(2)}) copy-start(f32[24,24]{1,0:T(8,128)} %param.26) | copy-start | bytes 6916
  35.1 0.7 copy-start.2
  39.6 2.6 %collective-permute-start.3 = (f32[52,8,128]{2,1,0:T(8,128)S(1)}, f32[52,8,128]{2,1,0:T(8,128)S(1)}, u32[]{:S(2)}, u32[]{:S(2)}) collective-permute-start(f32[52,8,128]{2,1,0:T(8,128)S(1)} %slice.20), channel_id=1, source_target_pairs={{0,128},{128,0},{1,129},{129,1},{2,130},{130,2},{3,131},{131,3},{4... | collective-permute-start | bytes 638984 | tf_op jit(solution)/shard_map/ppermute | solution.py:711
  44.3 4.9 %collective-permute-start.4 = (f32[4,8,8,128]{3,2,1,0:T(8,128)S(1)}, f32[4,8,8,128]{3,2,1,0:T(8,128)S(1)}, u32[]{:S(2)}, u32[]{:S(2)}) collective-permute-start(f32[4,8,8,128]{3,2,1,0:T(8,128)S(1)} %get-tuple-element.38.own), channel_id=1, source_target_pairs={{128,16},{144,32},{160,48},{176,64},{192,80},{208,96},{224,112},{2... | collective-permute-start | bytes 393224 | tf_op jit(solution)/shard_map/ppermute | solution.py:747
  45.0 6.8 %collective-permute-start.6 = (f32[4,8,8,128]{3,2,1,0:T(8,128)S(1)}, f32[4,8,8,128]{3,2,1,0:T(8,128)S(1)}, u32[]{:S(2)}, u32[]{:S(2)}) collective-permute-start(f32[4,8,8,128]{3,2,1,0:T(8,128)S(1)} %get-tuple-element.38.own), channel_id=1, source_target_pairs={{0,128},{128,0},{1,129},{129,1},{2,130},{130,2},{3,131},{131,3},{4... | collective-permute-start | bytes 393224 | tf_op jit(solution)/shard_map/ppermute | solution.py:748
  49.2 3.6 %collective-permute-start.5 = (f32[4,8,8,128]{3,2,1,0:T(8,128)S(1)}, f32[4,8,8,128]{3,2,1,0:T(8,128)S(1)}, u32[]{:S(2)}, u32[]{:S(2)}) collective-permute-start(f32[4,8,8,128]{3,2,1,0:T(8,128)S(1)} %collective-permute-done.4.near), channel_id=1, source_target_pairs={{0,128},{128,0},{1,129},{129,1},{2,130},{130,2},{3,131},{131,3},{4... | collective-permute-start | bytes 393224 | tf_op jit(solution)/shard_map/ppermute | solution.py:749
  54.7 1.3 %collective-permute-start.7 = (f32[8,8,128]{2,1,0:T(8,128)S(1)}, f32[8,8,128]{2,1,0:T(8,128)S(1)}, u32[]{:S(2)}, u32[]{:S(2)}) collective-permute-start(f32[8,8,128]{2,1,0:T(8,128)S(1)} %shard_map.154), channel_id=1, source_target_pairs={{0,128},{128,0},{1,129},{129,1},{2,130},{130,2},{3,131},{131,3},{4... | collective-permute-start | bytes 98312 | tf_op jit(solution)/shard_map/ppermute | solution.py:770

commit v2 on v1

--- a/solution.py
+++ b/solution.py
@@ -30,12 +30,12 @@
 WHOLE = 64 * 1024 * 1024 - 65536
 
 
-def call(body, out_shapes, in_specs, scratch=(), budget=40 * 1024 * 1024):
+def call(body, out_shapes, in_specs, scratch=(), budget=40 * 1024 * 1024, out_spec=VM):
     return pl.pallas_call(
         body,
         out_shape=out_shapes,
         in_specs=in_specs,
-        out_specs=jax.tree.map(lambda _: VM, out_shapes),
+        out_specs=jax.tree.map(lambda _: out_spec, out_shapes),
         scratch_shapes=list(scratch),
         compiler_params=pltpu.CompilerParams(vmem_limit_bytes=budget),
     )
@@ -96,13 +96,19 @@
     nodes[8:11] = small[2]
 
 
-def pack_kernel(core, across, a, b, c, d, e, out, cells, cells_other, nodes, nodes_other, routes, sems):
+def pack_kernel(core, across, layer, a, b, c, d, e, packed, cells, cells_other, nodes, nodes_other, routes, out, sems, done):
     pairs = [(a, cells), (b, cells_other), (c, nodes), (d, nodes_other), (e, routes)]
     copies = [pltpu.make_async_copy(src, dst, sems.at[n]) for n, (src, dst) in enumerate(pairs)]
     for copy in copies:
         copy.start()
     for copy in copies:
         copy.wait()
+    sent = []
+
+    def send(at):
+        sent.append(pltpu.make_async_copy(out.at[:, at], packed.at[:, at], done.at[at]))
+        sent[-1].start()
+
     first = core[0] == 0
     lane = lanes((8, 128))
     low = lane < 64
@@ -155,6 +161,7 @@
                         win = jnp.where(in_high, roll(tiles[member][1], shift), win)
                     found.append(win)
                 out[chip, 4 * pair + i] = jnp.where(low, found[0], found[1])
+            send(4 * pair + i)
 
     def full_depth(i, r):
         full = []
@@ -181,6 +188,9 @@
             for j in range(4):
                 tile = jnp.where(lane // 32 == j, roll(full[j], 32 * j - start), tile)
             out[chip, 8 + at] = jnp.where((spot >= 0) & (spot < 128), tile, 0.0)
+        send(8 + at)
+    for copy in sent:
+        copy.wait()
 
 
 def low_mask(shape):
@@ -283,13 +293,12 @@
 
 
 def assembled(here, under):
-    summed = here[0:32] + under[32:64]
+    summed = [here[8 * j : 8 * j + 8] + roll(under[8 * j : 8 * j + 8], 4, 0) for j in range(4)]
     last = last_row((8, 512))
     return (
-        summed[0:8]
-        + roll(summed[8:16], 1)
-        + roll(jnp.where(last, 0.0, summed[16:24]), 32)
-        + roll(jnp.where(last, 0.0, summed[24:32]), 33)
+        summed[0]
+        + roll(summed[1], 1)
+        + roll(jnp.where(last, 0.0, summed[2] + roll(summed[3], 1)), 32)
     )
 
 
@@ -314,11 +323,11 @@
 
 
 def element_terms(matrix, coupling, v_here, v_next, lam, mu, press):
-    vals = jnp.concatenate(v_here + v_next, axis=0)
+    vals = jnp.concatenate([a + roll(b, 4, 0) for a, b in zip(v_here, v_next)], axis=0)
     high = vals.astype(bf16)
     low = (vals - high.astype(f32)).astype(bf16)
     both = jnp.dot(matrix, jnp.concatenate([high, low, high], axis=0), preferred_element_type=f32)
-    return coupling * (biot_coef * press) - (lam * both[0:64] + mu * both[64:128])
+    return coupling * (biot_coef * press) - (lam * both[0:32] + mu * both[32:64])
 
 
 def displacements(u, lam, mu, load, sup, safe, gain, means, stiff, aux, moved, least, most):
@@ -396,7 +405,8 @@
     def far(y, at):
         if at not in FAR:
             return jnp.zeros((8, 128), f32)
-        return halo[92 + 6 * y + FAR.index(at)] * ok[0]
+        at = 92 + 2 * y + at - 2 if at < 4 else 100 + 4 * y + at - 6
+        return halo[at] * ok[0]
 
     def beside(y, at):
         return jnp.zeros((8, 128), f32) if share is None else share[13 * y + at] * ok[1]
@@ -510,10 +520,10 @@
 
 def strain_rows(aux, nodes, blocks, strain):
     last_y = last_row((8, 512))
-    column = [jnp.broadcast_to(aux[8 * a : 8 * a + 8, 0:1], (8, 512)) for a in range(8)]
+    column = [jnp.broadcast_to(aux[8 * j : 8 * j + 8, 0:1], (8, 512)) for j in range(4)]
     for b in blocks:
-        here, following = nodes(b), nodes(b + 1)
-        parts = [column[a] * here + column[4 + a] * following for a in range(4)]
+        pair = nodes(b) + roll(nodes(b + 1), 4, 0)
+        parts = [column[j] * pair for j in range(4)]
         total = (
             parts[0]
             + roll(parts[1], 511)
@@ -641,16 +651,12 @@
 
 
 def corner_major(stiff):
-    grid = stiff.reshape(3, 8, 3, 8).transpose(1, 0, 3, 2)
-    return jnp.pad(grid, ((0, 0), (0, 5), (0, 0), (0, 5))).reshape(64, 64)
+    grid = stiff.reshape(3, 2, 4, 3, 2, 4).transpose(2, 1, 0, 5, 4, 3)
+    return jnp.pad(grid, ((0, 0), (0, 0), (0, 1), (0, 0), (0, 0), (0, 1))).reshape(32, 32)
 
 
 def corner_column(vec):
-    return jnp.pad(vec.reshape(3, 8).T, ((0, 0), (0, 5))).reshape(64)
-
-
-def pick_far(tiles):
-    return jnp.concatenate([tiles[:, 2:4], tiles[:, 6:10]], axis=1)
+    return jnp.pad(vec.reshape(3, 2, 4).transpose(2, 1, 0), ((0, 0), (0, 0), (0, 1))).reshape(32)
 
 
 def shape(*dims):
@@ -662,9 +668,9 @@
     load, support, lame_lambda, lame_mu, stiff_lambda, stiff_mu, coupling_vec,
 ):
     core = lax.axis_index("grp")
-    layer = lax.axis_index("gz")
     core_arg = jnp.full((1,), core, jnp.int32)
     row_arg = jnp.full((1,), lax.axis_index("gy"), jnp.int32)
+    layer = lax.axis_index("gz")
     layer_arg = jnp.full((1,), layer, jnp.int32)
     swap = [(0, 1), (1, 0)]
 
@@ -687,24 +693,34 @@
     packed = call(
         pack_kernel,
         shape(16, TILES, 8, 128),
-        [SM, SM] + [HB] * 5,
+        [SM, SM, SM] + [HB] * 5,
         [
             pltpu.VMEM((16, 8, 128), f32),
             pltpu.VMEM((16, 8, 128), f32),
             pltpu.VMEM((16, 512), f32),
             pltpu.VMEM((16, 512), f32),
             pltpu.VMEM((1, 8, 512), jnp.int32),
+            pltpu.VMEM((16, TILES, 8, 128), f32),
             pltpu.SemaphoreType.DMA((5,)),
+            pltpu.SemaphoreType.DMA((TILES,)),
         ],
         WHOLE,
-    )(core_arg, row_arg, cells, cells_other, nodes, nodes_other, block_route)
+        HB,
+    )(core_arg, row_arg, layer_arg, cells, cells_other, nodes, nodes_other, block_route)
     grid = lax.all_to_all(packed, ("gx", "gy"), 0, 0, tiled=True)
+    grid, core, layer, stiff_lambda, stiff_mu, coupling_vec = lax.optimization_barrier(
+        (grid, core, layer, stiff_lambda, stiff_mu, coupling_vec)
+    )
+    core_arg = jnp.full((1,), core, jnp.int32)
+    layer_arg = jnp.full((1,), layer, jnp.int32)
 
     ring = [(8 + z, (z + 1) % 8) for z in range(8)] + [(z, 8 + (z - 1) % 8) for z in range(8)]
+    first = core == 0
     sent = [
-        lax.dynamic_slice_in_dim(grid, 12 * core, 4, 0),
-        lax.dynamic_slice_in_dim(grid, 4 + 4 * core, 4, 0)[:, :10],
-        pick_far(lax.dynamic_slice_in_dim(grid, 8 - 4 * core, 4, 0)),
+        jnp.where(first, grid[0:4], grid[12:16]),
+        jnp.where(first, grid[4:8, :10], grid[8:12, :10]),
+        jnp.where(first, grid[8:12, 2:4], grid[4:8, 2:4]),
+        jnp.where(first, grid[8:12, 6:10], grid[4:8, 6:10]),
     ]
     sent = jnp.concatenate([part.reshape(-1, 8, 128) for part in sent], axis=0)
     halo = lax.ppermute(sent, ("grp", "gz"), ring)

time: 66.7 us -> 66.2 us (level)
  blocking collectives: 9.6 us -> 28.5 us
  waiting for transfers between devices: 18.6 us -> 5.73 us
  starting transfers between devices: 22.3 us -> 15.1 us
    all_to_all x0 -> x1, blocking collectives: none -> 18.8 us  [shards(): grid = lax.all_to_all(packed, ('gx', 'gy'), 0, 0, tiled=True)]
    all_to_all x1 -> x0, waiting for transfers between devices: 13.3 us -> none  [shards(): grid = lax.all_to_all(packed, ('gx', 'gy'), 0, 0, tiled=True)]
    all_to_all x1 -> x0, starting transfers between devices: 5.04 us -> none  [shards(): grid = lax.all_to_all(packed, ('gx', 'gy'), 0, 0, tiled=True)]
    ppermute x1, starting transfers between devices: 4.69 us -> 3.56 us  [shards(): halo = lax.ppermute(sent, ('grp', 'gz'), ring)]
    ppermute x1, starting transfers between devices: 1.23 us -> 2.31 us  [shards(): share = lax.ppermute(halo[:52], 'grp', swap)]
    ppermute x1, starting transfers between devices: 2.65 us -> 1.64 us  [shards(): across = lax.ppermute(near, 'grp', swap)]
    ppermute x1, waiting for transfers between devices: 0.01 us -> 1.02 us  [shards(): near = lax.ppermute(mid, ('grp', 'gz'), ring)]
    reshape x7 -> x9, local copies, waits for them, and re-layouts: 0.66 us -> 1.64 us  [the longest x4 1.03 us: corner_major(): grid = stiff.reshape(3, 2, 4, 3, 2, 4).transpose(2, 1, 0, 5, 4, 3)]
  transfers between devices with their start and end apart: 9 -> 8, of which waited for: 5 -> 5; matrix products, arithmetic and copies ran while one was open for 5% -> 6% of each run, Pallas kernels for 3% -> 3%
where the time goes in v2:
time: 66.2 us; the launch traced here: 65.8 us
  blocking collectives  28.5 us (43%)
  starting transfers between devices  15.1 us (23%)
  Pallas kernels  10.9 us (16%)
  waiting for transfers between devices  5.73 us (9%)
  local copies, waits for them, and re-layouts  4.6 us (7%)
  between operations  0.8 us (1%)
    all_to_all x1, blocking collectives, shards(): grid = lax.all_to_all(packed, ('gx', 'gy'), 0, 0, tiled=True)  18.8 us
    all_to_all x1, blocking collectives, shards(): back = lax.all_to_all(whole, ('gx', 'gy'), 0, 0, tiled=True)  9.71 us
    ppermute x1, starting transfers between devices, shards(): partner = lax.ppermute(mid, 'grp', swap)  3.66 us
    ppermute x1, starting transfers between devices, shards(): halo = lax.ppermute(sent, ('grp', 'gz'), ring)  3.56 us
    ppermute x1, starting transfers between devices, shards(): cells_other = lax.ppermute(cells, 'grp', swap)  3.33 us
    pallas_call x1, Pallas kernels, shards(): call(pack_kernel, shape(16, TILES, 8, 128), [SM, SM, SM] + [HB] * 5, [plt...  2.55 us
    ppermute x1, starting transfers between devices, shards(): share = lax.ppermute(halo[:52], 'grp', swap)  2.31 us
    pallas_call x1, Pallas kernels, shards(): call(first_kernel, (shape(4, 8, 8, 128), shape(3, EARLY, 32, 128), shape(...  2.14 us
  transfers between devices with their start and end apart: 8, of which 5 were waited for; matrix products, arithmetic and copies ran while one was open for 6% of the time, Pallas kernels for 3%

profile of v2, /device:TPU:1, one launch (start us, length us, event | category | flops | bytes accessed | tf_op | source)
XLA Modules:
  0.0 65.8 jit_solution(8160943927622897271)
XLA Ops:
  0.6 1.6 %shard_map.149 = (f32[16,8,128]{2,1,0:T(8,128)}, f32[16,512]{1,0:T(8,128)}) custom-call(f32[16]{0:T(128)} %perms.1, f32[4,8,128]{2,1,0:T(8,128)} %p0.1, f32[4,8,128]{2,1,0:T(8,128)} %src.1, f32[4,8,128]{2,1,0:T(8,128)} %sto.1, s32[4,8,128]{2,1,0:T(8,128)} %cls.1, f32[3,512]{1,0:T(4,128)} %disp.1, f32[3,512]{1,0:T(4,128)} %load.1, f32[3,512]{1,0:T(4,128)} %sup.1, ...), custom_call_target="tpu_custom_call" | custom-call | tf_op jit(solution)/shard_map/pallas_call | solution.py:677
  2.2 3.3 %collective-permute-start = (f32[16,8,128]{2,1,0:T(8,128)}, f32[16,8,128]{2,1,0:T(8,128)}, u32[]{:S(2)}, u32[]{:S(2)}) collective-permute-start(f32[16,8,128]{2,1,0:T(8,128)} %get-tuple-element.30.a), channel_id=1, source_target_pairs={{0,128},{128,0},{1,129},{129,1},{2,130},{130,2},{3,131},{131,3},{4... | collective-permute-start | bytes 196616 | tf_op jit(solution)/shard_map/ppermute | solution.py:691
  5.5 0.1 collective-permute-start.1
  5.6 1.4 %collective-permute-done.1.d = f32[16,512]{1,0:T(8,128)} collective-permute-done((f32[16,512]{1,0:T(8,128)}, f32[16,512]{1,0:T(8,128)}, u32[]{:S(2)}, u32[]{:S(2)}) %collective-permute-start.1) | collective-permute-done | bytes 32800 | tf_op jit(solution)/shard_map/ppermute | solution.py:692
  7.1 0.0 collective-permute-done.b
  7.1 2.5 %shard_map.150 = f32[16,13,8,128]{3,2,1,0:T(8,128)} custom-call(s32[1]{0:T(128)} %bitcast.core, s32[1]{0:T(128)} %bitcast.1.across, s32[1]{0:T(128)} %bitcast.2.layer, f32[16,8,128]{2,1,0:T(8,128)} %get-tuple-element.30.a, f32[16,8,128]{2,1,0:T(8,128)} %collective-permute-done.b, f32[16,512]{1,0:T(8,128)} %get-tuple-element.31.c, ...), custom_call_target="tpu_custom_call" | custom-call | tf_op jit(solution)/shard_map/pallas_call | solution.py:693
  9.6 18.8 %all_to_all.10.grid = f32[16,13,8,128]{3,2,1,0:T(8,128)S(1)} all-to-all(f32[16,13,8,128]{3,2,1,0:T(8,128)} %shard_map.150), channel_id=1, replica_groups=mesh['grp'=2,'gz'=8,'gx'=4,'gy'=4] {'gx','gy'}, dimensions={0} | all-to-all | bytes 1703936 | tf_op jit(solution)/shard_map/all_to_all | solution.py:710
  28.5 0.0 copy-start
  28.6 3.6 %collective-permute-start.2 = (f32[116,8,128]{2,1,0:T(8,128)S(1)}, f32[116,8,128]{2,1,0:T(8,128)S(1)}, u32[]{:S(2)}, u32[]{:S(2)}) collective-permute-start(f32[116,8,128]{2,1,0:T(8,128)S(1)} %pad_maximum_fusion), channel_id=1, source_target_pairs={{128,16},{144,32},{160,48},{176,64},{192,80},{208,96},{224,112},{2... | collective-permute-start | bytes 1425416 | tf_op jit(solution)/shard_map/ppermute | solution.py:726
  32.2 0.0 copy-done
  32.2 0.1 reshape.41
  32.3 0.0 copy-start.1
  32.3 0.8 %gather_fusion = f32[24]{0:T(128)S(1)} fusion(f32[24,24]{1,0:T(8,128)S(1)} %copy-done, s32[24]{0:T(128)S(1)} %or_bitcast_fusion), kind=kCustom, calls=%fused_computation | custom fusion | bytes 384 | tf_op jit(solution)/shard_map/jit(_diag)/jit(diagonal)/cond/branch_0_fun/gather | solution.py:730
  33.1 0.0 copy-done.1
  33.1 0.8 %gather_fusion.1 = f32[24]{0:T(128)S(1)} fusion(f32[24,24]{1,0:T(8,128)S(1)} %copy-done.1, s32[24]{0:T(128)S(1)} %or_bitcast_fusion), kind=kCustom, calls=%fused_computation.1 | custom fusion | bytes 384 | tf_op jit(solution)/shard_map/jit(_diag)/jit(diagonal)/cond/branch_0_fun/gather | solution.py:730
  33.9 0.1 reshape.43
  34.0 0.1 reshape.46
  34.1 0.1 copy.39
  34.2 0.1 stack_reshape.10
  34.3 0.1 reshape.47
  34.4 0.1 copy.40
  34.5 0.0 copy-start.2
  34.5 0.1 stack_reshape.11
  34.6 0.6 copy-done.2
  35.1 0.1 reshape.45
  35.2 0.1 copy.38
  35.3 0.1 stack_reshape.9
  35.4 0.1 copy.37
  35.5 0.4 copy.32
  36.0 0.2 reshape.42
  36.2 0.4 copy.33
  36.6 0.2 reshape.44
  36.8 2.0 %collective-permute-done.2.halo = f32[116,8,128]{2,1,0:T(8,128)S(1)} collective-permute-done((f32[116,8,128]{2,1,0:T(8,128)S(1)}, f32[116,8,128]{2,1,0:T(8,128)S(1)}, u32[]{:S(2)}, u32[]{:S(2)}) %collective-permute-start.2) | collective-permute-done | bytes 475168 | tf_op jit(solution)/shard_map/ppermute | solution.py:726
  38.8 2.3 %collective-permute-start.3 = (f32[52,8,128]{2,1,0:T(8,128)S(1)}, f32[52,8,128]{2,1,0:T(8,128)S(1)}, u32[]{:S(2)}, u32[]{:S(2)}) collective-permute-start(f32[52,8,128]{2,1,0:T(8,128)S(1)} %slice.40), channel_id=1, source_target_pairs={{0,128},{128,0},{1,129},{129,1},{2,130},{130,2},{3,131},{131,3},{4... | collective-permute-start | bytes 638984 | tf_op jit(solution)/shard_map/ppermute | solution.py:727
  41.1 1.5 %shard_map.151 = (f32[12,32,128]{2,1,0:T(8,128)S(1)}, f32[4,32,128]{2,1,0:T(8,128)S(1)}, f32[3,11,32,128]{3,2,1,0:T(8,128)S(1)}, f32[11,32,128]{2,1,0:T(8,128)S(...) custom-call(s32[1]{0:T(128)} %bitcast.3.core, ...), custom_call_target="tpu_custom_call" | custom-call | tf_op jit(solution)/shard_map/pallas_call | solution.py:734
  42.6 0.0 collective-permute-done.3.share
  42.6 2.1 %shard_map.152 = (f32[4,8,8,128]{3,2,1,0:T(8,128)S(1)}, f32[3,5,32,128]{3,2,1,0:T(8,128)S(1)}, f32[5,32,128]{2,1,0:T(8,128)S(1)}, f32[5,32,128]{2,1,0:T(8,128)S(1)}, f32[2,8,512]{2,1,0:T(8,128)S(1)}) custom-call(s32[1]{0:T(128)} %bitcast.3.core, s32[1]{0:T(128)} %bitcast.4.layer, f32[116,8,128]{2,1,0:T(8,128)S(1)} %collective-permute-done.2.halo, ...), custom_call_target="tpu_custom_call" | custom-call | tf_op jit(solution)/shard_map/pallas_call | solution.py:745
  44.7 0.1 collective-permute-start.4
  44.8 3.7 %collective-permute-start.6 = (f32[4,8,8,128]{3,2,1,0:T(8,128)S(1)}, f32[4,8,8,128]{3,2,1,0:T(8,128)S(1)}, u32[]{:S(2)}, u32[]{:S(2)}) collective-permute-start(f32[4,8,8,128]{3,2,1,0:T(8,128)S(1)} %get-tuple-element.50.own), channel_id=1, source_target_pairs={{0,128},{128,0},{1,129},{129,1},{2,130},{130,2},{3,131},{131,3},{4... | collective-permute-start | bytes 393224 | tf_op jit(solution)/shard_map/ppermute | solution.py:764
  48.5 1.0 %collective-permute-done.4.near = f32[4,8,8,128]{3,2,1,0:T(8,128)S(1)} collective-permute-done((f32[4,8,8,128]{3,2,1,0:T(8,128)S(1)}, f32[4,8,8,128]{3,2,1,0:T(8,128)S(1)}, u32[]{:S(2)}, u32[]{:S(2)}) %collective-permute-start.4) | collective-permute-done | bytes 131104 | tf_op jit(solution)/shard_map/ppermute | solution.py:763
  49.5 1.6 %collective-permute-start.5 = (f32[4,8,8,128]{3,2,1,0:T(8,128)S(1)}, f32[4,8,8,128]{3,2,1,0:T(8,128)S(1)}, u32[]{:S(2)}, u32[]{:S(2)}) collective-permute-start(f32[4,8,8,128]{3,2,1,0:T(8,128)S(1)} %collective-permute-done.4.near), channel_id=1, source_target_pairs={{0,128},{128,0},{1,129},{129,1},{2,130},{130,2},{3,131},{131,3},{4... | collective-permute-start | bytes 393224 | tf_op jit(solution)/shard_map/ppermute | solution.py:765
  51.2 0.0 collective-permute-done.6.partner
  51.2 0.6 shard_map.153
  51.7 0.4 collective-permute-done.5.across
  52.1 1.9 %shard_map.154 = f32[8,8,128]{2,1,0:T(8,128)S(1)} custom-call(s32[1]{0:T(128)} %bitcast.3.core, s32[1]{0:T(128)} %bitcast.4.layer, f32[4,8,8,128]{3,2,1,0:T(8,128)S(1)} %collective-permute-done.5.across, f32[64,32]{1,0:T(8,128)S(1)} %constant_dynamic-update-slice_fusion.stiff, f32[32,128]{1,0:T(8,128)S(1)} %pad.26.aux, ...), custom_call_target="tpu_custom_call" | custom-call | tf_op jit(solution)/shard_map/pallas_call | solution.py:772
  54.0 0.4 collective-permute-start.7
  54.5 0.9 %collective-permute-done.7 = f32[8,8,128]{2,1,0:T(8,128)S(1)} collective-permute-done((f32[8,8,128]{2,1,0:T(8,128)S(1)}, f32[8,8,128]{2,1,0:T(8,128)S(1)}, u32[]{:S(2)}, u32[]{:S(2)}) %collective-permute-start.7) | collective-permute-done | bytes 32800 | tf_op jit(solution)/shard_map/ppermute | solution.py:786
  55.3 9.7 %all_to_all.11.got = f32[16,8,128]{2,1,0:T(8,128)S(1)} all-to-all(f32[16,8,128]{2,1,0:T(8,128)S(1)} %pad_maximum_fusion.1), channel_id=1, replica_groups=mesh['grp'=2,'gz'=8,'gx'=4,'gy'=4] {'gx','gy'}, dimensions={0} | all-to-all | bytes 131072 | tf_op jit(solution)/shard_map/all_to_all | solution.py:788
  65.0 0.8 %shard_map.155 = (f32[4,8,128]{2,1,0:T(8,128)}, f32[3,512]{1,0:T(4,128)}) custom-call(s32[1]{0:T(128)} %bitcast.3.core, f32[16,8,128]{2,1,0:T(8,128)S(1)} %all_to_all.11.got), custom_call_target="tpu_custom_call" | custom-call | tf_op jit(solution)/shard_map/pallas_call | solution.py:789
  (18 shorter events, 0.3 us)
Async XLA Ops:
  2.2 4.9 %collective-permute-start = (f32[16,8,128]{2,1,0:T(8,128)}, f32[16,8,128]{2,1,0:T(8,128)}, u32[]{:S(2)}, u32[]{:S(2)}) collective-permute-start(f32[16,8,128]{2,1,0:T(8,128)} %get-tuple-element.30.a), channel_id=1, source_target_pairs={{0,128},{128,0},{1,129},{129,1},{2,130},{130,2},{3,131},{131,3},{4... | collective-permute-start | bytes 196616 | tf_op jit(solution)/shard_map/ppermute | solution.py:691
  5.5 1.6 %collective-permute-start.1 = (f32[16,512]{1,0:T(8,128)}, f32[16,512]{1,0:T(8,128)}, u32[]{:S(2)}, u32[]{:S(2)}) collective-permute-start(f32[16,512]{1,0:T(8,128)} %get-tuple-element.31.c), channel_id=1, source_target_pairs={{0,128},{128,0},{1,129},{129,1},{2,130},{130,2},{3,131},{131,3},{4... | collective-permute-start | bytes 98312 | tf_op jit(solution)/shard_map/ppermute | solution.py:692
  28.5 3.6 %copy-start = (f32[24,24]{1,0:T(8,128)S(1)}, f32[24,24]{1,0:T(8,128)}, u32[]{:S(2)}) copy-start(f32[24,24]{1,0:T(8,128)} %param.25) | copy-start | bytes 6916
  28.6 10.2 %collective-permute-start.2 = (f32[116,8,128]{2,1,0:T(8,128)S(1)}, f32[116,8,128]{2,1,0:T(8,128)S(1)}, u32[]{:S(2)}, u32[]{:S(2)}) collective-permute-start(f32[116,8,128]{2,1,0:T(8,128)S(1)} %pad_maximum_fusion), channel_id=1, source_target_pairs={{128,16},{144,32},{160,48},{176,64},{192,80},{208,96},{224,112},{2... | collective-permute-start | bytes 1425416 | tf_op jit(solution)/shard_map/ppermute | solution.py:726
  32.3 0.8 %copy-start.1 = (f32[24,24]{1,0:T(8,128)S(1)}, f32[24,24]{1,0:T(8,128)}, u32[]{:S(2)}) copy-start(f32[24,24]{1,0:T(8,128)} %param.26) | copy-start | bytes 6916
  34.5 0.7 %copy-start.2 = (f32[24]{0:T(128)S(1)}, f32[24]{0:T(128)}, u32[]{:S(2)}) copy-start(f32[24]{0:T(128)} %param.27) | copy-start | bytes 292
  38.8 3.8 %collective-permute-start.3 = (f32[52,8,128]{2,1,0:T(8,128)S(1)}, f32[52,8,128]{2,1,0:T(8,128)S(1)}, u32[]{:S(2)}, u32[]{:S(2)}) collective-permute-start(f32[52,8,128]{2,1,0:T(8,128)S(1)} %slice.40), channel_id=1, source_target_pairs={{0,128},{128,0},{1,129},{129,1},{2,130},{130,2},{3,131},{131,3},{4... | collective-permute-start | bytes 638984 | tf_op jit(solution)/shard_map/ppermute | solution.py:727
  44.7 4.8 %collective-permute-start.4 = (f32[4,8,8,128]{3,2,1,0:T(8,128)S(1)}, f32[4,8,8,128]{3,2,1,0:T(8,128)S(1)}, u32[]{:S(2)}, u32[]{:S(2)}) collective-permute-start(f32[4,8,8,128]{3,2,1,0:T(8,128)S(1)} %get-tuple-element.50.own), channel_id=1, source_target_pairs={{128,16},{144,32},{160,48},{176,64},{192,80},{208,96},{224,112},{2... | collective-permute-start | bytes 393224 | tf_op jit(solution)/shard_map/ppermute | solution.py:763
  44.8 6.3 %collective-permute-start.6 = (f32[4,8,8,128]{3,2,1,0:T(8,128)S(1)}, f32[4,8,8,128]{3,2,1,0:T(8,128)S(1)}, u32[]{:S(2)}, u32[]{:S(2)}) collective-permute-start(f32[4,8,8,128]{3,2,1,0:T(8,128)S(1)} %get-tuple-element.50.own), channel_id=1, source_target_pairs={{0,128},{128,0},{1,129},{129,1},{2,130},{130,2},{3,131},{131,3},{4... | collective-permute-start | bytes 393224 | tf_op jit(solution)/shard_map/ppermute | solution.py:764
  49.5 2.6 %collective-permute-start.5 = (f32[4,8,8,128]{3,2,1,0:T(8,128)S(1)}, f32[4,8,8,128]{3,2,1,0:T(8,128)S(1)}, u32[]{:S(2)}, u32[]{:S(2)}) collective-permute-start(f32[4,8,8,128]{3,2,1,0:T(8,128)S(1)} %collective-permute-done.4.near), channel_id=1, source_target_pairs={{0,128},{128,0},{1,129},{129,1},{2,130},{130,2},{3,131},{131,3},{4... | collective-permute-start | bytes 393224 | tf_op jit(solution)/shard_map/ppermute | solution.py:765
  54.0 1.3 %collective-permute-start.7 = (f32[8,8,128]{2,1,0:T(8,128)S(1)}, f32[8,8,128]{2,1,0:T(8,128)S(1)}, u32[]{:S(2)}, u32[]{:S(2)}) collective-permute-start(f32[8,8,128]{2,1,0:T(8,128)S(1)} %shard_map.154), channel_id=1, source_target_pairs={{0,128},{128,0},{1,129},{129,1},{2,130},{130,2},{3,131},{131,3},{4... | collective-permute-start | bytes 98312 | tf_op jit(solution)/shard_map/ppermute | solution.py:786

commit v3 on v2

--- a/solution.py
+++ b/solution.py
@@ -65,18 +65,22 @@
     return lax.dot_general(a, b, (((1,), (1,)), ((), ())), preferred_element_type=f32)
 
 
-def stage_kernel(perms, p0, src, sto, cls, disp, load, sup, lam, mu, cells, nodes, held, small, pair, classes, sems):
+def pack_kernel(
+    core, across, layer, perms, p0, src, sto, cls, disp, load, sup, lam, mu, blocks,
+    packed, cells, nodes, routes, held, small, pair, classes, out, sems, done,
+):
     copies = [
-        pltpu.make_async_copy(perms, classes, sems.at[9]),
-        pltpu.make_async_copy(p0, cells.at[0:4], sems.at[0]),
-        pltpu.make_async_copy(src, cells.at[4:8], sems.at[1]),
-        pltpu.make_async_copy(sto, cells.at[8:12], sems.at[2]),
-        pltpu.make_async_copy(cls, held, sems.at[3]),
-        pltpu.make_async_copy(disp, small.at[0], sems.at[4]),
-        pltpu.make_async_copy(load, small.at[1], sems.at[5]),
-        pltpu.make_async_copy(sup, small.at[2], sems.at[6]),
-        pltpu.make_async_copy(lam, pair.at[0], sems.at[7]),
-        pltpu.make_async_copy(mu, pair.at[1], sems.at[8]),
+        pltpu.make_async_copy(perms, classes, sems.at[0]),
+        pltpu.make_async_copy(cls, held, sems.at[1]),
+        pltpu.make_async_copy(p0, cells.at[0:4], sems.at[2]),
+        pltpu.make_async_copy(src, cells.at[4:8], sems.at[3]),
+        pltpu.make_async_copy(sto, cells.at[8:12], sems.at[4]),
+        pltpu.make_async_copy(disp, small.at[0], sems.at[5]),
+        pltpu.make_async_copy(load, small.at[1], sems.at[6]),
+        pltpu.make_async_copy(sup, small.at[2], sems.at[7]),
+        pltpu.make_async_copy(lam, pair.at[0], sems.at[8]),
+        pltpu.make_async_copy(mu, pair.at[1], sems.at[9]),
+        pltpu.make_async_copy(blocks, routes, sems.at[10]),
     ]
     for copy in copies:
         copy.start()
@@ -90,19 +94,8 @@
             perm = jnp.where(which == member, classes[member], perm)
         cells[12 + i] = perm
     nodes[0:3] = small[0]
-    nodes[3:4] = pair[0]
     nodes[4:7] = small[1]
-    nodes[7:8] = pair[1]
     nodes[8:11] = small[2]
-
-
-def pack_kernel(core, across, layer, a, b, c, d, e, packed, cells, cells_other, nodes, nodes_other, routes, out, sems, done):
-    pairs = [(a, cells), (b, cells_other), (c, nodes), (d, nodes_other), (e, routes)]
-    copies = [pltpu.make_async_copy(src, dst, sems.at[n]) for n, (src, dst) in enumerate(pairs)]
-    for copy in copies:
-        copy.start()
-    for copy in copies:
-        copy.wait()
     sent = []
 
     def send(at):
@@ -114,29 +107,24 @@
     low = lane < 64
     sub = rows((8, 128))
 
-    placed = jnp.zeros((192, 128), f32)
     device = lanes((1, 512)) // 64
-    for half in range(2):
-        mine = jnp.zeros((8, 128), jnp.int32)
-        for y in range(4):
-            at = 256 * half + y // 2 * 128
-            mine = jnp.where(across[0] == y, roll(routes[0, :, at : at + 128], 64 * (y % 2)), mine)
-        block = jnp.concatenate(
-            [jnp.where(low[0:1], mine[2 * m : 2 * m + 1], roll(mine[2 * m + 1 : 2 * m + 2], 64)) for m in range(4)],
-            axis=1,
-        )
-        row = block // 64 % 4 * 8 + block // 256 * 4 + device % 4
-        depth = device // 4 * 64 + block % 64
-        at_row = rows((32, 512)) == row
-        at_depth = jnp.where(rows((128, 512)) == depth, 1.0, 0.0).astype(bf16)
-        spread = []
-        for source in (3, 7):
-            own = nodes[source : source + 1, :]
-            other = nodes_other[source : source + 1, :]
-            value = jnp.where(first, own, other) if half == 0 else jnp.where(first, other, own)
-            for part in three_parts(value):
-                spread.append(jnp.where(at_row, part.astype(f32), 0.0))
-        placed = placed + nt_dot(jnp.concatenate(spread, axis=0).astype(bf16), at_depth)
+    mine = jnp.zeros((8, 128), jnp.int32)
+    for k in range(8):
+        at = k // 2 * 128
+        here = (core[0] == k // 4) & (across[0] == k % 4)
+        mine = jnp.where(here, roll(routes[0, :, at : at + 128], 64 * (k % 2)), mine)
+    block = jnp.concatenate(
+        [jnp.where(low[0:1], mine[2 * m : 2 * m + 1], roll(mine[2 * m + 1 : 2 * m + 2], 64)) for m in range(4)],
+        axis=1,
+    )
+    row = block // 64 % 4 * 8 + block // 256 * 4 + device % 4
+    depth = device // 4 * 64 + block % 64
+    at_row = rows((32, 512)) == row
+    at_depth = jnp.where(rows((128, 512)) == depth, 1.0, 0.0).astype(bf16)
+    spread = [
+        jnp.where(at_row, part.astype(f32), 0.0) for v in range(2) for part in three_parts(pair[v])
+    ]
+    placed = nt_dot(jnp.concatenate(spread, axis=0).astype(bf16), at_depth)
     grids = [placed[96 * v : 96 * v + 32] + placed[96 * v + 32 : 96 * v + 64] + placed[96 * v + 64 : 96 * v + 96] for v in range(2)]
 
     for pair in range(2):
@@ -144,8 +132,7 @@
             tiles = []
             for field in (2 * pair, 2 * pair + 1):
                 own = cells[4 * field + i]
-                other = cells_other[4 * field + i]
-                tiles.append((jnp.where(first, own, other), jnp.where(first, other, own)))
+                tiles.append((jnp.where(first, own, 0.0), jnp.where(first, 0.0, own)))
             for chip in range(CHIPS):
                 start = 16 * chip - 24
                 spot = lane % 64 + start
@@ -168,9 +155,8 @@
         for j in range(4):
             at = (i * 4 + j) // 2 * 128
             own = nodes[8 * r : 8 * r + 8, at : at + 128]
-            other = nodes_other[8 * r : 8 * r + 8, at : at + 128]
-            near = jnp.where(first, own, other)
-            deep = jnp.where(first, other, own)
+            near = jnp.where(first, own, 0.0)
+            deep = jnp.where(first, 0.0, own)
             if j % 2 == 0:
                 full.append(jnp.where(low, near, roll(deep, 64)))
             else:
@@ -674,39 +660,26 @@
     layer_arg = jnp.full((1,), layer, jnp.int32)
     swap = [(0, 1), (1, 0)]
 
-    cells, nodes = call(
-        stage_kernel,
-        (shape(16, 8, 128), shape(16, 512)),
-        [HB] * 10,
+    packed = call(
+        pack_kernel,
+        shape(16, TILES, 8, 128),
+        [SM, SM, SM] + [HB] * 11,
         [
+            pltpu.VMEM((16, 8, 128), f32),
+            pltpu.VMEM((16, 512), f32),
+            pltpu.VMEM((1, 8, 512), jnp.int32),
             pltpu.VMEM((4, 8, 128), jnp.int32),
             pltpu.VMEM((3, 3, 512), f32),
             pltpu.VMEM((2, 1, 512), f32),
             pltpu.SMEM((CLASSES,), f32),
-            pltpu.SemaphoreType.DMA((10,)),
-        ],
-        WHOLE,
-    )(class_perm, pressure_start, source, storage, perm_class, displacement_start, load, support,
-      lame_lambda, lame_mu)
-    cells_other = lax.ppermute(cells, "grp", swap)
-    nodes_other = lax.ppermute(nodes, "grp", swap)
-    packed = call(
-        pack_kernel,
-        shape(16, TILES, 8, 128),
-        [SM, SM, SM] + [HB] * 5,
-        [
-            pltpu.VMEM((16, 8, 128), f32),
-            pltpu.VMEM((16, 8, 128), f32),
-            pltpu.VMEM((16, 512), f32),
-            pltpu.VMEM((16, 512), f32),
-            pltpu.VMEM((1, 8, 512), jnp.int32),
             pltpu.VMEM((16, TILES, 8, 128), f32),
-            pltpu.SemaphoreType.DMA((5,)),
+            pltpu.SemaphoreType.DMA((11,)),
             pltpu.SemaphoreType.DMA((TILES,)),
         ],
         WHOLE,
         HB,
-    )(core_arg, row_arg, layer_arg, cells, cells_other, nodes, nodes_other, block_route)
+    )(core_arg, row_arg, layer_arg, class_perm, pressure_start, source, storage, perm_class,
+      displacement_start, load, support, lame_lambda, lame_mu, block_route)
     grid = lax.all_to_all(packed, ("gx", "gy"), 0, 0, tiled=True)
     grid, core, layer, stiff_lambda, stiff_mu, coupling_vec = lax.optimization_barrier(
         (grid, core, layer, stiff_lambda, stiff_mu, coupling_vec)
@@ -715,6 +688,7 @@
     layer_arg = jnp.full((1,), layer, jnp.int32)
 
     ring = [(8 + z, (z + 1) % 8) for z in range(8)] + [(z, 8 + (z - 1) % 8) for z in range(8)]
+    grid = grid + lax.ppermute(grid, "grp", swap)
     first = core == 0
     sent = [
         jnp.where(first, grid[0:4], grid[12:16]),

time: 66.2 us -> 65.6 us (level)
  starting transfers between devices: 15.1 us -> 12.2 us
  blocking collectives: 28.5 us -> 31.2 us
  Pallas kernels: 10.9 us -> 9.26 us
  waiting for transfers between devices: 5.73 us -> 6.96 us
    all_to_all x1, blocking collectives: 18.8 us -> 21.5 us  [shards(): grid = lax.all_to_all(packed, ('gx', 'gy'), 0, 0, tiled=True)]
    pallas_call x2 -> x1, Pallas kernels: 4.11 us -> 2.49 us  [shards(): call(pack_kernel, shape(16, TILES, 8, 128), [SM, SM, SM] + [HB] * 11, [pl...]
    ppermute x1, starting transfers between devices: 3.56 us -> 1.98 us  [shards(): halo = lax.ppermute(sent, ('grp', 'gz'), ring)]
    ppermute x2 -> x1, starting transfers between devices: 3.43 us -> 1.86 us  [shards(): grid = grid + lax.ppermute(grid, 'grp', swap)]
    ppermute x1, starting transfers between devices: 2.31 us -> 3.87 us  [shards(): share = lax.ppermute(halo[:52], 'grp', swap)]
    ppermute x1, starting transfers between devices: 3.66 us -> 2.98 us  [shards(): partner = lax.ppermute(mid, 'grp', swap)]
    ppermute x1, starting transfers between devices: 1.64 us -> 0.96 us  [shards(): across = lax.ppermute(near, 'grp', swap)]
    ppermute x1, waiting for transfers between devices: 1.02 us -> 1.69 us  [shards(): near = lax.ppermute(mid, ('grp', 'gz'), ring)]
  transfers between devices with their start and end apart: 8 -> 7, of which waited for: 5 -> 5; matrix products, arithmetic and copies ran while one was open for 6% -> 6% of each run, Pallas kernels for 3% -> 3%
where the time goes in v3:
time: 65.6 us; the launch traced here: 65.3 us
  blocking collectives  31.2 us (48%)
  starting transfers between devices  12.2 us (19%)
  Pallas kernels  9.26 us (14%)
  waiting for transfers between devices  6.96 us (11%)
  local copies, waits for them, and re-layouts  4.6 us (7%)
  between operations  0.8 us (1%)
    all_to_all x1, blocking collectives, shards(): grid = lax.all_to_all(packed, ('gx', 'gy'), 0, 0, tiled=True)  21.5 us
    all_to_all x1, blocking collectives, shards(): back = lax.all_to_all(whole, ('gx', 'gy'), 0, 0, tiled=True)  9.76 us
    ppermute x1, starting transfers between devices, shards(): share = lax.ppermute(halo[:52], 'grp', swap)  3.87 us
    ppermute x1, starting transfers between devices, shards(): partner = lax.ppermute(mid, 'grp', swap)  2.98 us
    pallas_call x1, Pallas kernels, shards(): call(pack_kernel, shape(16, TILES, 8, 128), [SM, SM, SM] + [HB] * 11, [pl...  2.49 us
    pallas_call x1, Pallas kernels, shards(): call(first_kernel, (shape(4, 8, 8, 128), shape(3, EARLY, 32, 128), shape(...  2.14 us
    ppermute x1, waiting for transfers between devices, shards(): grid = grid + lax.ppermute(grid, 'grp', swap)  2.01 us
    ppermute x1, starting transfers between devices, shards(): halo = lax.ppermute(sent, ('grp', 'gz'), ring)  1.98 us
  transfers between devices with their start and end apart: 7, of which 5 were waited for; matrix products, arithmetic and copies ran while one was open for 6% of the time, Pallas kernels for 3%

profile of v3, /device:TPU:1, one launch (start us, length us, event | category | flops | bytes accessed | tf_op | source)
XLA Modules:
  0.0 65.3 jit_solution(14190465228095780209)
XLA Ops:
  0.6 2.5 %shard_map.149 = f32[16,13,8,128]{3,2,1,0:T(8,128)} custom-call(s32[1]{0:T(128)} %bitcast.core, s32[1]{0:T(128)} %bitcast.1.across, s32[1]{0:T(128)} %bitcast.2.layer, f32[16]{0:T(128)} %perms.1, f32[4,8,128]{2,1,0:T(8,128)} %p0.1, f32[4,8,128]{2,1,0:T(8,128)} %src.1, f32[4,8,128]{2,1,0:T(8,128)} %sto.1, s32[4,8,128]{2,1,0:T(8,128)} %cls.1, f32[3,512]{1,0:T(4,128)} %disp.1, ...), custom_call_target="tpu_custom_call" | custom-call | tf_op jit(solution)/shard_map/pallas_call | solution.py:663
  3.1 21.5 %all_to_all.10 = f32[16,13,8,128]{3,2,1,0:T(8,128)S(1)} all-to-all(f32[16,13,8,128]{3,2,1,0:T(8,128)} %shard_map.149), channel_id=1, replica_groups=mesh['grp'=2,'gz'=8,'gx'=4,'gy'=4] {'gx','gy'}, dimensions={0} | all-to-all | bytes 1703936 | tf_op jit(solution)/shard_map/all_to_all | solution.py:683
  24.6 1.9 %collective-permute-start = (f32[16,13,8,128]{3,2,1,0:T(8,128)S(1)}, f32[16,13,8,128]{3,2,1,0:T(8,128)S(1)}, u32[]{:S(2)}, u32[]{:S(2)}) collective-permute-start(f32[16,13,8,128]{3,2,1,0:T(8,128)S(1)} %all_to_all.10), channel_id=1, source_target_pairs={{0,128},{128,0},{1,129},{129,1},{2,130},{130,2},{3,131},{131,3},{4... | collective-permute-start | bytes 2555912 | tf_op jit(solution)/shard_map/ppermute | solution.py:691
  26.5 2.0 %collective-permute-done = f32[16,13,8,128]{3,2,1,0:T(8,128)S(1)} collective-permute-done((f32[16,13,8,128]{3,2,1,0:T(8,128)S(1)}, f32[16,13,8,128]{3,2,1,0:T(8,128)S(1)}, u32[]{:S(2)}, u32[]{:S(2)}) %collective-permute-start) | collective-permute-done | bytes 852000 | tf_op jit(solution)/shard_map/ppermute | solution.py:691
  28.5 0.1 add.23.grid
  28.7 0.0 copy-start
  28.7 2.0 %collective-permute-start.1 = (f32[116,8,128]{2,1,0:T(8,128)S(1)}, f32[116,8,128]{2,1,0:T(8,128)S(1)}, u32[]{:S(2)}, u32[]{:S(2)}) collective-permute-start(f32[116,8,128]{2,1,0:T(8,128)S(1)} %pad_maximum_fusion), channel_id=1, source_target_pairs={{128,16},{144,32},{160,48},{176,64},{192,80},{208,96},{224,112},{2... | collective-permute-start | bytes 1425416 | tf_op jit(solution)/shard_map/ppermute | solution.py:700
  30.7 0.0 copy-done
  30.7 0.1 reshape.41
  30.8 0.0 copy-start.1
  30.8 0.8 %gather_fusion = f32[24]{0:T(128)S(1)} fusion(f32[24,24]{1,0:T(8,128)S(1)} %copy-done, s32[24]{0:T(128)S(1)} %or_bitcast_fusion), kind=kCustom, calls=%fused_computation | custom fusion | bytes 384 | tf_op jit(solution)/shard_map/jit(_diag)/jit(diagonal)/cond/branch_0_fun/gather | solution.py:704
  31.6 0.0 copy-done.1
  31.6 0.8 %gather_fusion.1 = f32[24]{0:T(128)S(1)} fusion(f32[24,24]{1,0:T(8,128)S(1)} %copy-done.1, s32[24]{0:T(128)S(1)} %or_bitcast_fusion), kind=kCustom, calls=%fused_computation.1 | custom fusion | bytes 384 | tf_op jit(solution)/shard_map/jit(_diag)/jit(diagonal)/cond/branch_0_fun/gather | solution.py:704
  32.4 0.1 reshape.43
  32.5 0.1 reshape.46
  32.6 0.1 copy.39
  32.7 0.1 stack_reshape.10
  32.8 0.1 reshape.47
  32.9 0.1 copy.40
  33.0 0.0 copy-start.2
  33.0 0.1 stack_reshape.11
  33.1 0.6 copy-done.2
  33.7 0.1 reshape.45
  33.8 0.1 copy.38
  33.9 0.1 stack_reshape.9
  34.0 0.1 copy.37
  34.1 0.4 copy.32
  34.5 0.2 reshape.42
  34.7 0.4 copy.33
  35.2 0.2 reshape.44
  35.4 2.0 %collective-permute-done.1.halo = f32[116,8,128]{2,1,0:T(8,128)S(1)} collective-permute-done((f32[116,8,128]{2,1,0:T(8,128)S(1)}, f32[116,8,128]{2,1,0:T(8,128)S(1)}, u32[]{:S(2)}, u32[]{:S(2)}) %collective-permute-start.1) | collective-permute-done | bytes 475168 | tf_op jit(solution)/shard_map/ppermute | solution.py:700
  37.4 3.9 %collective-permute-start.2 = (f32[52,8,128]{2,1,0:T(8,128)S(1)}, f32[52,8,128]{2,1,0:T(8,128)S(1)}, u32[]{:S(2)}, u32[]{:S(2)}) collective-permute-start(f32[52,8,128]{2,1,0:T(8,128)S(1)} %slice.48), channel_id=1, source_target_pairs={{0,128},{128,0},{1,129},{129,1},{2,130},{130,2},{3,131},{131,3},{4... | collective-permute-start | bytes 638984 | tf_op jit(solution)/shard_map/ppermute | solution.py:701
  41.2 1.5 %shard_map.150 = (f32[12,32,128]{2,1,0:T(8,128)S(1)}, f32[4,32,128]{2,1,0:T(8,128)S(1)}, f32[3,11,32,128]{3,2,1,0:T(8,128)S(1)}, f32[11,32,128]{2,1,0:T(8,128)S(...) custom-call(s32[1]{0:T(128)} %bitcast.3.core, ...), custom_call_target="tpu_custom_call" | custom-call | tf_op jit(solution)/shard_map/pallas_call | solution.py:708
  42.7 0.0 collective-permute-done.2.share
  42.7 2.1 %shard_map.151 = (f32[4,8,8,128]{3,2,1,0:T(8,128)S(1)}, f32[3,5,32,128]{3,2,1,0:T(8,128)S(1)}, f32[5,32,128]{2,1,0:T(8,128)S(1)}, f32[5,32,128]{2,1,0:T(8,128)S(1)}, f32[2,8,512]{2,1,0:T(8,128)S(1)}) custom-call(s32[1]{0:T(128)} %bitcast.3.core, s32[1]{0:T(128)} %bitcast.4.layer, f32[116,8,128]{2,1,0:T(8,128)S(1)} %collective-permute-done.1.halo, ...), custom_call_target="tpu_custom_call" | custom-call | tf_op jit(solution)/shard_map/pallas_call | solution.py:719
  44.8 0.1 collective-permute-start.3
  44.9 3.0 %collective-permute-start.5 = (f32[4,8,8,128]{3,2,1,0:T(8,128)S(1)}, f32[4,8,8,128]{3,2,1,0:T(8,128)S(1)}, u32[]{:S(2)}, u32[]{:S(2)}) collective-permute-start(f32[4,8,8,128]{3,2,1,0:T(8,128)S(1)} %get-tuple-element.46.own), channel_id=1, source_target_pairs={{0,128},{128,0},{1,129},{129,1},{2,130},{130,2},{3,131},{131,3},{4... | collective-permute-start | bytes 393224 | tf_op jit(solution)/shard_map/ppermute | solution.py:738
  47.9 1.7 %collective-permute-done.3.near = f32[4,8,8,128]{3,2,1,0:T(8,128)S(1)} collective-permute-done((f32[4,8,8,128]{3,2,1,0:T(8,128)S(1)}, f32[4,8,8,128]{3,2,1,0:T(8,128)S(1)}, u32[]{:S(2)}, u32[]{:S(2)}) %collective-permute-start.3) | collective-permute-done | bytes 131104 | tf_op jit(solution)/shard_map/ppermute | solution.py:737
  49.6 1.0 %collective-permute-start.4 = (f32[4,8,8,128]{3,2,1,0:T(8,128)S(1)}, f32[4,8,8,128]{3,2,1,0:T(8,128)S(1)}, u32[]{:S(2)}, u32[]{:S(2)}) collective-permute-start(f32[4,8,8,128]{3,2,1,0:T(8,128)S(1)} %collective-permute-done.3.near), channel_id=1, source_target_pairs={{0,128},{128,0},{1,129},{129,1},{2,130},{130,2},{3,131},{131,3},{4... | collective-permute-start | bytes 393224 | tf_op jit(solution)/shard_map/ppermute | solution.py:739
  50.6 0.0 collective-permute-done.5.partner
  50.6 0.6 shard_map.152
  51.2 0.4 collective-permute-done.4.across
  51.6 1.9 %shard_map.153 = f32[8,8,128]{2,1,0:T(8,128)S(1)} custom-call(s32[1]{0:T(128)} %bitcast.3.core, s32[1]{0:T(128)} %bitcast.4.layer, f32[4,8,8,128]{3,2,1,0:T(8,128)S(1)} %collective-permute-done.4.across, f32[64,32]{1,0:T(8,128)S(1)} %constant_dynamic-update-slice_fusion.stiff, f32[32,128]{1,0:T(8,128)S(1)} %pad.26.aux, ...), custom_call_target="tpu_custom_call" | custom-call | tf_op jit(solution)/shard_map/pallas_call | solution.py:746
  53.4 0.4 collective-permute-start.6
  53.9 0.9 %collective-permute-done.6 = f32[8,8,128]{2,1,0:T(8,128)S(1)} collective-permute-done((f32[8,8,128]{2,1,0:T(8,128)S(1)}, f32[8,8,128]{2,1,0:T(8,128)S(1)}, u32[]{:S(2)}, u32[]{:S(2)}) %collective-permute-start.6) | collective-permute-done | bytes 32800 | tf_op jit(solution)/shard_map/ppermute | solution.py:760
  54.8 9.8 %all_to_all.11.got = f32[16,8,128]{2,1,0:T(8,128)S(1)} all-to-all(f32[16,8,128]{2,1,0:T(8,128)S(1)} %pad_maximum_fusion.1), channel_id=1, replica_groups=mesh['grp'=2,'gz'=8,'gx'=4,'gy'=4] {'gx','gy'}, dimensions={0} | all-to-all | bytes 131072 | tf_op jit(solution)/shard_map/all_to_all | solution.py:762
  64.5 0.8 %shard_map.154 = (f32[4,8,128]{2,1,0:T(8,128)}, f32[3,512]{1,0:T(4,128)}) custom-call(s32[1]{0:T(128)} %bitcast.3.core, f32[16,8,128]{2,1,0:T(8,128)S(1)} %all_to_all.11.got), custom_call_target="tpu_custom_call" | custom-call | tf_op jit(solution)/shard_map/pallas_call | solution.py:763
  (18 shorter events, 0.3 us)
Async XLA Ops:
  24.6 3.9 %collective-permute-start = (f32[16,13,8,128]{3,2,1,0:T(8,128)S(1)}, f32[16,13,8,128]{3,2,1,0:T(8,128)S(1)}, u32[]{:S(2)}, u32[]{:S(2)}) collective-permute-start(f32[16,13,8,128]{3,2,1,0:T(8,128)S(1)} %all_to_all.10), channel_id=1, source_target_pairs={{0,128},{128,0},{1,129},{129,1},{2,130},{130,2},{3,131},{131,3},{4... | collective-permute-start | bytes 2555912 | tf_op jit(solution)/shard_map/ppermute | solution.py:691
  28.7 2.0 %copy-start = (f32[24,24]{1,0:T(8,128)S(1)}, f32[24,24]{1,0:T(8,128)}, u32[]{:S(2)}) copy-start(f32[24,24]{1,0:T(8,128)} %param.25) | copy-start | bytes 6916
  28.7 8.6 %collective-permute-start.1 = (f32[116,8,128]{2,1,0:T(8,128)S(1)}, f32[116,8,128]{2,1,0:T(8,128)S(1)}, u32[]{:S(2)}, u32[]{:S(2)}) collective-permute-start(f32[116,8,128]{2,1,0:T(8,128)S(1)} %pad_maximum_fusion), channel_id=1, source_target_pairs={{128,16},{144,32},{160,48},{176,64},{192,80},{208,96},{224,112},{2... | collective-permute-start | bytes 1425416 | tf_op jit(solution)/shard_map/ppermute | solution.py:700
  30.8 0.8 %copy-start.1 = (f32[24,24]{1,0:T(8,128)S(1)}, f32[24,24]{1,0:T(8,128)}, u32[]{:S(2)}) copy-start(f32[24,24]{1,0:T(8,128)} %param.26) | copy-start | bytes 6916
  33.0 0.7 %copy-start.2 = (f32[24]{0:T(128)S(1)}, f32[24]{0:T(128)}, u32[]{:S(2)}) copy-start(f32[24]{0:T(128)} %param.27) | copy-start | bytes 292
  37.4 5.3 %collective-permute-start.2 = (f32[52,8,128]{2,1,0:T(8,128)S(1)}, f32[52,8,128]{2,1,0:T(8,128)S(1)}, u32[]{:S(2)}, u32[]{:S(2)}) collective-permute-start(f32[52,8,128]{2,1,0:T(8,128)S(1)} %slice.48), channel_id=1, source_target_pairs={{0,128},{128,0},{1,129},{129,1},{2,130},{130,2},{3,131},{131,3},{4... | collective-permute-start | bytes 638984 | tf_op jit(solution)/shard_map/ppermute | solution.py:701
  44.8 4.8 %collective-permute-start.3 = (f32[4,8,8,128]{3,2,1,0:T(8,128)S(1)}, f32[4,8,8,128]{3,2,1,0:T(8,128)S(1)}, u32[]{:S(2)}, u32[]{:S(2)}) collective-permute-start(f32[4,8,8,128]{3,2,1,0:T(8,128)S(1)} %get-tuple-element.46.own), channel_id=1, source_target_pairs={{128,16},{144,32},{160,48},{176,64},{192,80},{208,96},{224,112},{2... | collective-permute-start | bytes 393224 | tf_op jit(solution)/shard_map/ppermute | solution.py:737
  44.9 5.6 %collective-permute-start.5 = (f32[4,8,8,128]{3,2,1,0:T(8,128)S(1)}, f32[4,8,8,128]{3,2,1,0:T(8,128)S(1)}, u32[]{:S(2)}, u32[]{:S(2)}) collective-permute-start(f32[4,8,8,128]{3,2,1,0:T(8,128)S(1)} %get-tuple-element.46.own), channel_id=1, source_target_pairs={{0,128},{128,0},{1,129},{129,1},{2,130},{130,2},{3,131},{131,3},{4... | collective-permute-start | bytes 393224 | tf_op jit(solution)/shard_map/ppermute | solution.py:738
  49.6 1.9 %collective-permute-start.4 = (f32[4,8,8,128]{3,2,1,0:T(8,128)S(1)}, f32[4,8,8,128]{3,2,1,0:T(8,128)S(1)}, u32[]{:S(2)}, u32[]{:S(2)}) collective-permute-start(f32[4,8,8,128]{3,2,1,0:T(8,128)S(1)} %collective-permute-done.3.near), channel_id=1, source_target_pairs={{0,128},{128,0},{1,129},{129,1},{2,130},{130,2},{3,131},{131,3},{4... | collective-permute-start | bytes 393224 | tf_op jit(solution)/shard_map/ppermute | solution.py:739
  53.4 1.3 %collective-permute-start.6 = (f32[8,8,128]{2,1,0:T(8,128)S(1)}, f32[8,8,128]{2,1,0:T(8,128)S(1)}, u32[]{:S(2)}, u32[]{:S(2)}) collective-permute-start(f32[8,8,128]{2,1,0:T(8,128)S(1)} %shard_map.153), channel_id=1, source_target_pairs={{0,128},{128,0},{1,129},{129,1},{2,130},{130,2},{3,131},{131,3},{4... | collective-permute-start | bytes 98312 | tf_op jit(solution)/shard_map/ppermute | solution.py:760

commit v4 on v3

--- a/solution.py
+++ b/solution.py
@@ -14,7 +14,7 @@
 NODES = 16
 TILES = 13
 EARLY = 5
-FAR = (2, 3, 6, 7, 8, 9)
+FAR = (2, 3, 6, 7, 8)
 
 stabilize = 0.5
 biot_coef = 0.8
@@ -84,7 +84,7 @@
     ]
     for copy in copies:
         copy.start()
-    nodes[...] = jnp.zeros((16, 512), f32)
+    nodes[...] = jnp.zeros((24, 512), f32)
     for copy in copies:
         copy.wait()
     for i in range(4):
@@ -94,8 +94,8 @@
             perm = jnp.where(which == member, classes[member], perm)
         cells[12 + i] = perm
     nodes[0:3] = small[0]
-    nodes[4:7] = small[1]
-    nodes[8:11] = small[2]
+    nodes[8:11] = small[1]
+    nodes[16:19] = small[2]
     sent = []
 
     def send(at):
@@ -163,8 +163,10 @@
                 full.append(jnp.where(low, roll(near, 64), deep))
         return full
 
-    supports = [jnp.where(sub < 4, a, pltpu.roll(b, 4, 0)) for a, b in zip(full_depth(0, 1), full_depth(1, 1))]
-    members = [full_depth(0, 0), full_depth(1, 0), supports]
+    members = [
+        [jnp.where(sub < 4, a, pltpu.roll(b, 4, 0)) for a, b in zip(full_depth(0, r), full_depth(1, r))]
+        for r in range(3)
+    ]
     members += [[grid[8 * j : 8 * j + 8] for j in range(4)] for grid in grids]
     for at, full in enumerate(members):
         for chip in range(CHIPS):
@@ -382,20 +384,24 @@
     def plane(x):
         return lambda y, at: grid[4 * x + y, at]
 
+    none = jnp.zeros((8, 128), f32)
+
     def near(y, at):
-        return halo[13 * y + at] * ok[0]
+        if at < 11:
+            return halo[11 * y + at] * ok[0]
+        return halo[33 + at] * ok[0] if y == 0 else none
 
     def middle(y, at):
-        return halo[52 + 10 * y + at] * ok[0] if at < 10 else jnp.zeros((8, 128), f32)
+        return halo[46 + 9 * y + at] * ok[0] if at < 9 else none
 
     def far(y, at):
         if at not in FAR:
-            return jnp.zeros((8, 128), f32)
-        at = 92 + 2 * y + at - 2 if at < 4 else 100 + 4 * y + at - 6
+            return none
+        at = 82 + 2 * y + at - 2 if at < 4 else 90 + 3 * y + at - 6
         return halo[at] * ok[0]
 
     def beside(y, at):
-        return jnp.zeros((8, 128), f32) if share is None else share[13 * y + at] * ok[1]
+        return none if share is None else share[11 * y + at] * ok[1]
 
     inside = [plane(x) for x in range(4)]
     return [[far, middle, near] + inside + [beside], [beside] + inside + [near, middle, far]]
@@ -433,16 +439,12 @@
         for unit in range(8):
             for y in range(4):
                 at = slice(128 * y, 128 * y + 128)
-                for i in range(2):
-                    n = 2 * unit + i
-                    tile_a = units[unit](y, 8 + i)
-                    u[n, :, at] = jnp.where(sub < 3, tile_a, 0.0)
-                    if 4 <= n <= 11:
-                        load[n, :, at] = jnp.where(sub < 3, pltpu.roll(tile_a, 4, 0), 0.0)
-                        tile_b = units[unit](y, 10)
-                        if i == 1:
-                            tile_b = pltpu.roll(tile_b, 4, 0)
-                        sup[n, :, at] = jnp.where(sub < 3, tile_b, 0.0)
+                for member, target in ((8, u), (9, load), (10, sup)):
+                    if member > 8 and not 2 <= unit <= 5:
+                        continue
+                    tile = units[unit](y, member)
+                    target[2 * unit, :, at] = jnp.where(sub < 3, tile, 0.0)
+                    target[2 * unit + 1, :, at] = jnp.where(sub < 3, pltpu.roll(tile, 4, 0), 0.0)
             if 1 <= unit <= 5:
                 for at, param in ((11, lam), (12, mu)):
                     total = units[unit](0, at) + units[unit](1, at) + units[unit](2, at) + units[unit](3, at)
@@ -480,9 +482,9 @@
 
     window(core, units_of(None, halo, share, ok), unpack)
     for y in range(4):
-        for i in range(2):
-            tile = share[13 * y + 8 + i] * ok[1]
-            beside[i, :, 128 * y : 128 * y + 128] = jnp.where(sub < 3, tile, 0.0)
+        tile = share[11 * y + 8] * ok[1]
+        beside[0, :, 128 * y : 128 * y + 128] = jnp.where(sub < 3, tile, 0.0)
+        beside[1, :, 128 * y : 128 * y + 128] = jnp.where(sub < 3, pltpu.roll(tile, 4, 0), 0.0)
     for x in range(4, PLANES):
         press[0, x] = start[x - 4]
     cell_coefs(
@@ -666,7 +668,7 @@
         [SM, SM, SM] + [HB] * 11,
         [
             pltpu.VMEM((16, 8, 128), f32),
-            pltpu.VMEM((16, 512), f32),
+            pltpu.VMEM((24, 512), f32),
             pltpu.VMEM((1, 8, 512), jnp.int32),
             pltpu.VMEM((4, 8, 128), jnp.int32),
             pltpu.VMEM((3, 3, 512), f32),
@@ -691,14 +693,15 @@
     grid = grid + lax.ppermute(grid, "grp", swap)
     first = core == 0
     sent = [
-        jnp.where(first, grid[0:4], grid[12:16]),
-        jnp.where(first, grid[4:8, :10], grid[8:12, :10]),
+        jnp.where(first, grid[0:4, :11], grid[12:16, :11]),
+        jnp.sum(jnp.where(first, grid[0:4, 11:], grid[12:16, 11:]), axis=0),
+        jnp.where(first, grid[4:8, :9], grid[8:12, :9]),
         jnp.where(first, grid[8:12, 2:4], grid[4:8, 2:4]),
-        jnp.where(first, grid[8:12, 6:10], grid[4:8, 6:10]),
+        jnp.where(first, grid[8:12, 6:9], grid[4:8, 6:9]),
     ]
     sent = jnp.concatenate([part.reshape(-1, 8, 128) for part in sent], axis=0)
     halo = lax.ppermute(sent, ("grp", "gz"), ring)
-    share = lax.ppermute(halo[:52], "grp", swap)
+    share = lax.ppermute(halo[:44], "grp", swap)
 
     stiff = jnp.concatenate([corner_major(stiff_lambda), corner_major(stiff_mu)], axis=0)
     columns = [corner_column(coupling_vec), corner_column(jnp.diag(stiff_lambda)), corner_column(jnp.diag(stiff_mu))]

time: 65.6 us -> 65 us (level)
  no operation moved by 1% of the time
where the time goes in v4:
time: 65 us; the launch traced here: 64.7 us
  blocking collectives  31.2 us (48%)
  starting transfers between devices  12.2 us (19%)
  Pallas kernels  9.24 us (14%)
  waiting for transfers between devices  6.34 us (10%)
  local copies, waits for them, and re-layouts  4.64 us (7%)
  between operations  0.84 us (1%)
    all_to_all x1, blocking collectives, shards(): grid = lax.all_to_all(packed, ('gx', 'gy'), 0, 0, tiled=True)  21.5 us
    all_to_all x1, blocking collectives, shards(): back = lax.all_to_all(whole, ('gx', 'gy'), 0, 0, tiled=True)  9.76 us
    ppermute x1, starting transfers between devices, shards(): share = lax.ppermute(halo[:44], 'grp', swap)  3.87 us
    ppermute x1, starting transfers between devices, shards(): partner = lax.ppermute(mid, 'grp', swap)  2.98 us
    pallas_call x1, Pallas kernels, shards(): call(pack_kernel, shape(16, TILES, 8, 128), [SM, SM, SM] + [HB] * 11, [pl...  2.48 us
    pallas_call x1, Pallas kernels, shards(): call(first_kernel, (shape(4, 8, 8, 128), shape(3, EARLY, 32, 128), shape(...  2.14 us
    ppermute x1, waiting for transfers between devices, shards(): grid = grid + lax.ppermute(grid, 'grp', swap)  2.01 us
    ppermute x1, starting transfers between devices, shards(): halo = lax.ppermute(sent, ('grp', 'gz'), ring)  1.98 us
  transfers between devices with their start and end apart: 7, of which 5 were waited for; matrix products, arithmetic and copies ran while one was open for 6% of the time, Pallas kernels for 3%

profile of v4, /device:TPU:1, one launch (start us, length us, event | category | flops | bytes accessed | tf_op | source)
XLA Modules:
  0.0 64.7 jit_solution(17257863170020484660)
XLA Ops:
  0.6 2.5 %shard_map.149 = f32[16,13,8,128]{3,2,1,0:T(8,128)} custom-call(s32[1]{0:T(128)} %bitcast.core, s32[1]{0:T(128)} %bitcast.1.across, s32[1]{0:T(128)} %bitcast.2.layer, f32[16]{0:T(128)} %perms.1, f32[4,8,128]{2,1,0:T(8,128)} %p0.1, f32[4,8,128]{2,1,0:T(8,128)} %src.1, f32[4,8,128]{2,1,0:T(8,128)} %sto.1, s32[4,8,128]{2,1,0:T(8,128)} %cls.1, f32[3,512]{1,0:T(4,128)} %disp.1, ...), custom_call_target="tpu_custom_call" | custom-call | tf_op jit(solution)/shard_map/pallas_call | solution.py:665
  3.1 21.5 %all_to_all.10 = f32[16,13,8,128]{3,2,1,0:T(8,128)S(1)} all-to-all(f32[16,13,8,128]{3,2,1,0:T(8,128)} %shard_map.149), channel_id=1, replica_groups=mesh['grp'=2,'gz'=8,'gx'=4,'gy'=4] {'gx','gy'}, dimensions={0} | all-to-all | bytes 1703936 | tf_op jit(solution)/shard_map/all_to_all | solution.py:685
  24.6 1.9 %collective-permute-start = (f32[16,13,8,128]{3,2,1,0:T(8,128)S(1)}, f32[16,13,8,128]{3,2,1,0:T(8,128)S(1)}, u32[]{:S(2)}, u32[]{:S(2)}) collective-permute-start(f32[16,13,8,128]{3,2,1,0:T(8,128)S(1)} %all_to_all.10), channel_id=1, source_target_pairs={{0,128},{128,0},{1,129},{129,1},{2,130},{130,2},{3,131},{131,3},{4... | collective-permute-start | bytes 2555912 | tf_op jit(solution)/shard_map/ppermute | solution.py:693
  26.5 2.0 %collective-permute-done = f32[16,13,8,128]{3,2,1,0:T(8,128)S(1)} collective-permute-done((f32[16,13,8,128]{3,2,1,0:T(8,128)S(1)}, f32[16,13,8,128]{3,2,1,0:T(8,128)S(1)}, u32[]{:S(2)}, u32[]{:S(2)}) %collective-permute-start) | collective-permute-done | bytes 852000 | tf_op jit(solution)/shard_map/ppermute | solution.py:693
  28.5 0.1 add.23.grid
  28.7 0.0 copy-start
  28.7 2.0 %collective-permute-start.1 = (f32[102,8,128]{2,1,0:T(8,128)S(1)}, f32[102,8,128]{2,1,0:T(8,128)S(1)}, u32[]{:S(2)}, u32[]{:S(2)}) collective-permute-start(f32[102,8,128]{2,1,0:T(8,128)S(1)} %constant_dynamic-update-slice_fusion), channel_id=1, source_target_pairs={{128,16},{144,32},{160,48},{176,64},{192,80},{208,96},{224,112},{2... | collective-permute-start | bytes 1253384 | tf_op jit(solution)/shard_map/ppermute | solution.py:703
  30.7 0.0 copy-done
  30.7 0.1 reshape.41
  30.9 0.0 copy-start.1
  30.9 0.8 %gather_fusion = f32[24]{0:T(128)S(1)} fusion(f32[24,24]{1,0:T(8,128)S(1)} %copy-done, s32[24]{0:T(128)S(1)} %or_bitcast_fusion), kind=kCustom, calls=%fused_computation | custom fusion | bytes 384 | tf_op jit(solution)/shard_map/jit(_diag)/jit(diagonal)/cond/branch_0_fun/gather | solution.py:707
  31.7 0.0 copy-done.1
  31.7 0.8 %gather_fusion.1 = f32[24]{0:T(128)S(1)} fusion(f32[24,24]{1,0:T(8,128)S(1)} %copy-done.1, s32[24]{0:T(128)S(1)} %or_bitcast_fusion), kind=kCustom, calls=%fused_computation.1 | custom fusion | bytes 384 | tf_op jit(solution)/shard_map/jit(_diag)/jit(diagonal)/cond/branch_0_fun/gather | solution.py:707
  32.4 0.1 reshape.43
  32.6 0.1 reshape.46
  32.6 0.1 copy.39
  32.8 0.1 stack_reshape.10
  32.8 0.1 reshape.47
  32.9 0.1 copy.40
  33.0 0.0 copy-start.2
  33.0 0.1 stack_reshape.11
  33.1 0.6 copy-done.2
  33.7 0.1 reshape.45
  33.8 0.1 copy.38
  33.9 0.1 stack_reshape.9
  34.0 0.1 copy.37
  34.1 0.4 copy.32
  34.6 0.2 reshape.42
  34.7 0.4 copy.33
  35.2 0.2 reshape.44
  35.4 1.4 %collective-permute-done.1.halo = f32[102,8,128]{2,1,0:T(8,128)S(1)} collective-permute-done((f32[102,8,128]{2,1,0:T(8,128)S(1)}, f32[102,8,128]{2,1,0:T(8,128)S(1)}, u32[]{:S(2)}, u32[]{:S(2)}) %collective-permute-start.1) | collective-permute-done | bytes 417824 | tf_op jit(solution)/shard_map/ppermute | solution.py:703
  36.8 3.9 %collective-permute-start.2 = (f32[44,8,128]{2,1,0:T(8,128)S(1)}, f32[44,8,128]{2,1,0:T(8,128)S(1)}, u32[]{:S(2)}, u32[]{:S(2)}) collective-permute-start(f32[44,8,128]{2,1,0:T(8,128)S(1)} %slice.58), channel_id=1, source_target_pairs={{0,128},{128,0},{1,129},{129,1},{2,130},{130,2},{3,131},{131,3},{4... | collective-permute-start | bytes 540680 | tf_op jit(solution)/shard_map/ppermute | solution.py:704
  40.6 1.5 %shard_map.150 = (f32[12,32,128]{2,1,0:T(8,128)S(1)}, f32[4,32,128]{2,1,0:T(8,128)S(1)}, f32[3,11,32,128]{3,2,1,0:T(8,128)S(1)}, f32[11,32,128]{2,1,0:T(8,128)S(...) custom-call(s32[1]{0:T(128)} %bitcast.3.core, ...), custom_call_target="tpu_custom_call" | custom-call | tf_op jit(solution)/shard_map/pallas_call | solution.py:711
  42.1 0.0 collective-permute-done.2.share
  42.1 2.1 %shard_map.151 = (f32[4,8,8,128]{3,2,1,0:T(8,128)S(1)}, f32[3,5,32,128]{3,2,1,0:T(8,128)S(1)}, f32[5,32,128]{2,1,0:T(8,128)S(1)}, f32[5,32,128]{2,1,0:T(8,128)S(1)}, f32[2,8,512]{2,1,0:T(8,128)S(1)}) custom-call(s32[1]{0:T(128)} %bitcast.3.core, s32[1]{0:T(128)} %bitcast.4.layer, f32[102,8,128]{2,1,0:T(8,128)S(1)} %collective-permute-done.1.halo, ...), custom_call_target="tpu_custom_call" | custom-call | tf_op jit(solution)/shard_map/pallas_call | solution.py:722
  44.2 0.1 collective-permute-start.3
  44.4 3.0 %collective-permute-start.5 = (f32[4,8,8,128]{3,2,1,0:T(8,128)S(1)}, f32[4,8,8,128]{3,2,1,0:T(8,128)S(1)}, u32[]{:S(2)}, u32[]{:S(2)}) collective-permute-start(f32[4,8,8,128]{3,2,1,0:T(8,128)S(1)} %get-tuple-element.46.own), channel_id=1, source_target_pairs={{0,128},{128,0},{1,129},{129,1},{2,130},{130,2},{3,131},{131,3},{4... | collective-permute-start | bytes 393224 | tf_op jit(solution)/shard_map/ppermute | solution.py:741
  47.3 1.7 %collective-permute-done.3.near = f32[4,8,8,128]{3,2,1,0:T(8,128)S(1)} collective-permute-done((f32[4,8,8,128]{3,2,1,0:T(8,128)S(1)}, f32[4,8,8,128]{3,2,1,0:T(8,128)S(1)}, u32[]{:S(2)}, u32[]{:S(2)}) %collective-permute-start.3) | collective-permute-done | bytes 131104 | tf_op jit(solution)/shard_map/ppermute | solution.py:740
  49.0 1.0 %collective-permute-start.4 = (f32[4,8,8,128]{3,2,1,0:T(8,128)S(1)}, f32[4,8,8,128]{3,2,1,0:T(8,128)S(1)}, u32[]{:S(2)}, u32[]{:S(2)}) collective-permute-start(f32[4,8,8,128]{3,2,1,0:T(8,128)S(1)} %collective-permute-done.3.near), channel_id=1, source_target_pairs={{0,128},{128,0},{1,129},{129,1},{2,130},{130,2},{3,131},{131,3},{4... | collective-permute-start | bytes 393224 | tf_op jit(solution)/shard_map/ppermute | solution.py:742
  50.0 0.0 collective-permute-done.5.partner
  50.0 0.6 shard_map.152
  50.6 0.4 collective-permute-done.4.across
  51.0 1.9 %shard_map.153 = f32[8,8,128]{2,1,0:T(8,128)S(1)} custom-call(s32[1]{0:T(128)} %bitcast.3.core, s32[1]{0:T(128)} %bitcast.4.layer, f32[4,8,8,128]{3,2,1,0:T(8,128)S(1)} %collective-permute-done.4.across, f32[64,32]{1,0:T(8,128)S(1)} %constant_dynamic-update-slice_fusion.5.stiff, f32[32,128]{1,0:T(8,128)S(1)} %pad.26.aux, ...), custom_call_target="tpu_custom_call" | custom-call | tf_op jit(solution)/shard_map/pallas_call | solution.py:749
  52.8 0.4 collective-permute-start.6
  53.3 0.9 %collective-permute-done.6 = f32[8,8,128]{2,1,0:T(8,128)S(1)} collective-permute-done((f32[8,8,128]{2,1,0:T(8,128)S(1)}, f32[8,8,128]{2,1,0:T(8,128)S(1)}, u32[]{:S(2)}, u32[]{:S(2)}) %collective-permute-start.6) | collective-permute-done | bytes 32800 | tf_op jit(solution)/shard_map/ppermute | solution.py:763
  54.2 9.8 %all_to_all.11.got = f32[16,8,128]{2,1,0:T(8,128)S(1)} all-to-all(f32[16,8,128]{2,1,0:T(8,128)S(1)} %pad_maximum_fusion), channel_id=1, replica_groups=mesh['grp'=2,'gz'=8,'gx'=4,'gy'=4] {'gx','gy'}, dimensions={0} | all-to-all | bytes 131072 | tf_op jit(solution)/shard_map/all_to_all | solution.py:765
  63.9 0.8 %shard_map.154 = (f32[4,8,128]{2,1,0:T(8,128)}, f32[3,512]{1,0:T(4,128)}) custom-call(s32[1]{0:T(128)} %bitcast.3.core, f32[16,8,128]{2,1,0:T(8,128)S(1)} %all_to_all.11.got), custom_call_target="tpu_custom_call" | custom-call | tf_op jit(solution)/shard_map/pallas_call | solution.py:766
  (22 shorter events, 0.3 us)
Async XLA Ops:
  24.6 3.9 %collective-permute-start = (f32[16,13,8,128]{3,2,1,0:T(8,128)S(1)}, f32[16,13,8,128]{3,2,1,0:T(8,128)S(1)}, u32[]{:S(2)}, u32[]{:S(2)}) collective-permute-start(f32[16,13,8,128]{3,2,1,0:T(8,128)S(1)} %all_to_all.10), channel_id=1, source_target_pairs={{0,128},{128,0},{1,129},{129,1},{2,130},{130,2},{3,131},{131,3},{4... | collective-permute-start | bytes 2555912 | tf_op jit(solution)/shard_map/ppermute | solution.py:693
  28.7 2.0 %copy-start = (f32[24,24]{1,0:T(8,128)S(1)}, f32[24,24]{1,0:T(8,128)}, u32[]{:S(2)}) copy-start(f32[24,24]{1,0:T(8,128)} %param.25) | copy-start | bytes 6916
  28.7 8.0 %collective-permute-start.1 = (f32[102,8,128]{2,1,0:T(8,128)S(1)}, f32[102,8,128]{2,1,0:T(8,128)S(1)}, u32[]{:S(2)}, u32[]{:S(2)}) collective-permute-start(f32[102,8,128]{2,1,0:T(8,128)S(1)} %constant_dynamic-update-slice_fusion), channel_id=1, source_target_pairs={{128,16},{144,32},{160,48},{176,64},{192,80},{208,96},{224,112},{2... | collective-permute-start | bytes 1253384 | tf_op jit(solution)/shard_map/ppermute | solution.py:703
  30.9 0.8 %copy-start.1 = (f32[24,24]{1,0:T(8,128)S(1)}, f32[24,24]{1,0:T(8,128)}, u32[]{:S(2)}) copy-start(f32[24,24]{1,0:T(8,128)} %param.26) | copy-start | bytes 6916
  33.0 0.7 %copy-start.2 = (f32[24]{0:T(128)S(1)}, f32[24]{0:T(128)}, u32[]{:S(2)}) copy-start(f32[24]{0:T(128)} %param.27) | copy-start | bytes 292
  36.8 5.3 %collective-permute-start.2 = (f32[44,8,128]{2,1,0:T(8,128)S(1)}, f32[44,8,128]{2,1,0:T(8,128)S(1)}, u32[]{:S(2)}, u32[]{:S(2)}) collective-permute-start(f32[44,8,128]{2,1,0:T(8,128)S(1)} %slice.58), channel_id=1, source_target_pairs={{0,128},{128,0},{1,129},{129,1},{2,130},{130,2},{3,131},{131,3},{4... | collective-permute-start | bytes 540680 | tf_op jit(solution)/shard_map/ppermute | solution.py:704
  44.2 4.8 %collective-permute-start.3 = (f32[4,8,8,128]{3,2,1,0:T(8,128)S(1)}, f32[4,8,8,128]{3,2,1,0:T(8,128)S(1)}, u32[]{:S(2)}, u32[]{:S(2)}) collective-permute-start(f32[4,8,8,128]{3,2,1,0:T(8,128)S(1)} %get-tuple-element.46.own), channel_id=1, source_target_pairs={{128,16},{144,32},{160,48},{176,64},{192,80},{208,96},{224,112},{2... | collective-permute-start | bytes 393224 | tf_op jit(solution)/shard_map/ppermute | solution.py:740
  44.4 5.6 %collective-permute-start.5 = (f32[4,8,8,128]{3,2,1,0:T(8,128)S(1)}, f32[4,8,8,128]{3,2,1,0:T(8,128)S(1)}, u32[]{:S(2)}, u32[]{:S(2)}) collective-permute-start(f32[4,8,8,128]{3,2,1,0:T(8,128)S(1)} %get-tuple-element.46.own), channel_id=1, source_target_pairs={{0,128},{128,0},{1,129},{129,1},{2,130},{130,2},{3,131},{131,3},{4... | collective-permute-start | bytes 393224 | tf_op jit(solution)/shard_map/ppermute | solution.py:741
  49.0 1.9 %collective-permute-start.4 = (f32[4,8,8,128]{3,2,1,0:T(8,128)S(1)}, f32[4,8,8,128]{3,2,1,0:T(8,128)S(1)}, u32[]{:S(2)}, u32[]{:S(2)}) collective-permute-start(f32[4,8,8,128]{3,2,1,0:T(8,128)S(1)} %collective-permute-done.3.near), channel_id=1, source_target_pairs={{0,128},{128,0},{1,129},{129,1},{2,130},{130,2},{3,131},{131,3},{4... | collective-permute-start | bytes 393224 | tf_op jit(solution)/shard_map/ppermute | solution.py:742
  52.8 1.3 %collective-permute-start.6 = (f32[8,8,128]{2,1,0:T(8,128)S(1)}, f32[8,8,128]{2,1,0:T(8,128)S(1)}, u32[]{:S(2)}, u32[]{:S(2)}) collective-permute-start(f32[8,8,128]{2,1,0:T(8,128)S(1)} %shard_map.153), channel_id=1, source_target_pairs={{0,128},{128,0},{1,129},{129,1},{2,130},{130,2},{3,131},{131,3},{4... | collective-permute-start | bytes 98312 | tf_op jit(solution)/shard_map/ppermute | solution.py:763

commit v5 on v4

--- a/solution.py
+++ b/solution.py
@@ -222,11 +222,11 @@
     return lambda way, x: early[way, x] if x < EARLY else late[way, x - EARLY]
 
 
-def one_sweep(src, dst, coef, rhs, inverse, least):
-    outer = coef(0, least - 1) * src[least - 1]
-    p = src[least]
-    for x in range(least, PLANES):
-        q = src[x + 1] if x < PLANES - 1 else roll(p, 64)
+def one_sweep(src, dst, coef, rhs, inverse, least, most=PLANES):
+    outer = coef(0, least - 1) * src(least - 1)
+    p = src(least)
+    for x in range(least, most):
+        q = src(x + 1) if x < PLANES - 1 else roll(p, 64)
         inner, up, deep = coef(0, x), coef(1, x), coef(2, x)
         total = rhs[x] + inner * q + outer
         total = total + up * roll(p, 31, 0) + roll(up * p, 1, 0)
@@ -238,7 +238,7 @@
 
 def sweeps(press, coef, rhs, inverse, first):
     for n in range(SWEEPS):
-        one_sweep(press.at[n % 2], press.at[1 - n % 2], coef, rhs, inverse, first + n)
+        one_sweep(lambda x, n=n: press[n % 2, x], press.at[1 - n % 2], coef, rhs, inverse, first + n)
 
 
 def pair_matrix():
@@ -538,7 +538,10 @@
             rhs[x] = fixed(x) + stabilize * press[x] - (8.0 * biot_coef) * change
 
 
-def resume_kernel(core, layer, own, partner, near, aux, start, fixed_late, press, u, rhs, strain, moved):
+def resume_kernel(
+    core, layer, own, partner, near, aux, start, coef_late, fixed_late, inverse_late,
+    press, u, rhs, edges, inner, strain, moved, swept,
+):
     ok = inside_flags(core, layer)
     low = low_mask((32, 128))
 
@@ -580,10 +583,22 @@
         moved[n] = u[n] - start[n]
     strain_rows(aux, lambda n: moved[n], range(3, 13), strain)
     right_sides(strain, range(3, 8), press, lambda x: fixed_late[x - EARLY], rhs)
+    for k in range(SWEEPS + 1):
+        if k:
+            one_sweep(
+                lambda x, k=k: press[x] if k == 1 else swept[k % 2, x], swept.at[1 - k % 2],
+                lambda way, x: coef_late[way, x - EARLY], rhs, lambda x: inverse_late[x - EARLY], 5 + k,
+            )
+        level = press if k == 0 else swept.at[1 - k % 2]
+        if k < SWEEPS:
+            edges[k, 0] = level[5 + k]
+            edges[k, 1] = level[6 + k]
+    for x in range(11, PLANES):
+        inner[x - 11] = swept[1, x]
 
 
 def second_kernel(
-    core, layer, across, stiff, aux, held, u, rhs_late,
+    core, layer, across, stiff, aux, held, u, rhs_late, edges, inner,
     coef_late, fixed_late, inverse_late, start, lam, mu, load, sup, safe, gain,
     coef_early, fixed_early, inverse_early, beside,
     last, press, rhs, means, nodes, strain, moved,
@@ -591,9 +606,9 @@
     ok = inside_flags(core, layer)
     low = low_mask((32, 128))
     first = core[0] == 0
-    for x in range(2, PLANES):
+    for x in range(2, 6):
         press[0, x] = held[x]
-    for x in range(6, PLANES):
+    for x in range(6, 11):
         rhs[x] = rhs_late[x]
     for n in range(2, 14):
         nodes[n] = u[n]
@@ -612,7 +627,13 @@
     strain[14] = jnp.zeros((1, 512), f32)
     strain_rows(aux, lambda n: moved[0, n], (1, 2, 13), strain)
     right_sides(strain, (1, 2), press.at[0], both(fixed_early, fixed_late), rhs)
-    sweeps(press, both_faces(coef_early, coef_late), rhs, both(inverse_early, inverse_late), 3)
+    for k in range(1, SWEEPS + 1):
+        one_sweep(
+            lambda x, k=k: press[1 - k % 2, x] if x < 4 + k else edges[k - 1, x - 4 - k], press.at[k % 2],
+            both_faces(coef_early, coef_late), rhs, both(inverse_early, inverse_late), 2 + k, 5 + k,
+        )
+    for x in range(11, PLANES):
+        press[0, x] = inner[x - 11]
     block_means(press.at[0], means, 4, 10)
     displacements(nodes, lam, mu, load, sup, safe, gain, means, stiff, aux, moved, 6, 9)
     pack_last(press.at[0], moved, last)
@@ -742,14 +763,21 @@
     across = lax.ppermute(near, "grp", swap)
     resumed = call(
         resume_kernel,
-        (shape(PLANES, 32, 128), shape(NODES, 8, 512), shape(PLANES, 32, 128)),
-        [SM, SM] + [VM] * 6,
-        [pltpu.VMEM((PLANES, 1, 512), f32), pltpu.VMEM((NODES, 8, 512), f32)],
-    )(core_arg, layer_arg, mid, partner, near, aux, statics[5], statics[3])
+        (
+            shape(PLANES, 32, 128), shape(NODES, 8, 512), shape(PLANES, 32, 128),
+            shape(SWEEPS, 2, 32, 128), shape(PLANES - 11, 32, 128),
+        ),
+        [SM, SM] + [VM] * 8,
+        [
+            pltpu.VMEM((PLANES, 1, 512), f32),
+            pltpu.VMEM((NODES, 8, 512), f32),
+            pltpu.VMEM((2, PLANES, 32, 128), f32),
+        ],
+    )(core_arg, layer_arg, mid, partner, near, aux, statics[5], *statics[2:5])
     last = call(
         second_kernel,
         shape(8, 8, 128),
-        [SM, SM] + [VM] * 20,
+        [SM, SM] + [VM] * 22,
         [
             pltpu.VMEM((2, PLANES, 32, 128), f32),
             pltpu.VMEM((PLANES, 32, 128), f32),

time: 65 us -> 65 us (level)
  transfers between devices with their start and end apart: 7 -> 7, of which waited for: 5 -> 4; matrix products, arithmetic and copies ran while one was open for 6% -> 6% of each run, Pallas kernels for 3% -> 4%
where the time goes in v5:
time: 65 us; the launch traced here: 64.6 us
  blocking collectives  31.2 us (48%)
  starting transfers between devices  12.1 us (19%)
  Pallas kernels  9.58 us (15%)
  waiting for transfers between devices  6.05 us (9%)
  local copies, waits for them, and re-layouts  4.64 us (7%)
  between operations  0.85 us (1%)
    all_to_all x1, blocking collectives, shards(): grid = lax.all_to_all(packed, ('gx', 'gy'), 0, 0, tiled=True)  21.5 us
    all_to_all x1, blocking collectives, shards(): back = lax.all_to_all(whole, ('gx', 'gy'), 0, 0, tiled=True)  9.76 us
    ppermute x1, starting transfers between devices, shards(): share = lax.ppermute(halo[:44], 'grp', swap)  3.87 us
    ppermute x1, starting transfers between devices, shards(): partner = lax.ppermute(mid, 'grp', swap)  2.98 us
    pallas_call x1, Pallas kernels, shards(): call(pack_kernel, shape(16, TILES, 8, 128), [SM, SM, SM] + [HB] * 11, [pl...  2.48 us
    pallas_call x1, Pallas kernels, shards(): call(first_kernel, (shape(4, 8, 8, 128), shape(3, EARLY, 32, 128), shape(...  2.14 us
    ppermute x1, waiting for transfers between devices, shards(): grid = grid + lax.ppermute(grid, 'grp', swap)  2.01 us
    ppermute x1, starting transfers between devices, shards(): halo = lax.ppermute(sent, ('grp', 'gz'), ring)  1.98 us
  transfers between devices with their start and end apart: 7, of which 4 were waited for; matrix products, arithmetic and copies ran while one was open for 6% of the time, Pallas kernels for 4%

profile of v5, /device:TPU:1, one launch (start us, length us, event | category | flops | bytes accessed | tf_op | source)
XLA Modules:
  0.0 64.6 jit_solution(17574531877149269641)
XLA Ops:
  0.6 2.5 %shard_map.149 = f32[16,13,8,128]{3,2,1,0:T(8,128)} custom-call(s32[1]{0:T(128)} %bitcast.core, s32[1]{0:T(128)} %bitcast.1.across, s32[1]{0:T(128)} %bitcast.2.layer, f32[16]{0:T(128)} %perms.1, f32[4,8,128]{2,1,0:T(8,128)} %p0.1, f32[4,8,128]{2,1,0:T(8,128)} %src.1, f32[4,8,128]{2,1,0:T(8,128)} %sto.1, s32[4,8,128]{2,1,0:T(8,128)} %cls.1, f32[3,512]{1,0:T(4,128)} %disp.1, ...), custom_call_target="tpu_custom_call" | custom-call | tf_op jit(solution)/shard_map/pallas_call | solution.py:686
  3.1 21.5 %all_to_all.10 = f32[16,13,8,128]{3,2,1,0:T(8,128)S(1)} all-to-all(f32[16,13,8,128]{3,2,1,0:T(8,128)} %shard_map.149), channel_id=1, replica_groups=mesh['grp'=2,'gz'=8,'gx'=4,'gy'=4] {'gx','gy'}, dimensions={0} | all-to-all | bytes 1703936 | tf_op jit(solution)/shard_map/all_to_all | solution.py:706
  24.6 1.9 %collective-permute-start = (f32[16,13,8,128]{3,2,1,0:T(8,128)S(1)}, f32[16,13,8,128]{3,2,1,0:T(8,128)S(1)}, u32[]{:S(2)}, u32[]{:S(2)}) collective-permute-start(f32[16,13,8,128]{3,2,1,0:T(8,128)S(1)} %all_to_all.10), channel_id=1, source_target_pairs={{0,128},{128,0},{1,129},{129,1},{2,130},{130,2},{3,131},{131,3},{4... | collective-permute-start | bytes 2555912 | tf_op jit(solution)/shard_map/ppermute | solution.py:714
  26.5 2.0 %collective-permute-done = f32[16,13,8,128]{3,2,1,0:T(8,128)S(1)} collective-permute-done((f32[16,13,8,128]{3,2,1,0:T(8,128)S(1)}, f32[16,13,8,128]{3,2,1,0:T(8,128)S(1)}, u32[]{:S(2)}, u32[]{:S(2)}) %collective-permute-start) | collective-permute-done | bytes 852000 | tf_op jit(solution)/shard_map/ppermute | solution.py:714
  28.5 0.1 add.23.grid
  28.7 0.0 copy-start
  28.7 2.0 %collective-permute-start.1 = (f32[102,8,128]{2,1,0:T(8,128)S(1)}, f32[102,8,128]{2,1,0:T(8,128)S(1)}, u32[]{:S(2)}, u32[]{:S(2)}) collective-permute-start(f32[102,8,128]{2,1,0:T(8,128)S(1)} %constant_dynamic-update-slice_fusion), channel_id=1, source_target_pairs={{128,16},{144,32},{160,48},{176,64},{192,80},{208,96},{224,112},{2... | collective-permute-start | bytes 1253384 | tf_op jit(solution)/shard_map/ppermute | solution.py:724
  30.7 0.0 copy-done
  30.7 0.1 reshape.41
  30.9 0.0 copy-start.1
  30.9 0.8 %gather_fusion = f32[24]{0:T(128)S(1)} fusion(f32[24,24]{1,0:T(8,128)S(1)} %copy-done, s32[24]{0:T(128)S(1)} %or_bitcast_fusion), kind=kCustom, calls=%fused_computation | custom fusion | bytes 384 | tf_op jit(solution)/shard_map/jit(_diag)/jit(diagonal)/cond/branch_0_fun/gather | solution.py:728
  31.7 0.0 copy-done.1
  31.7 0.8 %gather_fusion.1 = f32[24]{0:T(128)S(1)} fusion(f32[24,24]{1,0:T(8,128)S(1)} %copy-done.1, s32[24]{0:T(128)S(1)} %or_bitcast_fusion), kind=kCustom, calls=%fused_computation.1 | custom fusion | bytes 384 | tf_op jit(solution)/shard_map/jit(_diag)/jit(diagonal)/cond/branch_0_fun/gather | solution.py:728
  32.4 0.1 reshape.43
  32.6 0.1 reshape.46
  32.6 0.1 copy.39
  32.8 0.1 stack_reshape.10
  32.8 0.1 reshape.47
  32.9 0.1 copy.40
  33.0 0.0 copy-start.2
  33.0 0.1 stack_reshape.11
  33.1 0.6 copy-done.2
  33.7 0.1 reshape.45
  33.8 0.1 copy.38
  33.9 0.1 stack_reshape.9
  34.0 0.1 copy.37
  34.1 0.4 copy.32
  34.6 0.2 reshape.42
  34.7 0.4 copy.33
  35.2 0.2 reshape.44
  35.4 1.4 %collective-permute-done.1.halo = f32[102,8,128]{2,1,0:T(8,128)S(1)} collective-permute-done((f32[102,8,128]{2,1,0:T(8,128)S(1)}, f32[102,8,128]{2,1,0:T(8,128)S(1)}, u32[]{:S(2)}, u32[]{:S(2)}) %collective-permute-start.1) | collective-permute-done | bytes 417824 | tf_op jit(solution)/shard_map/ppermute | solution.py:724
  36.8 3.9 %collective-permute-start.2 = (f32[44,8,128]{2,1,0:T(8,128)S(1)}, f32[44,8,128]{2,1,0:T(8,128)S(1)}, u32[]{:S(2)}, u32[]{:S(2)}) collective-permute-start(f32[44,8,128]{2,1,0:T(8,128)S(1)} %slice.58), channel_id=1, source_target_pairs={{0,128},{128,0},{1,129},{129,1},{2,130},{130,2},{3,131},{131,3},{4... | collective-permute-start | bytes 540680 | tf_op jit(solution)/shard_map/ppermute | solution.py:725
  40.6 1.5 %shard_map.150 = (f32[12,32,128]{2,1,0:T(8,128)S(1)}, f32[4,32,128]{2,1,0:T(8,128)S(1)}, f32[3,11,32,128]{3,2,1,0:T(8,128)S(1)}, f32[11,32,128]{2,1,0:T(8,128)S(...) custom-call(s32[1]{0:T(128)} %bitcast.3.core, ...), custom_call_target="tpu_custom_call" | custom-call | tf_op jit(solution)/shard_map/pallas_call | solution.py:732
  42.1 0.0 collective-permute-done.2.share
  42.1 2.1 %shard_map.151 = (f32[4,8,8,128]{3,2,1,0:T(8,128)S(1)}, f32[3,5,32,128]{3,2,1,0:T(8,128)S(1)}, f32[5,32,128]{2,1,0:T(8,128)S(1)}, f32[5,32,128]{2,1,0:T(8,128)S(1)}, f32[2,8,512]{2,1,0:T(8,128)S(1)}) custom-call(s32[1]{0:T(128)} %bitcast.3.core, s32[1]{0:T(128)} %bitcast.4.layer, f32[102,8,128]{2,1,0:T(8,128)S(1)} %collective-permute-done.1.halo, ...), custom_call_target="tpu_custom_call" | custom-call | tf_op jit(solution)/shard_map/pallas_call | solution.py:743
  44.2 0.1 collective-permute-start.3
  44.4 3.0 %collective-permute-start.5 = (f32[4,8,8,128]{3,2,1,0:T(8,128)S(1)}, f32[4,8,8,128]{3,2,1,0:T(8,128)S(1)}, u32[]{:S(2)}, u32[]{:S(2)}) collective-permute-start(f32[4,8,8,128]{3,2,1,0:T(8,128)S(1)} %get-tuple-element.48.own), channel_id=1, source_target_pairs={{0,128},{128,0},{1,129},{129,1},{2,130},{130,2},{3,131},{131,3},{4... | collective-permute-start | bytes 393224 | tf_op jit(solution)/shard_map/ppermute | solution.py:762
  47.3 1.7 %collective-permute-done.3.near = f32[4,8,8,128]{3,2,1,0:T(8,128)S(1)} collective-permute-done((f32[4,8,8,128]{3,2,1,0:T(8,128)S(1)}, f32[4,8,8,128]{3,2,1,0:T(8,128)S(1)}, u32[]{:S(2)}, u32[]{:S(2)}) %collective-permute-start.3) | collective-permute-done | bytes 131104 | tf_op jit(solution)/shard_map/ppermute | solution.py:761
  49.0 1.0 %collective-permute-start.4 = (f32[4,8,8,128]{3,2,1,0:T(8,128)S(1)}, f32[4,8,8,128]{3,2,1,0:T(8,128)S(1)}, u32[]{:S(2)}, u32[]{:S(2)}) collective-permute-start(f32[4,8,8,128]{3,2,1,0:T(8,128)S(1)} %collective-permute-done.3.near), channel_id=1, source_target_pairs={{0,128},{128,0},{1,129},{129,1},{2,130},{130,2},{3,131},{131,3},{4... | collective-permute-start | bytes 393224 | tf_op jit(solution)/shard_map/ppermute | solution.py:763
  50.0 0.0 collective-permute-done.5.partner
  50.0 1.1 %shard_map.152 = (f32[16,32,128]{2,1,0:T(8,128)S(1)}, f32[16,8,512]{2,1,0:T(8,128)S(1)}, f32[16,32,128]{2,1,0:T(8,128)S(1)}, f32[6,2,32,128]{3,2,1,0:T(8,128)S(1)}, f32[5,32,128]{2,1,0:T(8,128)S(1)}) custom-call(s32[1]{0:T(128)} %bitcast.3.core, s32[1]{0:T(128)} %bitcast.4.layer, f32[4,8,8,128]{3,2,1,0:T(8,128)S(1)} %get-tuple-element.48.own, ...), custom_call_target="tpu_custom_call" | custom-call | tf_op jit(solution)/shard_map/pallas_call | solution.py:764
  51.1 0.0 collective-permute-done.4.across
  51.1 1.7 %shard_map.153 = f32[8,8,128]{2,1,0:T(8,128)S(1)} custom-call(s32[1]{0:T(128)} %bitcast.3.core, s32[1]{0:T(128)} %bitcast.4.layer, f32[4,8,8,128]{3,2,1,0:T(8,128)S(1)} %collective-permute-done.4.across, f32[64,32]{1,0:T(8,128)S(1)} %constant_dynamic-update-slice_fusion.5.stiff, f32[32,128]{1,0:T(8,128)S(1)} %pad.26.aux, ...), custom_call_target="tpu_custom_call" | custom-call | tf_op jit(solution)/shard_map/pallas_call | solution.py:777
  52.8 0.3 collective-permute-start.6
  53.1 1.0 %collective-permute-done.6 = f32[8,8,128]{2,1,0:T(8,128)S(1)} collective-permute-done((f32[8,8,128]{2,1,0:T(8,128)S(1)}, f32[8,8,128]{2,1,0:T(8,128)S(1)}, u32[]{:S(2)}, u32[]{:S(2)}) %collective-permute-start.6) | collective-permute-done | bytes 32800 | tf_op jit(solution)/shard_map/ppermute | solution.py:791
  54.1 9.8 %all_to_all.11.got = f32[16,8,128]{2,1,0:T(8,128)S(1)} all-to-all(f32[16,8,128]{2,1,0:T(8,128)S(1)} %pad_maximum_fusion), channel_id=1, replica_groups=mesh['grp'=2,'gz'=8,'gx'=4,'gy'=4] {'gx','gy'}, dimensions={0} | all-to-all | bytes 131072 | tf_op jit(solution)/shard_map/all_to_all | solution.py:793
  63.8 0.8 %shard_map.154 = (f32[4,8,128]{2,1,0:T(8,128)}, f32[3,512]{1,0:T(4,128)}) custom-call(s32[1]{0:T(128)} %bitcast.3.core, f32[16,8,128]{2,1,0:T(8,128)S(1)} %all_to_all.11.got), custom_call_target="tpu_custom_call" | custom-call | tf_op jit(solution)/shard_map/pallas_call | solution.py:794
  (22 shorter events, 0.3 us)
Async XLA Ops:
  24.6 3.9 %collective-permute-start = (f32[16,13,8,128]{3,2,1,0:T(8,128)S(1)}, f32[16,13,8,128]{3,2,1,0:T(8,128)S(1)}, u32[]{:S(2)}, u32[]{:S(2)}) collective-permute-start(f32[16,13,8,128]{3,2,1,0:T(8,128)S(1)} %all_to_all.10), channel_id=1, source_target_pairs={{0,128},{128,0},{1,129},{129,1},{2,130},{130,2},{3,131},{131,3},{4... | collective-permute-start | bytes 2555912 | tf_op jit(solution)/shard_map/ppermute | solution.py:714
  28.7 2.0 %copy-start = (f32[24,24]{1,0:T(8,128)S(1)}, f32[24,24]{1,0:T(8,128)}, u32[]{:S(2)}) copy-start(f32[24,24]{1,0:T(8,128)} %param.25) | copy-start | bytes 6916
  28.7 8.0 %collective-permute-start.1 = (f32[102,8,128]{2,1,0:T(8,128)S(1)}, f32[102,8,128]{2,1,0:T(8,128)S(1)}, u32[]{:S(2)}, u32[]{:S(2)}) collective-permute-start(f32[102,8,128]{2,1,0:T(8,128)S(1)} %constant_dynamic-update-slice_fusion), channel_id=1, source_target_pairs={{128,16},{144,32},{160,48},{176,64},{192,80},{208,96},{224,112},{2... | collective-permute-start | bytes 1253384 | tf_op jit(solution)/shard_map/ppermute | solution.py:724
  30.9 0.8 %copy-start.1 = (f32[24,24]{1,0:T(8,128)S(1)}, f32[24,24]{1,0:T(8,128)}, u32[]{:S(2)}) copy-start(f32[24,24]{1,0:T(8,128)} %param.26) | copy-start | bytes 6916
  33.0 0.7 %copy-start.2 = (f32[24]{0:T(128)S(1)}, f32[24]{0:T(128)}, u32[]{:S(2)}) copy-start(f32[24]{0:T(128)} %param.27) | copy-start | bytes 292
  36.8 5.3 %collective-permute-start.2 = (f32[44,8,128]{2,1,0:T(8,128)S(1)}, f32[44,8,128]{2,1,0:T(8,128)S(1)}, u32[]{:S(2)}, u32[]{:S(2)}) collective-permute-start(f32[44,8,128]{2,1,0:T(8,128)S(1)} %slice.58), channel_id=1, source_target_pairs={{0,128},{128,0},{1,129},{129,1},{2,130},{130,2},{3,131},{131,3},{4... | collective-permute-start | bytes 540680 | tf_op jit(solution)/shard_map/ppermute | solution.py:725
  44.2 4.8 %collective-permute-start.3 = (f32[4,8,8,128]{3,2,1,0:T(8,128)S(1)}, f32[4,8,8,128]{3,2,1,0:T(8,128)S(1)}, u32[]{:S(2)}, u32[]{:S(2)}) collective-permute-start(f32[4,8,8,128]{3,2,1,0:T(8,128)S(1)} %get-tuple-element.48.own), channel_id=1, source_target_pairs={{128,16},{144,32},{160,48},{176,64},{192,80},{208,96},{224,112},{2... | collective-permute-start | bytes 393224 | tf_op jit(solution)/shard_map/ppermute | solution.py:761
  44.4 5.6 %collective-permute-start.5 = (f32[4,8,8,128]{3,2,1,0:T(8,128)S(1)}, f32[4,8,8,128]{3,2,1,0:T(8,128)S(1)}, u32[]{:S(2)}, u32[]{:S(2)}) collective-permute-start(f32[4,8,8,128]{3,2,1,0:T(8,128)S(1)} %get-tuple-element.48.own), channel_id=1, source_target_pairs={{0,128},{128,0},{1,129},{129,1},{2,130},{130,2},{3,131},{131,3},{4... | collective-permute-start | bytes 393224 | tf_op jit(solution)/shard_map/ppermute | solution.py:762
  49.0 2.1 %collective-permute-start.4 = (f32[4,8,8,128]{3,2,1,0:T(8,128)S(1)}, f32[4,8,8,128]{3,2,1,0:T(8,128)S(1)}, u32[]{:S(2)}, u32[]{:S(2)}) collective-permute-start(f32[4,8,8,128]{3,2,1,0:T(8,128)S(1)} %collective-permute-done.3.near), channel_id=1, source_target_pairs={{0,128},{128,0},{1,129},{129,1},{2,130},{130,2},{3,131},{131,3},{4... | collective-permute-start | bytes 393224 | tf_op jit(solution)/shard_map/ppermute | solution.py:763
  52.8 1.3 %collective-permute-start.6 = (f32[8,8,128]{2,1,0:T(8,128)S(1)}, f32[8,8,128]{2,1,0:T(8,128)S(1)}, u32[]{:S(2)}, u32[]{:S(2)}) collective-permute-start(f32[8,8,128]{2,1,0:T(8,128)S(1)} %shard_map.153), channel_id=1, source_target_pairs={{0,128},{128,0},{1,129},{129,1},{2,130},{130,2},{3,131},{131,3},{4... | collective-permute-start | bytes 98312 | tf_op jit(solution)/shard_map/ppermute | solution.py:791

commit v6 on v5

--- a/solution.py
+++ b/solution.py
@@ -501,8 +501,8 @@
     pack_mid(core, press.at[0], moved, mid)
 
 
-def node_of(ref, k, y):
-    value = ref[y, 5 + k // 2]
+def node_of(ref, k, y, least=5):
+    value = ref[y, least + k // 2]
     return jnp.where(rows((8, 128)) < 4, roll(value, 4, 0) if k % 2 else value, 0.0)
 
 
@@ -618,8 +618,8 @@
         press[0, x] = jnp.where(low & jnp.logical_not(first), turned, held[x])
     for y in range(4):
         at = slice(128 * y, 128 * y + 128)
-        nodes[1, :, at] = jnp.where(first, u[1, :, at], node_of(across, 3, y) * ok[1])
-        nodes[14, :, at] = jnp.where(first, node_of(across, 0, y) * ok[1], u[14, :, at])
+        nodes[1, :, at] = jnp.where(first, u[1, :, at], node_of(across, 3, y, 2) * ok[1])
+        nodes[14, :, at] = jnp.where(first, node_of(across, 0, y, 2) * ok[1], u[14, :, at])
     for n in (2, 3, 13):
         moved[0, n] = nodes[n] - start[n]
     moved[0, 1] = nodes[1] - jnp.where(first, start[1], beside[1])
@@ -760,7 +760,7 @@
 
     near = lax.ppermute(mid, ("grp", "gz"), ring)
     partner = lax.ppermute(mid, "grp", swap)
-    across = lax.ppermute(near, "grp", swap)
+    across = lax.ppermute(jnp.concatenate([near[:, 0:2], near[:, 5:7]], axis=1), "grp", swap)
     resumed = call(
         resume_kernel,
         (

time: 65 us -> 65.1 us (level)
  no operation moved by 1% of the time
where the time goes in v6:
time: 65.1 us; the launch traced here: 64.7 us
  blocking collectives  31.2 us (48%)
  starting transfers between devices  12.1 us (19%)
  Pallas kernels  9.59 us (15%)
  waiting for transfers between devices  6.14 us (9%)
  local copies, waits for them, and re-layouts  4.65 us (7%)
  between operations  0.86 us (1%)
    all_to_all x1, blocking collectives, shards(): grid = lax.all_to_all(packed, ('gx', 'gy'), 0, 0, tiled=True)  21.5 us
    all_to_all x1, blocking collectives, shards(): back = lax.all_to_all(whole, ('gx', 'gy'), 0, 0, tiled=True)  9.75 us
    ppermute x1, starting transfers between devices, shards(): share = lax.ppermute(halo[:44], 'grp', swap)  3.87 us
    ppermute x1, starting transfers between devices, shards(): partner = lax.ppermute(mid, 'grp', swap)  2.99 us
    pallas_call x1, Pallas kernels, shards(): call(pack_kernel, shape(16, TILES, 8, 128), [SM, SM, SM] + [HB] * 11, [pl...  2.49 us
    pallas_call x1, Pallas kernels, shards(): call(first_kernel, (shape(4, 8, 8, 128), shape(3, EARLY, 32, 128), shape(...  2.14 us
    ppermute x1, waiting for transfers between devices, shards(): grid = grid + lax.ppermute(grid, 'grp', swap)  2.01 us
    ppermute x1, starting transfers between devices, shards(): halo = lax.ppermute(sent, ('grp', 'gz'), ring)  1.98 us
  transfers between devices with their start and end apart: 7, of which 4 were waited for; matrix products, arithmetic and copies ran while one was open for 6% of the time, Pallas kernels for 4%

profile of v6, /device:TPU:1, one launch (start us, length us, event | category | flops | bytes accessed | tf_op | source)
XLA Modules:
  0.0 64.7 jit_solution(2004737205281607384)
XLA Ops:
  0.6 2.5 %shard_map.149 = f32[16,13,8,128]{3,2,1,0:T(8,128)} custom-call(s32[1]{0:T(128)} %bitcast.core, s32[1]{0:T(128)} %bitcast.1.across, s32[1]{0:T(128)} %bitcast.2.layer, f32[16]{0:T(128)} %perms.1, f32[4,8,128]{2,1,0:T(8,128)} %p0.1, f32[4,8,128]{2,1,0:T(8,128)} %src.1, f32[4,8,128]{2,1,0:T(8,128)} %sto.1, s32[4,8,128]{2,1,0:T(8,128)} %cls.1, f32[3,512]{1,0:T(4,128)} %disp.1, ...), custom_call_target="tpu_custom_call" | custom-call | tf_op jit(solution)/shard_map/pallas_call | solution.py:686
  3.1 21.5 %all_to_all.10 = f32[16,13,8,128]{3,2,1,0:T(8,128)S(1)} all-to-all(f32[16,13,8,128]{3,2,1,0:T(8,128)} %shard_map.149), channel_id=1, replica_groups=mesh['grp'=2,'gz'=8,'gx'=4,'gy'=4] {'gx','gy'}, dimensions={0} | all-to-all | bytes 1703936 | tf_op jit(solution)/shard_map/all_to_all | solution.py:706
  24.6 1.9 %collective-permute-start = (f32[16,13,8,128]{3,2,1,0:T(8,128)S(1)}, f32[16,13,8,128]{3,2,1,0:T(8,128)S(1)}, u32[]{:S(2)}, u32[]{:S(2)}) collective-permute-start(f32[16,13,8,128]{3,2,1,0:T(8,128)S(1)} %all_to_all.10), channel_id=1, source_target_pairs={{0,128},{128,0},{1,129},{129,1},{2,130},{130,2},{3,131},{131,3},{4... | collective-permute-start | bytes 2555912 | tf_op jit(solution)/shard_map/ppermute | solution.py:714
  26.5 2.0 %collective-permute-done = f32[16,13,8,128]{3,2,1,0:T(8,128)S(1)} collective-permute-done((f32[16,13,8,128]{3,2,1,0:T(8,128)S(1)}, f32[16,13,8,128]{3,2,1,0:T(8,128)S(1)}, u32[]{:S(2)}, u32[]{:S(2)}) %collective-permute-start) | collective-permute-done | bytes 852000 | tf_op jit(solution)/shard_map/ppermute | solution.py:714
  28.5 0.1 add.23.grid
  28.7 0.0 copy-start
  28.8 2.0 %collective-permute-start.1 = (f32[102,8,128]{2,1,0:T(8,128)S(1)}, f32[102,8,128]{2,1,0:T(8,128)S(1)}, u32[]{:S(2)}, u32[]{:S(2)}) collective-permute-start(f32[102,8,128]{2,1,0:T(8,128)S(1)} %constant_dynamic-update-slice_fusion), channel_id=1, source_target_pairs={{128,16},{144,32},{160,48},{176,64},{192,80},{208,96},{224,112},{2... | collective-permute-start | bytes 1253384 | tf_op jit(solution)/shard_map/ppermute | solution.py:724
  30.7 0.0 copy-done
  30.7 0.1 reshape.41
  30.9 0.0 copy-start.1
  30.9 0.8 %gather_fusion = f32[24]{0:T(128)S(1)} fusion(f32[24,24]{1,0:T(8,128)S(1)} %copy-done, s32[24]{0:T(128)S(1)} %or_bitcast_fusion), kind=kCustom, calls=%fused_computation | custom fusion | bytes 384 | tf_op jit(solution)/shard_map/jit(_diag)/jit(diagonal)/cond/branch_0_fun/gather | solution.py:728
  31.7 0.0 copy-done.1
  31.7 0.8 %gather_fusion.1 = f32[24]{0:T(128)S(1)} fusion(f32[24,24]{1,0:T(8,128)S(1)} %copy-done.1, s32[24]{0:T(128)S(1)} %or_bitcast_fusion), kind=kCustom, calls=%fused_computation.1 | custom fusion | bytes 384 | tf_op jit(solution)/shard_map/jit(_diag)/jit(diagonal)/cond/branch_0_fun/gather | solution.py:728
  32.5 0.1 reshape.43
  32.6 0.1 reshape.46
  32.7 0.1 copy.39
  32.8 0.1 stack_reshape.10
  32.9 0.1 reshape.47
  32.9 0.1 copy.40
  33.0 0.0 copy-start.2
  33.1 0.1 stack_reshape.11
  33.1 0.6 copy-done.2
  33.7 0.1 reshape.45
  33.8 0.1 copy.38
  33.9 0.1 stack_reshape.9
  34.0 0.1 copy.37
  34.1 0.4 copy.32
  34.6 0.2 reshape.42
  34.8 0.4 copy.33
  35.2 0.2 reshape.44
  35.4 1.4 %collective-permute-done.1.halo = f32[102,8,128]{2,1,0:T(8,128)S(1)} collective-permute-done((f32[102,8,128]{2,1,0:T(8,128)S(1)}, f32[102,8,128]{2,1,0:T(8,128)S(1)}, u32[]{:S(2)}, u32[]{:S(2)}) %collective-permute-start.1) | collective-permute-done | bytes 417824 | tf_op jit(solution)/shard_map/ppermute | solution.py:724
  36.8 3.9 %collective-permute-start.2 = (f32[44,8,128]{2,1,0:T(8,128)S(1)}, f32[44,8,128]{2,1,0:T(8,128)S(1)}, u32[]{:S(2)}, u32[]{:S(2)}) collective-permute-start(f32[44,8,128]{2,1,0:T(8,128)S(1)} %slice.66), channel_id=1, source_target_pairs={{0,128},{128,0},{1,129},{129,1},{2,130},{130,2},{3,131},{131,3},{4... | collective-permute-start | bytes 540680 | tf_op jit(solution)/shard_map/ppermute | solution.py:725
  40.6 1.5 %shard_map.150 = (f32[12,32,128]{2,1,0:T(8,128)S(1)}, f32[4,32,128]{2,1,0:T(8,128)S(1)}, f32[3,11,32,128]{3,2,1,0:T(8,128)S(1)}, f32[11,32,128]{2,1,0:T(8,128)S(...) custom-call(s32[1]{0:T(128)} %bitcast.3.core, ...), custom_call_target="tpu_custom_call" | custom-call | tf_op jit(solution)/shard_map/pallas_call | solution.py:732
  42.1 0.0 collective-permute-done.2.share
  42.1 2.1 %shard_map.151 = (f32[4,8,8,128]{3,2,1,0:T(8,128)S(1)}, f32[3,5,32,128]{3,2,1,0:T(8,128)S(1)}, f32[5,32,128]{2,1,0:T(8,128)S(1)}, f32[5,32,128]{2,1,0:T(8,128)S(1)}, f32[2,8,512]{2,1,0:T(8,128)S(1)}) custom-call(s32[1]{0:T(128)} %bitcast.3.core, s32[1]{0:T(128)} %bitcast.4.layer, f32[102,8,128]{2,1,0:T(8,128)S(1)} %collective-permute-done.1.halo, ...), custom_call_target="tpu_custom_call" | custom-call | tf_op jit(solution)/shard_map/pallas_call | solution.py:743
  44.3 0.1 collective-permute-start.3
  44.4 3.0 %collective-permute-start.5 = (f32[4,8,8,128]{3,2,1,0:T(8,128)S(1)}, f32[4,8,8,128]{3,2,1,0:T(8,128)S(1)}, u32[]{:S(2)}, u32[]{:S(2)}) collective-permute-start(f32[4,8,8,128]{3,2,1,0:T(8,128)S(1)} %get-tuple-element.48.own), channel_id=1, source_target_pairs={{0,128},{128,0},{1,129},{129,1},{2,130},{130,2},{3,131},{131,3},{4... | collective-permute-start | bytes 393224 | tf_op jit(solution)/shard_map/ppermute | solution.py:762
  47.4 1.7 %collective-permute-done.3.near = f32[4,8,8,128]{3,2,1,0:T(8,128)S(1)} collective-permute-done((f32[4,8,8,128]{3,2,1,0:T(8,128)S(1)}, f32[4,8,8,128]{3,2,1,0:T(8,128)S(1)}, u32[]{:S(2)}, u32[]{:S(2)}) %collective-permute-start.3) | collective-permute-done | bytes 131104 | tf_op jit(solution)/shard_map/ppermute | solution.py:761
  49.0 1.1 %collective-permute-start.4 = (f32[4,4,8,128]{3,2,1,0:T(8,128)S(1)}, f32[4,4,8,128]{3,2,1,0:T(8,128)S(1)}, u32[]{:S(2)}, u32[]{:S(2)}) collective-permute-start(f32[4,4,8,128]{3,2,1,0:T(8,128)S(1)} %pad_maximum_fusion), channel_id=1, source_target_pairs={{0,128},{128,0},{1,129},{129,1},{2,130},{130,2},{3,131},{131,3},{4... | collective-permute-start | bytes 196616 | tf_op jit(solution)/shard_map/ppermute | solution.py:763
  50.1 0.0 collective-permute-done.5.partner
  50.1 1.1 %shard_map.152 = (f32[16,32,128]{2,1,0:T(8,128)S(1)}, f32[16,8,512]{2,1,0:T(8,128)S(1)}, f32[16,32,128]{2,1,0:T(8,128)S(1)}, f32[6,2,32,128]{3,2,1,0:T(8,128)S(1)}, f32[5,32,128]{2,1,0:T(8,128)S(1)}) custom-call(s32[1]{0:T(128)} %bitcast.3.core, s32[1]{0:T(128)} %bitcast.4.layer, f32[4,8,8,128]{3,2,1,0:T(8,128)S(1)} %get-tuple-element.48.own, ...), custom_call_target="tpu_custom_call" | custom-call | tf_op jit(solution)/shard_map/pallas_call | solution.py:764
  51.2 0.0 collective-permute-done.4.across
  51.2 1.7 %shard_map.153 = f32[8,8,128]{2,1,0:T(8,128)S(1)} custom-call(s32[1]{0:T(128)} %bitcast.3.core, s32[1]{0:T(128)} %bitcast.4.layer, f32[4,4,8,128]{3,2,1,0:T(8,128)S(1)} %collective-permute-done.4.across, f32[64,32]{1,0:T(8,128)S(1)} %constant_dynamic-update-slice_fusion.5.stiff, f32[32,128]{1,0:T(8,128)S(1)} %pad.26.aux, ...), custom_call_target="tpu_custom_call" | custom-call | tf_op jit(solution)/shard_map/pallas_call | solution.py:777
  52.9 0.2 collective-permute-start.6
  53.1 1.1 %collective-permute-done.6 = f32[8,8,128]{2,1,0:T(8,128)S(1)} collective-permute-done((f32[8,8,128]{2,1,0:T(8,128)S(1)}, f32[8,8,128]{2,1,0:T(8,128)S(1)}, u32[]{:S(2)}, u32[]{:S(2)}) %collective-permute-start.6) | collective-permute-done | bytes 32800 | tf_op jit(solution)/shard_map/ppermute | solution.py:791
  54.2 9.8 %all_to_all.11.got = f32[16,8,128]{2,1,0:T(8,128)S(1)} all-to-all(f32[16,8,128]{2,1,0:T(8,128)S(1)} %pad_maximum_fusion.1), channel_id=1, replica_groups=mesh['grp'=2,'gz'=8,'gx'=4,'gy'=4] {'gx','gy'}, dimensions={0} | all-to-all | bytes 131072 | tf_op jit(solution)/shard_map/all_to_all | solution.py:793
  64.0 0.8 %shard_map.154 = (f32[4,8,128]{2,1,0:T(8,128)}, f32[3,512]{1,0:T(4,128)}) custom-call(s32[1]{0:T(128)} %bitcast.3.core, f32[16,8,128]{2,1,0:T(8,128)S(1)} %all_to_all.11.got), custom_call_target="tpu_custom_call" | custom-call | tf_op jit(solution)/shard_map/pallas_call | solution.py:794
  (24 shorter events, 0.3 us)
Async XLA Ops:
  24.6 3.9 %collective-permute-start = (f32[16,13,8,128]{3,2,1,0:T(8,128)S(1)}, f32[16,13,8,128]{3,2,1,0:T(8,128)S(1)}, u32[]{:S(2)}, u32[]{:S(2)}) collective-permute-start(f32[16,13,8,128]{3,2,1,0:T(8,128)S(1)} %all_to_all.10), channel_id=1, source_target_pairs={{0,128},{128,0},{1,129},{129,1},{2,130},{130,2},{3,131},{131,3},{4... | collective-permute-start | bytes 2555912 | tf_op jit(solution)/shard_map/ppermute | solution.py:714
  28.7 2.0 %copy-start = (f32[24,24]{1,0:T(8,128)S(1)}, f32[24,24]{1,0:T(8,128)}, u32[]{:S(2)}) copy-start(f32[24,24]{1,0:T(8,128)} %param.25) | copy-start | bytes 6916
  28.8 8.0 %collective-permute-start.1 = (f32[102,8,128]{2,1,0:T(8,128)S(1)}, f32[102,8,128]{2,1,0:T(8,128)S(1)}, u32[]{:S(2)}, u32[]{:S(2)}) collective-permute-start(f32[102,8,128]{2,1,0:T(8,128)S(1)} %constant_dynamic-update-slice_fusion), channel_id=1, source_target_pairs={{128,16},{144,32},{160,48},{176,64},{192,80},{208,96},{224,112},{2... | collective-permute-start | bytes 1253384 | tf_op jit(solution)/shard_map/ppermute | solution.py:724
  30.9 0.8 %copy-start.1 = (f32[24,24]{1,0:T(8,128)S(1)}, f32[24,24]{1,0:T(8,128)}, u32[]{:S(2)}) copy-start(f32[24,24]{1,0:T(8,128)} %param.26) | copy-start | bytes 6916
  33.0 0.7 %copy-start.2 = (f32[24]{0:T(128)S(1)}, f32[24]{0:T(128)}, u32[]{:S(2)}) copy-start(f32[24]{0:T(128)} %param.27) | copy-start | bytes 292
  36.8 5.3 %collective-permute-start.2 = (f32[44,8,128]{2,1,0:T(8,128)S(1)}, f32[44,8,128]{2,1,0:T(8,128)S(1)}, u32[]{:S(2)}, u32[]{:S(2)}) collective-permute-start(f32[44,8,128]{2,1,0:T(8,128)S(1)} %slice.66), channel_id=1, source_target_pairs={{0,128},{128,0},{1,129},{129,1},{2,130},{130,2},{3,131},{131,3},{4... | collective-permute-start | bytes 540680 | tf_op jit(solution)/shard_map/ppermute | solution.py:725
  44.3 4.8 %collective-permute-start.3 = (f32[4,8,8,128]{3,2,1,0:T(8,128)S(1)}, f32[4,8,8,128]{3,2,1,0:T(8,128)S(1)}, u32[]{:S(2)}, u32[]{:S(2)}) collective-permute-start(f32[4,8,8,128]{3,2,1,0:T(8,128)S(1)} %get-tuple-element.48.own), channel_id=1, source_target_pairs={{128,16},{144,32},{160,48},{176,64},{192,80},{208,96},{224,112},{2... | collective-permute-start | bytes 393224 | tf_op jit(solution)/shard_map/ppermute | solution.py:761
  44.4 5.7 %collective-permute-start.5 = (f32[4,8,8,128]{3,2,1,0:T(8,128)S(1)}, f32[4,8,8,128]{3,2,1,0:T(8,128)S(1)}, u32[]{:S(2)}, u32[]{:S(2)}) collective-permute-start(f32[4,8,8,128]{3,2,1,0:T(8,128)S(1)} %get-tuple-element.48.own), channel_id=1, source_target_pairs={{0,128},{128,0},{1,129},{129,1},{2,130},{130,2},{3,131},{131,3},{4... | collective-permute-start | bytes 393224 | tf_op jit(solution)/shard_map/ppermute | solution.py:762
  49.0 2.2 %collective-permute-start.4 = (f32[4,4,8,128]{3,2,1,0:T(8,128)S(1)}, f32[4,4,8,128]{3,2,1,0:T(8,128)S(1)}, u32[]{:S(2)}, u32[]{:S(2)}) collective-permute-start(f32[4,4,8,128]{3,2,1,0:T(8,128)S(1)} %pad_maximum_fusion), channel_id=1, source_target_pairs={{0,128},{128,0},{1,129},{129,1},{2,130},{130,2},{3,131},{131,3},{4... | collective-permute-start | bytes 196616 | tf_op jit(solution)/shard_map/ppermute | solution.py:763
  52.9 1.3 %collective-permute-start.6 = (f32[8,8,128]{2,1,0:T(8,128)S(1)}, f32[8,8,128]{2,1,0:T(8,128)S(1)}, u32[]{:S(2)}, u32[]{:S(2)}) collective-permute-start(f32[8,8,128]{2,1,0:T(8,128)S(1)} %shard_map.153), channel_id=1, source_target_pairs={{0,128},{128,0},{1,129},{129,1},{2,130},{130,2},{3,131},{131,3},{4... | collective-permute-start | bytes 98312 | tf_op jit(solution)/shard_map/ppermute | solution.py:791
